TPU v7x, 32 devices: a whole 2x2x4 slice. The times are simulated.
32 devices in a mesh: groups: 2 (over x), wide: 16 (over z, y, core).
Axes of the slice: x: 2, y: 2, z: 4, core: 2. Of those that a mesh axis runs over, the one named last changes fastest.
Arguments:
- frames_in: bfloat16 [128, 256, 768], P(('groups', 'wide')), parts along dimension 0, may hold values from -5 to 5
- qkv_spatial: bfloat16 [768, 2304], replicated, may hold values from -6.5 to 6.5
- out_spatial: bfloat16 [768, 768], replicated, may hold values from -0.21875 to 0.21875
- qkv_temporal: bfloat16 [768, 2304], replicated, may hold values from -6.5 to 6.5
- out_temporal: bfloat16 [768, 768], replicated, may hold values from -0.21875 to 0.21875
Outputs:
- frames_out: bfloat16 [128, 256, 768], P(('groups', 'wide')), parts along dimension 0
There are 2 independent parts, one for each index of `groups`. A program takes and returns all parts, laid end to end along the dimension named above; an argument that names none is the same for every part. Nothing has to cross between parts.
All inputs are finite; a program needn't handle non-finite values.
Results may differ from a plain program's by a relative error of at most 0.008.
Values may be sent and summed in bfloat16 or wider, within the bound.
No kernel may reach another device: no remote copies, remote signals or barrier semaphores. Data moves between devices by JAX's collectives and lax.ppermute only.
A program may use at most 128 MiB of HBM per device.

v0:
```python
import jax
import jax.numpy as jnp
from jax import lax
from jax.sharding import PartitionSpec as P

HEADS = 12
HEAD_DIM = 64


def normalize(tensor):
    floats = tensor.astype(jnp.float32)
    average = jnp.mean(floats, axis=-1, keepdims=True)
    centred = floats - average
    spread = jnp.mean(centred * centred, axis=-1, keepdims=True)
    return (centred * lax.rsqrt(spread + 1e-06)).astype(jnp.bfloat16)


def project(flat_rows, matrix):
    return jnp.dot(flat_rows, matrix, preferred_element_type=jnp.float32)


def attend(projected, score_form, mix_form):
    leading = projected.shape[:-1]
    split = projected.reshape(leading + (3, HEADS, HEAD_DIM))
    queries = split[..., 0, :, :]
    key_part = split[..., 1, :, :]
    values = split[..., 2, :, :]
    scores = jnp.einsum(
        score_form, queries, key_part, preferred_element_type=jnp.float32
    ) * HEAD_DIM ** (-0.5)
    weights = jax.nn.softmax(scores, axis=-1).astype(jnp.bfloat16)
    mixed = jnp.einsum(mix_form, weights, values, preferred_element_type=jnp.float32)
    return mixed.reshape(leading + (HEADS * HEAD_DIM,)).astype(jnp.bfloat16)


def attend_time(received):
    frame_total, single, item_count, columns = received.shape
    sequences = received.reshape(frame_total, item_count, columns)
    result = attend(sequences, "qbhd,kbhd->bhqk", "bhqk,kbhd->qbhd")
    return result.reshape(frame_total, single, item_count, HEADS * HEAD_DIM)


def shards(frames_in, qkv_spatial, out_spatial, qkv_temporal, out_temporal):
    frame_count, patch_count, features = frames_in.shape
    wide_count = lax.axis_size("wide")
    per_group = patch_count // wide_count
    first = normalize(frames_in)
    proj_one = project(first.reshape(-1, features), qkv_spatial).astype(jnp.bfloat16)
    proj_one = proj_one.reshape(frame_count, patch_count, 3 * features)
    spatial = attend(proj_one, "bqhd,bkhd->bhqk", "bhqk,bkhd->bqhd")
    update = project(spatial.reshape(-1, features), out_spatial).reshape(
        frame_count, patch_count, features
    )
    middle = (frames_in.astype(jnp.float32) + update).astype(jnp.bfloat16)
    second = normalize(middle)
    grouped = second.reshape(frame_count, wide_count, per_group, features)
    received = lax.all_to_all(grouped, "wide", split_axis=1, concat_axis=0, tiled=True)
    frame_total, single, item_count, columns = received.shape
    local_proj = project(received.reshape(-1, columns), qkv_temporal).astype(jnp.bfloat16)
    local_proj = local_proj.reshape(frame_total, single, item_count, 3 * columns)
    temporal = attend_time(local_proj)
    returned = lax.all_to_all(temporal, "wide", split_axis=0, concat_axis=1, tiled=True)
    change = project(returned.reshape(-1, features), out_temporal).reshape(
        frame_count, patch_count, features
    )
    return (middle.astype(jnp.float32) + change).astype(jnp.bfloat16)


def solution(mesh):
    return jax.shard_map(
        shards,
        mesh=mesh,
        in_specs=(P(("groups", "wide"), None, None), P(), P(), P(), P()),
        out_specs=P(("groups", "wide"), None, None),
        check_vma=False,
    )
```

profile of v0, /device:TPU:0, one launch (start us, length us, event | category | flops | bytes accessed | tf_op | source)
XLA Modules:
  0.0 206.1 jit_solution(2839607701515157252)
XLA Ops:
  0.0 1.8 convert_reduce_fusion.1
  1.9 2.1 %fusion.16 = f32[4,256]{1,0:T(4,128)S(1)} fusion(bf16[4,256,768]{2,1,0:T(8,128)(2,1)} %param.5, f32[4,256]{1,0:T(4,128)S(1)} %broadcast_multiply_fusion.1), kind=kLoop, calls=%fused_computation.26 | loop fusion | flops 3144704 | bytes 1581056 | tf_op jit(solution)/shard_map/reduce_sum | solution.py:14
  4.0 0.4 fusion.17
  4.5 0.0 copy-done
  4.5 5.5 %convolution_convert_fusion.1 = bf16[1024,2304]{1,0:T(8,128)(2,1)} fusion(bf16[1024,768]{1,0:T(8,128)(2,1)S(1)} %bitcast.56, bf16[768,2304]{1,0:T(8,128)(2,1)S(1)} %copy-done), kind=kOutput, calls=%fused_computation.11 | convolution fusion | flops 3626237952 | bytes 9830400 | tf_op jit(solution)/shard_map/dot_general | solution.py:19
  10.0 6.6 %copy.29 = bf16[1024,2304]{0,1:T(8,128)(2,1)} copy(bf16[1024,2304]{1,0:T(8,128)(2,1)} %convolution_convert_fusion.1) | data formatting | bytes 9437184 | tf_op jit(solution)/shard_map/convert_element_type | solution.py:48
  16.6 8.9 %reshape_reshape.3 = bf16[4,256,3,12,64]{1,0,4,3,2:T(4,128)(2,1)} reshape(bf16[1024,2304]{0,1:T(8,128)(2,1)} %copy.29) | data formatting | bytes 9437184 | tf_op jit(solution)/shard_map/reshape;reshape | solution.py:24
  25.5 3.3 %fusion.35 = (bf16[4,256,1,12,64]{1,0,4,3,2:T(4,128)(2,1)S(1)}, bf16[4,256,1,12,64]{1,0,4,3,2:T(4,128)(2,1)S(1)}, bf16[4,256,1,12,64]{1,0,4,3,2:T(4,128)(2,1)S(1)}) fusion(bf16[4,256,3,12,64]{1,0,4,3,2:T(4,128)(2,1)} %reshape_reshape.3), kind=kLoop, calls=%fused_computation.52 | loop fusion | bytes 9437184 | tf_op jit(solution)/shard_map/slice | solution.py:27
  28.9 6.4 %fusion.29 = f32[4,12,256,256]{2,3,1,0:T(8,128)} fusion(bf16[4,256,1,12,64]{1,0,4,3,2:T(4,128)(2,1)S(1)} %get-tuple-element.10, bf16[4,256,1,12,64]{1,0,4,3,2:T(4,128)(2,1)S(1)} %get-tuple-element.9), kind=kOutput, calls=%fused_computation.40 | convolution fusion | flops 402653184 | bytes 15728640 | tf_op jit(solution)/shard_map/bqhd,bkhd->bhqk/dot_general | solution.py:28
  35.3 15.8 %fusion.36 = (f32[4,12,256]{2,1,0:T(8,128)S(1)}, f32[4,12,256,256]{2,3,1,0:T(8,128)}) fusion(f32[4,12,256,256]{2,3,1,0:T(8,128)} %fusion.29), kind=kOutput, calls=%fused_computation.53 | output fusion | flops 12583167 | bytes 25214976 | tf_op jit(solution)/shard_map/sub | solution.py:31
  51.1 5.8 %fusion.28 = bf16[4,12,64,256]{3,2,1,0:T(8,128)(2,1)S(1)} fusion(f32[4,12,256,256]{2,3,1,0:T(8,128)} %get-tuple-element.12, f32[4,12,256]{2,1,0:T(8,128)S(1)} %get-tuple-element.11, bf16[4,256,1,12,64]{1,0,4,3,2:T(4,128)(2,1)S(1)} %get-tuple-element.8), kind=kOutput, calls=%fused_computation.38 | convolution fusion | flops 409731072 | bytes 15777792 | tf_op jit(solution)/shard_map/bhqk,bkhd->bqhd/dot_general | solution.py:32
  56.9 0.0 copy-done.3
  56.9 1.6 convert_reduce_fusion
  58.5 0.6 fusion.14
  59.1 0.4 fusion.15
  59.5 0.0 copy-start.6
  59.6 0.2 copy.35
  59.7 43.5 %all_to_all.30 = bf16[4,16,16,768]{3,2,0,1:T(8,128)(2,1)S(1)} all-to-all(bf16[4,16,16,768]{3,2,0,1:T(8,128)(2,1)S(1)} %copy.35), channel_id=1, replica_groups=mesh['groups'=2,'wide'=16] {'wide'}, dimensions={1} | all-to-all | bytes 3145728 | tf_op jit(solution)/shard_map/all_to_all | solution.py:57
  103.3 5.4 %convolution_convert_fusion = bf16[1024,2304]{1,0:T(8,128)(2,1)} fusion(bf16[1024,768]{1,0:T(8,128)(2,1)S(1)} %bitcast.58, bf16[768,2304]{1,0:T(8,128)(2,1)S(1)} %copy-done.6), kind=kOutput, calls=%fused_computation.10 | convolution fusion | flops 3626237952 | bytes 9830400 | tf_op jit(solution)/shard_map/dot_general | solution.py:19
  108.7 14.9 %reshape_reshape_reshape.3 = bf16[64,16,3,12,64]{4,3,2,1,0:T(8,128)(2,1)} reshape(bf16[1024,2304]{1,0:T(8,128)(2,1)} %convolution_convert_fusion) | data formatting | bytes 9437184 | tf_op jit(solution)/shard_map/reshape;reshape;reshape | solution.py:24
  123.6 9.2 %fusion.34 = (bf16[64,16,1,12,64]{4,3,2,1,0:T(8,128)(2,1)}, bf16[64,16,1,12,64]{4,3,2,1,0:T(8,128)(2,1)}, bf16[64,16,1,12,64]{4,3,2,1,0:T(8,128)(2,1)}) fusion(bf16[64,16,3,12,64]{4,3,2,1,0:T(8,128)(2,1)} %reshape_reshape_reshape.3), kind=kLoop, calls=%fused_computation.51 | loop fusion | bytes 9437184 | tf_op jit(solution)/shard_map/slice | solution.py:27
  132.9 6.4 %copy.48 = bf16[64,16,1,12,64]{0,4,3,1,2:T(8,128)(2,1)S(1)} copy(bf16[64,16,1,12,64]{4,3,2,1,0:T(8,128)(2,1)} %get-tuple-element.5) | data formatting | bytes 3145728
  139.3 7.2 %fusion.21 = f32[16,12,64,64]{2,3,1,0:T(8,128)S(1)} fusion(bf16[64,16,1,12,64]{4,3,2,1,0:T(8,128)(2,1)} %get-tuple-element.6, bf16[64,16,1,12,64]{4,3,2,1,0:T(8,128)(2,1)} %get-tuple-element.7), kind=kOutput, calls=%fused_computation.32 | convolution fusion | flops 100663296 | bytes 6291456 | tf_op jit(solution)/shard_map/qbhd,kbhd->bhqk/dot_general | solution.py:28
  146.5 9.2 %fusion.37 = (f32[16,12,64]{2,1,0:T(8,128)S(1)}, f32[16,12,64,64]{2,3,1,0:T(8,128)S(1)}) fusion(f32[16,12,64,64]{2,3,1,0:T(8,128)S(1)} %fusion.21), kind=kOutput, calls=%fused_computation.54 | output fusion | flops 3145791 | bytes 6340608 | tf_op jit(solution)/shard_map/sub | solution.py:31
  155.7 2.6 %fusion.25 = bf16[16,12,64,64]{3,2,1,0:T(8,128)(2,1)} fusion(f32[16,12,64,64]{2,3,1,0:T(8,128)S(1)} %get-tuple-element.16, f32[16,12,64]{2,1,0:T(8,128)S(1)} %get-tuple-element.15, bf16[64,16,1,12,64]{0,4,3,1,2:T(8,128)(2,1)S(1)} %copy.48), kind=kOutput, calls=%fused_computation.37 | convolution fusion | flops 103022592 | bytes 6340608 | tf_op jit(solution)/shard_map/bhqk,kbhd->qbhd/dot_general | solution.py:32
  158.3 3.9 %copy.40 = bf16[64,1,16,768]{3,2,1,0:T(8,128)(2,1)S(1)} copy(bf16[64,1,16,768]{0,3,2,1:T(8,128)(2,1)} %bitcast.55) | data formatting | bytes 3145728 | tf_op jit(solution)/shard_map/convert_element_type | solution.py:33
  162.2 0.0 copy-start.5
  162.2 0.0 copy-start.8
  162.2 41.2 %all_to_all.31 = bf16[64,1,16,768]{3,2,1,0:T(8,128)(2,1)S(1)} all-to-all(bf16[64,1,16,768]{3,2,1,0:T(8,128)(2,1)S(1)} %copy.40), channel_id=1, replica_groups=mesh['groups'=2,'wide'=16] {'wide'}, dimensions={0} | all-to-all | bytes 3145728 | tf_op jit(solution)/shard_map/all_to_all | solution.py:62
  203.4 0.1 copy.41
  203.5 0.0 copy-start.1
  203.6 2.5 %fusion.19 = bf16[4,256,768]{2,1,0:T(8,128)(2,1)} fusion(bf16[4,256,768]{2,1,0:T(8,128)(2,1)S(1)} %copy-done.5, bf16[4,256,768]{2,1,0:T(8,128)(2,1)S(1)} %bitcast.57, bf16[768,768]{1,0:T(8,128)(2,1)S(1)} %copy-done.8), kind=kOutput, calls=%fused_computation.29 | convolution fusion | flops 1210318848 | bytes 5898240 | tf_op jit(solution)/shard_map/dot_general | solution.py:19
  (16 shorter events, 0.1 us)
Async XLA Ops:
  0.0 4.5 %copy-start = (bf16[768,2304]{1,0:T(8,128)(2,1)S(1)}, bf16[768,2304]{1,0:T(8,128)(2,1)}, u32[]{:S(2)}) copy-start(bf16[768,2304]{1,0:T(8,128)(2,1)} %param.6) | copy-start | bytes 10616836
  0.0 4.0 %copy-start.2 = (bf16[4,256,768]{2,1,0:T(8,128)(2,1)S(1)}, bf16[4,256,768]{2,1,0:T(8,128)(2,1)}, u32[]{:S(2)}) copy-start(bf16[4,256,768]{2,1,0:T(8,128)(2,1)} %param.5) | copy-start | bytes 4718596
  51.1 5.8 %copy-start.3 = (bf16[4,256,768]{2,1,0:T(8,128)(2,1)S(1)}, bf16[4,256,768]{2,1,0:T(8,128)(2,1)}, u32[]{:S(2)}) copy-start(bf16[4,256,768]{2,1,0:T(8,128)(2,1)} %param.5) | copy-start | bytes 4718596
  51.1 5.8 %copy-start.7 = (bf16[768,768]{1,0:T(8,128)(2,1)S(1)}, bf16[768,768]{1,0:T(8,128)(2,1)}, u32[]{:S(2)}) copy-start(bf16[768,768]{1,0:T(8,128)(2,1)} %param.7) | copy-start | bytes 3538948
  58.5 1.2 copy-start.4
  59.5 43.7 %copy-start.6 = (bf16[768,2304]{1,0:T(8,128)(2,1)S(1)}, bf16[768,2304]{1,0:T(8,128)(2,1)}, u32[]{:S(2)}) copy-start(bf16[768,2304]{1,0:T(8,128)(2,1)} %param.8) | copy-start | bytes 10616836
  162.2 41.3 %copy-start.5 = (bf16[4,256,768]{2,1,0:T(8,128)(2,1)S(1)}, bf16[4,256,768]{2,1,0:T(8,128)(2,1)}, u32[]{:S(2)}) copy-start(bf16[4,256,768]{2,1,0:T(8,128)(2,1)} %copy-done.4) | copy-start | bytes 4718596
  162.2 41.3 %copy-start.8 = (bf16[768,768]{1,0:T(8,128)(2,1)S(1)}, bf16[768,768]{1,0:T(8,128)(2,1)}, u32[]{:S(2)}) copy-start(bf16[768,768]{1,0:T(8,128)(2,1)} %param.9) | copy-start | bytes 3538948
  203.5 2.6 %copy-start.1 = (bf16[768,2304]{1,0:T(8,128)(2,1)S(1)}, bf16[768,2304]{1,0:T(8,128)(2,1)}, u32[]{:S(2)}) copy-start(bf16[768,2304]{1,0:T(8,128)(2,1)} %param.6) | copy-start | bytes 10616836
where the time goes:
time: 207 us; the launch traced here: 206 us
  blocking collectives  84.7 us (41%)
  local copies, waits for them, and re-layouts  53.7 us (26%)
  matrix products  37.1 us (18%)
  other arithmetic  30.4 us (15%)
    all_to_all x1, blocking collectives, shards(): lax.all_to_all(grouped, 'wide', split_axis=1, concat_axis=0, tiled=True)  43.5 us
    all_to_all x1, blocking collectives, shards(): lax.all_to_all(temporal, 'wide', split_axis=0, concat_axis=1, tiled=True)  41.2 us
    sub x2, other arithmetic, attend(): weights = jax.nn.softmax(scores, axis=-1).astype(jnp.bfloat16)  24.9 us
    another operation x2, local copies, waits for them, and re-layouts, attend(): split = projected.reshape(leading + (3, HEADS, HEAD_DIM))  23.9 us
    dot_general x4, matrix products, project(): return jnp.dot(flat_rows, matrix, preferred_element_type=jnp.float32)  15.1 us
    dot_general x2, matrix products, attend(): jnp.einsum(score_form, queries, key_part, preferred_element_type=jnp.floa...  13.6 us
    slice x2, local copies, waits for them, and re-layouts, attend(): values = split[..., 2, :, :]  12.6 us
    dot_general x2, matrix products, attend(): jnp.einsum(mix_form, weights, values, preferred_element_type=jnp.float32)  8.46 us

commit v1 on v0

v1 whole, which is shorter than its diff:
```python
import functools

import jax
import jax.numpy as jnp
from jax import lax
from jax.experimental import pallas as pl
from jax.experimental.pallas import tpu as pltpu
from jax.sharding import PartitionSpec as P

HEADS = 12
HEAD_DIM = 64
LANES = 128
TILE = 16
HALF = TILE // 2
BF16 = jnp.bfloat16
F32 = jnp.float32
VMEM = pl.BlockSpec(memory_space=pltpu.VMEM)
SMEM = pl.BlockSpec(memory_space=pltpu.SMEM)

OUTER = (0, 8, 12, 4)
INNER = (0, 1, 2, 3)


def normalize(floats):
    average = jnp.mean(floats, axis=-1, keepdims=True)
    centred = floats - average
    spread = jnp.mean(centred * centred, axis=-1, keepdims=True)
    return (centred * lax.rsqrt(spread + 1e-06)).astype(BF16)


def project(flat_rows, matrix):
    return jnp.dot(flat_rows, matrix, preferred_element_type=F32)


def attend(projected, score_form, mix_form):
    leading = projected.shape[:-1]
    split = projected.reshape(leading + (3, HEADS, HEAD_DIM))
    queries = split[..., 0, :, :]
    key_part = split[..., 1, :, :]
    values = split[..., 2, :, :]
    scores = jnp.einsum(
        score_form, queries, key_part, preferred_element_type=F32
    ) * HEAD_DIM ** (-0.5)
    weights = jax.nn.softmax(scores, axis=-1).astype(BF16)
    mixed = jnp.einsum(mix_form, weights, values, preferred_element_type=F32)
    return mixed.reshape(leading + (HEADS * HEAD_DIM,)).astype(BF16)


def attend_time(received):
    frame_total, single, item_count, columns = received.shape
    sequences = received.reshape(frame_total, item_count, columns)
    result = attend(sequences, "qbhd,kbhd->bhqk", "bhqk,kbhd->qbhd")
    return result.reshape(frame_total, single, item_count, HEADS * HEAD_DIM)


def plain_shards(frames_in, qkv_spatial, out_spatial, qkv_temporal, out_temporal):
    frame_count, patch_count, features = frames_in.shape
    wide_count = lax.axis_size("wide")
    per_group = patch_count // wide_count
    first = normalize(frames_in.astype(F32))
    proj_one = project(first.reshape(-1, features), qkv_spatial).astype(BF16)
    proj_one = proj_one.reshape(frame_count, patch_count, 3 * features)
    spatial = attend(proj_one, "bqhd,bkhd->bhqk", "bhqk,bkhd->bqhd")
    update = project(spatial.reshape(-1, features), out_spatial).reshape(
        frame_count, patch_count, features
    )
    middle = (frames_in.astype(F32) + update).astype(BF16)
    second = normalize(middle.astype(F32))
    grouped = second.reshape(frame_count, wide_count, per_group, features)
    received = lax.all_to_all(grouped, "wide", split_axis=1, concat_axis=0, tiled=True)
    frame_total, single, item_count, columns = received.shape
    local_proj = project(received.reshape(-1, columns), qkv_temporal).astype(BF16)
    local_proj = local_proj.reshape(frame_total, single, item_count, 3 * columns)
    temporal = attend_time(local_proj)
    returned = lax.all_to_all(temporal, "wide", split_axis=0, concat_axis=1, tiled=True)
    change = project(returned.reshape(-1, features), out_temporal).reshape(
        frame_count, patch_count, features
    )
    return (middle.astype(F32) + change).astype(BF16)


def attend_pair(q, k, v, length):
    rows = q.shape[0]
    low = lax.broadcasted_iota(jnp.int32, (rows, LANES), 1) < HEAD_DIM
    mixed = []
    for half in range(2):
        mine = low if half == 0 else ~low
        one = jnp.where(mine, q, jnp.zeros_like(q))
        scores = lax.dot_general(
            one, k, (((1,), (1,)), ((), ())), preferred_element_type=F32
        )
        if rows > length:
            own = lax.broadcasted_iota(
                jnp.int32, (rows, rows), 0
            ) // length == lax.broadcasted_iota(jnp.int32, (rows, rows), 1) // length
            scores = jnp.where(own, scores, -jnp.inf)
        top = jnp.max(scores, axis=-1, keepdims=True)
        weights = jnp.exp(scores - top).astype(BF16)
        values = jnp.where(mine, v, jnp.ones_like(v))
        mixed.append(jnp.dot(weights, values, preferred_element_type=F32))
    total = pltpu.roll(jnp.where(low, mixed[1], mixed[0]), HEAD_DIM, 1)
    return (jnp.where(low, mixed[0], mixed[1]) / total).astype(BF16)


def layer_rows(a_ref, wqkv, qkv, mixed, length, block):
    rows, d = a_ref.shape
    group = 256
    for j in range(3 * d // group):
        cols = slice(j * group, (j + 1) * group)
        part = jnp.dot(a_ref[...], wqkv[:, cols], preferred_element_type=F32)
        part = part.astype(BF16)
        if j < d // group:
            part = part * BF16(HEAD_DIM**-0.5)
        qkv[:, cols] = part
    for start in range(0, rows, block):
        r = slice(start, start + block)
        for c in range(0, d, LANES):
            mixed[r, c : c + LANES] = attend_pair(
                qkv[r, c : c + LANES],
                qkv[r, d + c : d + c + LANES],
                qkv[r, 2 * d + c : 2 * d + c + LANES],
                length,
            )


def spatial_kernel(outer_first, me, x, wqkv, wo, middle, o0, o1, o2, o3, a, qkv, mixed, second):
    frames, patches, d = x.shape
    outs = (o0, o1, o2, o3)
    number = me[0]
    for f in range(frames):
        a[f * patches : (f + 1) * patches, :] = normalize(x[f].astype(F32))
    layer_rows(a, wqkv, qkv, mixed, patches, patches)
    for f in range(frames):
        r = slice(f * patches, (f + 1) * patches)
        update = jnp.dot(mixed[r, :], wo[...], preferred_element_type=F32)
        mid = (x[f].astype(F32) + update).astype(BF16)
        middle[f] = mid
        second[...] = normalize(mid.astype(F32))
        for p in range(4):
            for i in range(4):
                owner = number ^ (OUTER[p] ^ INNER[i])
                rows = second[pl.ds(pl.multiple_of(owner * TILE, TILE), TILE), :]
                if outer_first:
                    outs[p][f, i] = rows
                else:
                    outs[i][f, p] = rows


def spatial(me, x, wqkv, wo, outer_first):
    frames, patches, d = x.shape
    rows = frames * patches
    block = jax.ShapeDtypeStruct((frames, 4, TILE, d), BF16)
    return pl.pallas_call(
        functools.partial(spatial_kernel, outer_first),
        in_specs=[SMEM, VMEM, VMEM, VMEM],
        out_specs=[VMEM] * 5,
        out_shape=[jax.ShapeDtypeStruct(x.shape, BF16)] + [block] * 4,
        scratch_shapes=[
            pltpu.VMEM((rows, d), BF16),
            pltpu.VMEM((rows, 3 * d), BF16),
            pltpu.VMEM((rows, d), BF16),
            pltpu.VMEM((patches, d), BF16),
        ],
        compiler_params=pltpu.CompilerParams(vmem_limit_bytes=32 << 20),
        cost_estimate=pl.CostEstimate(
            flops=8 * rows * d * d + 16 * rows * patches * d,
            bytes_accessed=8 * d * d,
            transcendentals=rows * patches * HEADS,
        ),
        name="spatial_outer" if outer_first else "spatial_inner",
    )(me, x, wqkv, wo)


def regroup_kernel(*refs):
    ins, outs = refs[:4], refs[4:]
    for b in range(4):
        for a in range(4):
            if len(ins[0].shape) == 4:
                outs[b][a] = ins[a][:, b]
            else:
                outs[b][a] = ins[a][b]


def regroup(pieces):
    shape = pieces[0].shape
    shape = (4, shape[0]) + shape[2:] if len(shape) == 4 else shape
    return pl.pallas_call(
        regroup_kernel,
        in_specs=[VMEM] * 4,
        out_specs=[VMEM] * 4,
        out_shape=[jax.ShapeDtypeStruct(shape, BF16)] * 4,
        cost_estimate=pl.CostEstimate(flops=0, bytes_accessed=1 << 20, transcendentals=0),
        name="regroup",
    )(*pieces)


def chosen(rows, columns, source):
    r = lax.broadcasted_iota(jnp.int32, (rows, columns), 0)
    c = lax.broadcasted_iota(jnp.int32, (rows, columns), 1)
    return (c == source(r)).astype(F32).astype(BF16)


def temporal_kernel(half, outer_first, *refs):
    z_parts, y_parts = refs[:4], refs[4:8]
    wqkv, wo = refs[8:10]
    outs = refs[10:14]
    gathered, a, qkv, mixed = refs[14:]
    d = a.shape[1]
    length = a.shape[0] // HALF
    pick = chosen(HALF * TILE, TILE * TILE, lambda r: (r % TILE) * TILE + half * HALF + r // TILE)
    for p in range(4):
        for i in range(4):
            base = i * 4 * TILE
            for f in range(2):
                gathered[base + f * TILE : base + (f + 1) * TILE, :] = z_parts[i][p, f]
                gathered[base + (f + 2) * TILE : base + (f + 3) * TILE, :] = y_parts[p][i, f]
        taken = jnp.dot(pick, gathered[...], preferred_element_type=F32).astype(BF16)
        for q in range(HALF):
            start = q * length + p * TILE
            a[start : start + TILE, :] = taken[q * TILE : (q + 1) * TILE]
    layer_rows(a, wqkv, qkv, mixed, length, 4 * length)
    back = chosen(HALF * TILE, HALF * TILE, lambda r: (r % HALF) * TILE + r // HALF)
    for p in range(4):
        rows = jnp.concatenate(
            [mixed[q * length + p * TILE : q * length + (p + 1) * TILE, :] for q in range(HALF)],
            axis=0,
        )
        change = jnp.dot(rows, wo[...], preferred_element_type=F32).astype(BF16)
        change = jnp.dot(back, change, preferred_element_type=F32).astype(BF16)
        for i in range(4):
            piece = change[i * 2 * TILE : (i + 1) * 2 * TILE]
            if outer_first:
                outs[p][i] = piece
            else:
                outs[i][p] = piece


def temporal(half, z_parts, y_parts, wqkv, wo, outer_first):
    d = wo.shape[0]
    length = 4 * TILE
    rows = HALF * length
    block = jax.ShapeDtypeStruct((4, 2 * TILE, d), BF16)
    return pl.pallas_call(
        functools.partial(temporal_kernel, half, outer_first),
        in_specs=[VMEM] * 10,
        out_specs=[VMEM] * 4,
        out_shape=[block] * 4,
        scratch_shapes=[
            pltpu.VMEM((TILE * TILE, d), BF16),
            pltpu.VMEM((rows, d), BF16),
            pltpu.VMEM((rows, 3 * d), BF16),
            pltpu.VMEM((rows, d), BF16),
        ],
        compiler_params=pltpu.CompilerParams(vmem_limit_bytes=32 << 20),
        cost_estimate=pl.CostEstimate(
            flops=8 * rows * d * d + 16 * rows * 4 * length * d,
            bytes_accessed=8 * d * d,
            transcendentals=rows * 4 * length * HEADS,
        ),
        name="temporal",
    )(*z_parts, *y_parts, wqkv, wo)


def last_kernel(me, mid01, mid23, *refs):
    early, late, out = refs[:4], refs[4:8], refs[8]
    number = me[0]
    f = pl.program_id(0)

    def add(mid, frame, at):
        for p in range(4):
            for i in range(4):
                owner = number ^ (OUTER[p] ^ INNER[i])
                rows = pl.ds(pl.multiple_of(owner * TILE, TILE), TILE)
                change = jnp.concatenate(
                    [
                        early[i][p].astype(F32)[at * HALF : (at + 1) * HALF],
                        late[p][i].astype(F32)[at * HALF : (at + 1) * HALF],
                    ],
                    axis=0,
                )
                out[0, rows, :] = (mid[frame, rows, :].astype(F32) + change).astype(BF16)

    for at in range(4):
        pl.when(f == at)(functools.partial(add, mid01 if at < 2 else mid23, at % 2, at))


def last(me, mid01, mid23, early, late):
    _, patches, d = mid01.shape
    return pl.pallas_call(
        last_kernel,
        grid=(4,),
        in_specs=[SMEM] + [VMEM] * 10,
        out_specs=pl.BlockSpec((1, patches, d), lambda f: (f, 0, 0)),
        out_shape=jax.ShapeDtypeStruct((4, patches, d), BF16),
        cost_estimate=pl.CostEstimate(
            flops=patches * d * 4, bytes_accessed=patches * d * 8, transcendentals=0
        ),
        name="last",
    )(me, mid01, mid23, *early, *late)


def exchange(pieces, masks):
    size = lax.axis_size("wide")
    return [pieces[0]] + [
        lax.ppermute(piece, "wide", [(w, w ^ mask) for w in range(size)])
        for piece, mask in zip(pieces[1:], masks[1:])
    ]


def shards(frames_in, qkv_spatial, out_spatial, qkv_temporal, out_temporal):
    me = lax.axis_index("wide").astype(jnp.int32).reshape(1)
    mid01, *pieces = spatial(me, frames_in[:2], qkv_spatial, out_spatial, True)
    z_parts = exchange(regroup(exchange(pieces, OUTER)), INNER)
    mid23, *pieces = spatial(me, frames_in[2:], qkv_spatial, out_spatial, False)
    y_parts = exchange(regroup(exchange(pieces, INNER)), OUTER)
    pieces = temporal(0, z_parts, y_parts, qkv_temporal, out_temporal, True)
    early = exchange(regroup(exchange(pieces, OUTER)), INNER)
    pieces = temporal(1, z_parts, y_parts, qkv_temporal, out_temporal, False)
    late = exchange(regroup(exchange(pieces, INNER)), OUTER)
    return last(me, mid01, mid23, early, late)


def solution(mesh):
    wide = mesh.shape["wide"]

    def whole(frames_in, *weights):
        local = frames_in.shape[0] // (wide * mesh.shape["groups"])
        fits = wide == 16 and local == 4 and frames_in.shape[1] == wide * TILE
        return jax.shard_map(
            shards if fits else plain_shards,
            mesh=mesh,
            in_specs=(P(("groups", "wide"), None, None), P(), P(), P(), P()),
            out_specs=P(("groups", "wide"), None, None),
            check_vma=False,
        )(frames_in, *weights)

    return whole
```

time: 207 us -> 121 us (0.58)
  blocking collectives: 84.7 us -> 0 us
  Pallas kernels: 0 us -> 38.8 us
  local copies, waits for them, and re-layouts: 53.7 us -> 15 us
  matrix products: 37.1 us -> 0 us
  waiting for transfers between devices: 0 us -> 36.3 us
  other arithmetic: 30.4 us -> 0 us
  starting transfers between devices: 0 us -> 29.8 us
    all_to_all x2 -> x0, blocking collectives: 84.7 us -> none  [the longest x1 43.5 us: shards(): lax.all_to_all(grouped, 'wide', split_axis=1, concat_axis=0, tiled=True)]
    pallas_call x0 -> x9, Pallas kernels: none -> 38.8 us  [the longest x2 14.9 us: temporal(): pl.pallas_call(functools.partial(temporal_kernel, half, outer_first), in_...]
    dot_general x8 -> x0, matrix products: 37.1 us -> none  [the longest x4 15.1 us: project(): return jnp.dot(flat_rows, matrix, preferred_element_type=jnp.float32)]
    ppermute x0 -> x24, waiting for transfers between devices: none -> 36.3 us  [exchange(): lax.ppermute(piece, 'wide', [(w, w ^ mask) for w in range(size)])]
    ppermute x0 -> x24, starting transfers between devices: none -> 29.8 us  [exchange(): lax.ppermute(piece, 'wide', [(w, w ^ mask) for w in range(size)])]
    sub x2 -> x0, other arithmetic: 24.9 us -> none  [attend(): weights = jax.nn.softmax(scores, axis=-1).astype(jnp.bfloat16)]
    another operation x2 -> x0, local copies, waits for them, and re-layouts: 23.9 us -> none  [attend(): split = projected.reshape(leading + (3, HEADS, HEAD_DIM))]
    slice x2 -> x1, local copies, waits for them, and re-layouts: 12.6 us -> 1.57 us  [shards(): mid23, *pieces = spatial(me, frames_in[2:], qkv_spatial, out_spatial, False)]
  transfers between devices with their start and end apart: 0 -> 24, of which waited for: 0 -> 12; matrix products, arithmetic and copies ran while one was open for 0% -> 0% of each run, Pallas kernels for 0% -> 19%
where the time goes in v1:
time: 121 us; the launch traced here: 120 us
  Pallas kernels  38.8 us (32%)
  waiting for transfers between devices  36.3 us (30%)
  starting transfers between devices  29.8 us (25%)
  local copies, waits for them, and re-layouts  15 us (12%)
    ppermute x24, waiting for transfers between devices, exchange(): lax.ppermute(piece, 'wide', [(w, w ^ mask) for w in range(size)])  36.3 us
    ppermute x24, starting transfers between devices, exchange(): lax.ppermute(piece, 'wide', [(w, w ^ mask) for w in range(size)])  29.8 us
    pallas_call x2, Pallas kernels, temporal(): pl.pallas_call(functools.partial(temporal_kernel, half, outer_first), in_...  14.9 us
    unnamed x56, local copies, waits for them, and re-layouts  13.4 us
    pallas_call x2, Pallas kernels, spatial(): pl.pallas_call(functools.partial(spatial_kernel, outer_first), in_specs=[...  11.7 us
    pallas_call x4, Pallas kernels, regroup(): pl.pallas_call(regroup_kernel, in_specs=[VMEM] * 4, out_specs=[VMEM] * 4,...  8.52 us
    pallas_call x1, Pallas kernels, last(): pl.pallas_call(last_kernel, grid=(4,), in_specs=[SMEM] + [VMEM] * 10, out...  3.66 us
  transfers between devices with their start and end apart: 24, of which 12 were waited for; matrix products, arithmetic and copies ran while one was open for 0% of the time, Pallas kernels for 19%

profile of v1, /device:TPU:0, one launch (start us, length us, event | category | flops | bytes accessed | tf_op | source)
XLA Modules:
  0.0 120.1 jit_solution(11322749619966797933)
XLA Ops:
  0.0 1.6 %fusion = (bf16[2,256,768]{2,1,0:T(8,128)(2,1)S(1)}, bf16[2,256,768]{2,1,0:T(8,128)(2,1)S(1)}) fusion(bf16[4,256,768]{2,1,0:T(8,128)(2,1)} %param.5), kind=kLoop, calls=%fused_computation | loop fusion | bytes 3145728 | tf_op jit(solution)/shard_map/slice | solution.py:314
  1.7 2.0 %copy-done.6 = bf16[768,2304]{1,0:T(8,128)(2,1)S(1)} copy-done((bf16[768,2304]{1,0:T(8,128)(2,1)S(1)}, bf16[768,2304]{1,0:T(8,128)(2,1)}, u32[]{:S(2)}) %copy-start.6) | copy-done | bytes 3538968
  3.7 5.5 %spatial_outer.1 = (bf16[2,256,768]{2,1,0:T(8,128)(2,1)S(1)}, bf16[2,4,16,768]{3,2,1,0:T(8,128)(2,1)S(1)}, bf16[2,4,16,768]{3,2,1,0:T(8,128)(2,1)S(1)}, bf16[2,4...) custom-call(s32[1]{0:T(128)} %bitcast.me, bf16[2,256,768]{2,1,0:T(8,128)(2,1)S(1)} %get-tuple-element.74.x, ...), custom_call_target="tpu_custom_call" | custom-call | flops 4026531840 | bytes 4718592 | tf_op jit(solution)/shard_map/spatial_outer/pallas_call | solution.py:153
  10.8 4.0 %collective-permute-start = (bf16[2,4,16,768]{3,2,1,0:T(8,128)(2,1)S(1)}, bf16[2,4,16,768]{3,2,1,0:T(8,128)(2,1)S(1)}, u32[]{:S(2)}, u32[]{:S(2)}) collective-permute-start(bf16[2,4,16,768]{3,2,1,0:T(8,128)(2,1)S(1)} %get-tuple-element.42), channel_id=1, source_target_pairs={{0,8},{1,9},{2,10},{3,11},{4,12},{5,13},{6,14},{7,15},{8,0},{9,1},... | collective-permute-start | bytes 589832 | tf_op jit(solution)/shard_map/ppermute | solution.py:305
  14.9 1.3 %collective-permute-start.1 = (bf16[2,4,16,768]{3,2,1,0:T(8,128)(2,1)S(1)}, bf16[2,4,16,768]{3,2,1,0:T(8,128)(2,1)S(1)}, u32[]{:S(2)}, u32[]{:S(2)}) collective-permute-start(bf16[2,4,16,768]{3,2,1,0:T(8,128)(2,1)S(1)} %get-tuple-element.43), channel_id=1, source_target_pairs={{0,12},{1,13},{2,14},{3,15},{4,8},{5,9},{6,10},{7,11},{8,4},{9,5},... | collective-permute-start | bytes 589832 | tf_op jit(solution)/shard_map/ppermute | solution.py:305
  16.4 6.3 %spatial_inner.1 = (bf16[2,256,768]{2,1,0:T(8,128)(2,1)S(1)}, bf16[2,4,16,768]{3,2,1,0:T(8,128)(2,1)S(1)}, bf16[2,4,16,768]{3,2,1,0:T(8,128)(2,1)}, bf16[2,4,16,...) custom-call(s32[1]{0:T(128)} %bitcast.me, bf16[2,256,768]{2,1,0:T(8,128)(2,1)S(1)} %get-tuple-element.73.x, ...), custom_call_target="tpu_custom_call" | custom-call | flops 4026531840 | bytes 4718592 | tf_op jit(solution)/shard_map/spatial_inner/pallas_call | solution.py:153
  24.3 1.5 %collective-permute-start.7 = (bf16[2,4,16,768]{3,2,1,0:T(8,128)(2,1)}, bf16[2,4,16,768]{3,2,1,0:T(8,128)(2,1)}, u32[]{:S(2)}, u32[]{:S(2)}) collective-permute-start(bf16[2,4,16,768]{3,2,1,0:T(8,128)(2,1)} %get-tuple-element.51), channel_id=1, source_target_pairs={{0,2},{1,3},{2,0},{3,1},{4,6},{5,7},{6,4},{7,5},{8,10},{9,11},{10,... | collective-permute-start | bytes 589832 | tf_op jit(solution)/shard_map/ppermute | solution.py:305
  25.8 3.3 %collective-permute-done.refs_1_ = bf16[2,4,16,768]{3,2,1,0:T(8,128)(2,1)S(1)} collective-permute-done((bf16[2,4,16,768]{3,2,1,0:T(8,128)(2,1)S(1)}, bf16[2,4,16,768]{3,2,1,0:T(8,128)(2,1)S(1)}, u32[]{:S(2)}, u32[]{:S(2)}) %collective-permute-start) | collective-permute-done | bytes 196640 | tf_op jit(solution)/shard_map/ppermute | solution.py:305
  30.5 2.1 %regroup.4 = (bf16[4,2,16,768]{3,2,1,0:T(8,128)(2,1)}, bf16[4,2,16,768]{3,2,1,0:T(8,128)(2,1)}, bf16[4,2,16,768]{3,2,1,0:T(8,128)(2,1)}, bf16[4,2,16,768]{3,2,1,0:T(8,128)(2,1)}) custom-call(bf16[2,4,16,768]{3,2,1,0:T(8,128)(2,1)} %copy-done.5, bf16[2,4,16,768]{3,2,1,0:T(8,128)(2,1)} %copy-done.24, bf16[2,4,16,768]{3,2,1,0:T(8,128)(2,1)} %copy-done.26, ...), custom_call_target="tpu_custom_call" | custom-call | bytes 1048576 | tf_op jit(solution)/shard_map/regroup/pallas_call | solution.py:187
  32.6 1.9 %collective-permute-start.3 = (bf16[4,2,16,768]{3,2,1,0:T(8,128)(2,1)}, bf16[4,2,16,768]{3,2,1,0:T(8,128)(2,1)}, u32[]{:S(2)}, u32[]{:S(2)}) collective-permute-start(bf16[4,2,16,768]{3,2,1,0:T(8,128)(2,1)} %get-tuple-element.46), channel_id=1, source_target_pairs={{0,1},{1,0},{2,3},{3,2},{4,5},{5,4},{6,7},{7,6},{8,9},{9,8},{10,11... | collective-permute-start | bytes 589832 | tf_op jit(solution)/shard_map/ppermute | solution.py:305
  34.7 1.2 collective-permute-start.5
  36.3 2.1 %regroup.5 = (bf16[4,2,16,768]{3,2,1,0:T(8,128)(2,1)}, bf16[4,2,16,768]{3,2,1,0:T(8,128)(2,1)}, bf16[4,2,16,768]{3,2,1,0:T(8,128)(2,1)}, bf16[4,2,16,768]{3,2,1,0:T(8,128)(2,1)}) custom-call(bf16[2,4,16,768]{3,2,1,0:T(8,128)(2,1)} %copy-done.3, bf16[2,4,16,768]{3,2,1,0:T(8,128)(2,1)} %collective-permute-done.6.refs_1_, ...), custom_call_target="tpu_custom_call" | custom-call | bytes 1048576 | tf_op jit(solution)/shard_map/regroup/pallas_call | solution.py:187
  38.4 4.2 %collective-permute-start.9 = (bf16[4,2,16,768]{3,2,1,0:T(8,128)(2,1)}, bf16[4,2,16,768]{3,2,1,0:T(8,128)(2,1)S(1)}, u32[]{:S(2)}, u32[]{:S(2)}) collective-permute-start(bf16[4,2,16,768]{3,2,1,0:T(8,128)(2,1)} %get-tuple-element.54), channel_id=1, source_target_pairs={{0,8},{1,9},{2,10},{3,11},{4,12},{5,13},{6,14},{7,15},{8,0},{9,1},... | collective-permute-start | bytes 589832 | tf_op jit(solution)/shard_map/ppermute | solution.py:305
  43.2 1.8 %collective-permute-done.5.refs_3_ = bf16[4,2,16,768]{3,2,1,0:T(8,128)(2,1)} collective-permute-done((bf16[4,2,16,768]{3,2,1,0:T(8,128)(2,1)}, bf16[4,2,16,768]{3,2,1,0:T(8,128)(2,1)}, u32[]{:S(2)}, u32[]{:S(2)}) %collective-permute-start.5) | collective-permute-done | bytes 196640 | tf_op jit(solution)/shard_map/ppermute | solution.py:305
  44.9 12.0 %collective-permute-done.9.refs_5_ = bf16[4,2,16,768]{3,2,1,0:T(8,128)(2,1)S(1)} collective-permute-done((bf16[4,2,16,768]{3,2,1,0:T(8,128)(2,1)}, bf16[4,2,16,768]{3,2,1,0:T(8,128)(2,1)S(1)}, u32[]{:S(2)}, u32[]{:S(2)}) %collective-permute-start.9) | collective-permute-done | bytes 196640 | tf_op jit(solution)/shard_map/ppermute | solution.py:305
  56.9 1.2 collective-permute-done.11.refs_7_
  58.1 1.3 %copy-done.10 = bf16[768,768]{1,0:T(8,128)(2,1)S(1)} copy-done((bf16[768,768]{1,0:T(8,128)(2,1)S(1)}, bf16[768,768]{1,0:T(8,128)(2,1)}, u32[]{:S(2)}) %copy-start.10) | copy-done | bytes 1179672
  61.2 7.1 %temporal.2 = (bf16[4,32,768]{2,1,0:T(8,128)(2,1)S(1)}, bf16[4,32,768]{2,1,0:T(8,128)(2,1)S(1)}, bf16[4,32,768]{2,1,0:T(8,128)(2,1)S(1)}, bf16[4,32,768]{2,1,0:T(8,128)(2,1)S(1)}) custom-call(bf16[4,2,16,768]{3,2,1,0:T(8,128)(2,1)S(1)} %copy-done.11, bf16[4,2,16,768]{3,2,1,0:T(8,128)(2,1)} %collective-permute-done.3.refs_1_, ...), custom_call_target="tpu_custom_call" | custom-call | flops 4026531840 | bytes 4718592 | tf_op jit(solution)/shard_map/temporal/pallas_call | solution.py:243
  69.0 3.1 %collective-permute-start.12 = (bf16[4,32,768]{2,1,0:T(8,128)(2,1)S(1)}, bf16[4,32,768]{2,1,0:T(8,128)(2,1)S(1)}, u32[]{:S(2)}, u32[]{:S(2)}) collective-permute-start(bf16[4,32,768]{2,1,0:T(8,128)(2,1)S(1)} %get-tuple-element.58), channel_id=1, source_target_pairs={{0,8},{1,9},{2,10},{3,11},{4,12},{5,13},{6,14},{7,15},{8,0},{9,1},... | collective-permute-start | bytes 589832 | tf_op jit(solution)/shard_map/ppermute | solution.py:305
  72.2 2.7 %collective-permute-start.13 = (bf16[4,32,768]{2,1,0:T(8,128)(2,1)S(1)}, bf16[4,32,768]{2,1,0:T(8,128)(2,1)S(1)}, u32[]{:S(2)}, u32[]{:S(2)}) collective-permute-start(bf16[4,32,768]{2,1,0:T(8,128)(2,1)S(1)} %get-tuple-element.59), channel_id=1, source_target_pairs={{0,12},{1,13},{2,14},{3,15},{4,8},{5,9},{6,10},{7,11},{8,4},{9,5},... | collective-permute-start | bytes 589832 | tf_op jit(solution)/shard_map/ppermute | solution.py:305
  74.9 7.8 %temporal.3 = (bf16[4,32,768]{2,1,0:T(8,128)(2,1)S(1)}, bf16[4,32,768]{2,1,0:T(8,128)(2,1)}, bf16[4,32,768]{2,1,0:T(8,128)(2,1)}, bf16[4,32,768]{2,1,0:T(8,128)(2,1)}) custom-call(bf16[4,2,16,768]{3,2,1,0:T(8,128)(2,1)S(1)} %copy-done.11, bf16[4,2,16,768]{3,2,1,0:T(8,128)(2,1)} %collective-permute-done.3.refs_1_, ...), custom_call_target="tpu_custom_call" | custom-call | flops 4026531840 | bytes 4718592 | tf_op jit(solution)/shard_map/temporal/pallas_call | solution.py:243
  83.3 1.5 %collective-permute-start.19 = (bf16[4,32,768]{2,1,0:T(8,128)(2,1)}, bf16[4,32,768]{2,1,0:T(8,128)(2,1)S(1)}, u32[]{:S(2)}, u32[]{:S(2)}) collective-permute-start(bf16[4,32,768]{2,1,0:T(8,128)(2,1)} %get-tuple-element.67), channel_id=1, source_target_pairs={{0,2},{1,3},{2,0},{3,1},{4,6},{5,7},{6,4},{7,5},{8,10},{9,11},{10,... | collective-permute-start | bytes 589832 | tf_op jit(solution)/shard_map/ppermute | solution.py:305
  84.8 1.6 %collective-permute-done.12.refs_1_ = bf16[4,32,768]{2,1,0:T(8,128)(2,1)S(1)} collective-permute-done((bf16[4,32,768]{2,1,0:T(8,128)(2,1)S(1)}, bf16[4,32,768]{2,1,0:T(8,128)(2,1)S(1)}, u32[]{:S(2)}, u32[]{:S(2)}) %collective-permute-start.12) | collective-permute-done | bytes 196640 | tf_op jit(solution)/shard_map/ppermute | solution.py:305
  87.9 2.1 %regroup.6 = (bf16[4,32,768]{2,1,0:T(8,128)(2,1)}, bf16[4,32,768]{2,1,0:T(8,128)(2,1)}, bf16[4,32,768]{2,1,0:T(8,128)(2,1)}, bf16[4,32,768]{2,1,0:T(8,128)(2,1)}) custom-call(bf16[4,32,768]{2,1,0:T(8,128)(2,1)} %copy-done.4, bf16[4,32,768]{2,1,0:T(8,128)(2,1)} %copy-done.21, bf16[4,32,768]{2,1,0:T(8,128)(2,1)} %copy-done.23, bf16[4,32,768]{2,1,0:T(8,128)(2,1)} %copy-done.25), custom_call_target="tpu_custom_call" | custom-call | bytes 1048576 | tf_op jit(solution)/shard_map/regroup/pallas_call | solution.py:187
  90.0 1.6 %collective-permute-start.15 = (bf16[4,32,768]{2,1,0:T(8,128)(2,1)}, bf16[4,32,768]{2,1,0:T(8,128)(2,1)S(1)}, u32[]{:S(2)}, u32[]{:S(2)}) collective-permute-start(bf16[4,32,768]{2,1,0:T(8,128)(2,1)} %get-tuple-element.62), channel_id=1, source_target_pairs={{0,1},{1,0},{2,3},{3,2},{4,5},{5,4},{6,7},{7,6},{8,9},{9,8},{10,11... | collective-permute-start | bytes 589832 | tf_op jit(solution)/shard_map/ppermute | solution.py:305
  92.9 1.7 %collective-permute-done.20.refs_3_ = bf16[4,32,768]{2,1,0:T(8,128)(2,1)S(1)} collective-permute-done((bf16[4,32,768]{2,1,0:T(8,128)(2,1)}, bf16[4,32,768]{2,1,0:T(8,128)(2,1)S(1)}, u32[]{:S(2)}, u32[]{:S(2)}) %collective-permute-start.20) | collective-permute-done | bytes 196640 | tf_op jit(solution)/shard_map/ppermute | solution.py:305
  95.3 2.1 %regroup.7 = (bf16[4,32,768]{2,1,0:T(8,128)(2,1)}, bf16[4,32,768]{2,1,0:T(8,128)(2,1)}, bf16[4,32,768]{2,1,0:T(8,128)(2,1)}, bf16[4,32,768]{2,1,0:T(8,128)(2,1)}) custom-call(bf16[4,32,768]{2,1,0:T(8,128)(2,1)} %copy-done.2, bf16[4,32,768]{2,1,0:T(8,128)(2,1)} %copy-done.19, bf16[4,32,768]{2,1,0:T(8,128)(2,1)} %copy-done.20, bf16[4,32,768]{2,1,0:T(8,128)(2,1)} %copy-done.22), custom_call_target="tpu_custom_call" | custom-call | bytes 1048576 | tf_op jit(solution)/shard_map/regroup/pallas_call | solution.py:187
  97.5 2.4 %collective-permute-start.21 = (bf16[4,32,768]{2,1,0:T(8,128)(2,1)}, bf16[4,32,768]{2,1,0:T(8,128)(2,1)S(1)}, u32[]{:S(2)}, u32[]{:S(2)}) collective-permute-start(bf16[4,32,768]{2,1,0:T(8,128)(2,1)} %get-tuple-element.70), channel_id=1, source_target_pairs={{0,8},{1,9},{2,10},{3,11},{4,12},{5,13},{6,14},{7,15},{8,0},{9,1},... | collective-permute-start | bytes 589832 | tf_op jit(solution)/shard_map/ppermute | solution.py:305
  99.9 1.9 %collective-permute-start.22 = (bf16[4,32,768]{2,1,0:T(8,128)(2,1)}, bf16[4,32,768]{2,1,0:T(8,128)(2,1)S(1)}, u32[]{:S(2)}, u32[]{:S(2)}) collective-permute-start(bf16[4,32,768]{2,1,0:T(8,128)(2,1)} %get-tuple-element.71), channel_id=1, source_target_pairs={{0,12},{1,13},{2,14},{3,15},{4,8},{5,9},{6,10},{7,11},{8,4},{9,5},... | collective-permute-start | bytes 589832 | tf_op jit(solution)/shard_map/ppermute | solution.py:305
  101.9 1.2 collective-permute-done.17.refs_3_
  103.1 11.7 %collective-permute-done.21.refs_5_ = bf16[4,32,768]{2,1,0:T(8,128)(2,1)S(1)} collective-permute-done((bf16[4,32,768]{2,1,0:T(8,128)(2,1)}, bf16[4,32,768]{2,1,0:T(8,128)(2,1)S(1)}, u32[]{:S(2)}, u32[]{:S(2)}) %collective-permute-start.21) | collective-permute-done | bytes 196640 | tf_op jit(solution)/shard_map/ppermute | solution.py:305
  116.5 3.7 %last.1 = bf16[4,256,768]{2,1,0:T(8,128)(2,1)} custom-call(s32[1]{0:T(128)} %bitcast.me, bf16[2,256,768]{2,1,0:T(8,128)(2,1)} %copy-done, bf16[2,256,768]{2,1,0:T(8,128)(2,1)} %copy-done.1, bf16[4,32,768]{2,1,0:T(8,128)(2,1)} %get-tuple-element.61.refs_0_, bf16[4,32,768]{2,1,0:T(8,128)(2,1)} %copy-done.13, bf16[4,32,768]{2,1,0:T(8,128)(2,1)} %copy-done.14, ...), custom_call_target="tpu_custom_call" | custom-call | flops 786432 | bytes 1572864 | tf_op jit(solution)/shard_map/last/pallas_call | solution.py:289
  (82 shorter events, 14.5 us)
Async XLA Ops:
  0.0 1.7 %copy-start.9 = (bf16[768,768]{1,0:T(8,128)(2,1)S(1)}, bf16[768,768]{1,0:T(8,128)(2,1)}, u32[]{:S(2)}) copy-start(bf16[768,768]{1,0:T(8,128)(2,1)} %wo.3) | copy-start | bytes 3538948
  1.7 2.0 %copy-start.6 = (bf16[768,2304]{1,0:T(8,128)(2,1)S(1)}, bf16[768,2304]{1,0:T(8,128)(2,1)}, u32[]{:S(2)}) copy-start(bf16[768,2304]{1,0:T(8,128)(2,1)} %wqkv.3) | copy-start | bytes 10616836
  3.7 12.7 %copy-start.7 = (bf16[768,2304]{1,0:T(8,128)(2,1)S(1)}, bf16[768,2304]{1,0:T(8,128)(2,1)}, u32[]{:S(2)}) copy-start(bf16[768,2304]{1,0:T(8,128)(2,1)} %wqkv.3) | copy-start | bytes 10616836
  10.8 18.2 %collective-permute-start = (bf16[2,4,16,768]{3,2,1,0:T(8,128)(2,1)S(1)}, bf16[2,4,16,768]{3,2,1,0:T(8,128)(2,1)S(1)}, u32[]{:S(2)}, u32[]{:S(2)}) collective-permute-start(bf16[2,4,16,768]{3,2,1,0:T(8,128)(2,1)S(1)} %get-tuple-element.42), channel_id=1, source_target_pairs={{0,8},{1,9},{2,10},{3,11},{4,12},{5,13},{6,14},{7,15},{8,0},{9,1},... | collective-permute-start | bytes 589832 | tf_op jit(solution)/shard_map/ppermute | solution.py:305
  14.9 14.2 %collective-permute-start.1 = (bf16[2,4,16,768]{3,2,1,0:T(8,128)(2,1)S(1)}, bf16[2,4,16,768]{3,2,1,0:T(8,128)(2,1)S(1)}, u32[]{:S(2)}, u32[]{:S(2)}) collective-permute-start(bf16[2,4,16,768]{3,2,1,0:T(8,128)(2,1)S(1)} %get-tuple-element.43), channel_id=1, source_target_pairs={{0,12},{1,13},{2,14},{3,15},{4,8},{5,9},{6,10},{7,11},{8,4},{9,5},... | collective-permute-start | bytes 589832 | tf_op jit(solution)/shard_map/ppermute | solution.py:305
  16.2 13.3 %collective-permute-start.2 = (bf16[2,4,16,768]{3,2,1,0:T(8,128)(2,1)S(1)}, bf16[2,4,16,768]{3,2,1,0:T(8,128)(2,1)S(1)}, u32[]{:S(2)}, u32[]{:S(2)}) collective-permute-start(bf16[2,4,16,768]{3,2,1,0:T(8,128)(2,1)S(1)} %get-tuple-element.44), channel_id=1, source_target_pairs={{0,4},{1,5},{2,6},{3,7},{4,0},{5,1},{6,2},{7,3},{8,12},{9,13},{10,... | collective-permute-start | bytes 589832 | tf_op jit(solution)/shard_map/ppermute | solution.py:305
  16.4 41.6 %copy-start.8 = (bf16[768,2304]{1,0:T(8,128)(2,1)S(1)}, bf16[768,2304]{1,0:T(8,128)(2,1)}, u32[]{:S(2)}) copy-start(bf16[768,2304]{1,0:T(8,128)(2,1)} %refs_8_.3) | copy-start | bytes 10616836
  24.3 10.5 %collective-permute-start.6 = (bf16[2,4,16,768]{3,2,1,0:T(8,128)(2,1)}, bf16[2,4,16,768]{3,2,1,0:T(8,128)(2,1)}, u32[]{:S(2)}, u32[]{:S(2)}) collective-permute-start(bf16[2,4,16,768]{3,2,1,0:T(8,128)(2,1)} %get-tuple-element.50), channel_id=1, source_target_pairs={{0,1},{1,0},{2,3},{3,2},{4,5},{5,4},{6,7},{7,6},{8,9},{9,8},{10,11... | collective-permute-start | bytes 589832 | tf_op jit(solution)/shard_map/ppermute | solution.py:305
  24.3 11.6 %collective-permute-start.7 = (bf16[2,4,16,768]{3,2,1,0:T(8,128)(2,1)}, bf16[2,4,16,768]{3,2,1,0:T(8,128)(2,1)}, u32[]{:S(2)}, u32[]{:S(2)}) collective-permute-start(bf16[2,4,16,768]{3,2,1,0:T(8,128)(2,1)} %get-tuple-element.51), channel_id=1, source_target_pairs={{0,2},{1,3},{2,0},{3,1},{4,6},{5,7},{6,4},{7,5},{8,10},{9,11},{10,... | collective-permute-start | bytes 589832 | tf_op jit(solution)/shard_map/ppermute | solution.py:305
  29.1 7.2 %collective-permute-start.8 = (bf16[2,4,16,768]{3,2,1,0:T(8,128)(2,1)}, bf16[2,4,16,768]{3,2,1,0:T(8,128)(2,1)}, u32[]{:S(2)}, u32[]{:S(2)}) collective-permute-start(bf16[2,4,16,768]{3,2,1,0:T(8,128)(2,1)} %get-tuple-element.52), channel_id=1, source_target_pairs={{0,3},{1,2},{2,1},{3,0},{4,7},{5,6},{6,5},{7,4},{8,11},{9,10},{10,... | collective-permute-start | bytes 589832 | tf_op jit(solution)/shard_map/ppermute | solution.py:305
  32.6 10.4 %collective-permute-start.3 = (bf16[4,2,16,768]{3,2,1,0:T(8,128)(2,1)}, bf16[4,2,16,768]{3,2,1,0:T(8,128)(2,1)}, u32[]{:S(2)}, u32[]{:S(2)}) collective-permute-start(bf16[4,2,16,768]{3,2,1,0:T(8,128)(2,1)} %get-tuple-element.46), channel_id=1, source_target_pairs={{0,1},{1,0},{2,3},{3,2},{4,5},{5,4},{6,7},{7,6},{8,9},{9,8},{10,11... | collective-permute-start | bytes 589832 | tf_op jit(solution)/shard_map/ppermute | solution.py:305
  34.5 8.6 %collective-permute-start.4 = (bf16[4,2,16,768]{3,2,1,0:T(8,128)(2,1)}, bf16[4,2,16,768]{3,2,1,0:T(8,128)(2,1)}, u32[]{:S(2)}, u32[]{:S(2)}) collective-permute-start(bf16[4,2,16,768]{3,2,1,0:T(8,128)(2,1)} %get-tuple-element.47), channel_id=1, source_target_pairs={{0,2},{1,3},{2,0},{3,1},{4,6},{5,7},{6,4},{7,5},{8,10},{9,11},{10,... | collective-permute-start | bytes 589832 | tf_op jit(solution)/shard_map/ppermute | solution.py:305
  34.7 10.2 %collective-permute-start.5 = (bf16[4,2,16,768]{3,2,1,0:T(8,128)(2,1)}, bf16[4,2,16,768]{3,2,1,0:T(8,128)(2,1)}, u32[]{:S(2)}, u32[]{:S(2)}) collective-permute-start(bf16[4,2,16,768]{3,2,1,0:T(8,128)(2,1)} %get-tuple-element.48), channel_id=1, source_target_pairs={{0,3},{1,2},{2,1},{3,0},{4,7},{5,6},{6,5},{7,4},{8,11},{9,10},{10,... | collective-permute-start | bytes 589832 | tf_op jit(solution)/shard_map/ppermute | solution.py:305
  38.4 18.5 %collective-permute-start.9 = (bf16[4,2,16,768]{3,2,1,0:T(8,128)(2,1)}, bf16[4,2,16,768]{3,2,1,0:T(8,128)(2,1)S(1)}, u32[]{:S(2)}, u32[]{:S(2)}) collective-permute-start(bf16[4,2,16,768]{3,2,1,0:T(8,128)(2,1)} %get-tuple-element.54), channel_id=1, source_target_pairs={{0,8},{1,9},{2,10},{3,11},{4,12},{5,13},{6,14},{7,15},{8,0},{9,1},... | collective-permute-start | bytes 589832 | tf_op jit(solution)/shard_map/ppermute | solution.py:305
  42.6 14.3 %collective-permute-start.10 = (bf16[4,2,16,768]{3,2,1,0:T(8,128)(2,1)}, bf16[4,2,16,768]{3,2,1,0:T(8,128)(2,1)S(1)}, u32[]{:S(2)}, u32[]{:S(2)}) collective-permute-start(bf16[4,2,16,768]{3,2,1,0:T(8,128)(2,1)} %get-tuple-element.55), channel_id=1, source_target_pairs={{0,12},{1,13},{2,14},{3,15},{4,8},{5,9},{6,10},{7,11},{8,4},{9,5},... | collective-permute-start | bytes 589832 | tf_op jit(solution)/shard_map/ppermute | solution.py:305
  43.0 15.1 %collective-permute-start.11 = (bf16[4,2,16,768]{3,2,1,0:T(8,128)(2,1)}, bf16[4,2,16,768]{3,2,1,0:T(8,128)(2,1)S(1)}, u32[]{:S(2)}, u32[]{:S(2)}) collective-permute-start(bf16[4,2,16,768]{3,2,1,0:T(8,128)(2,1)} %get-tuple-element.56), channel_id=1, source_target_pairs={{0,4},{1,5},{2,6},{3,7},{4,0},{5,1},{6,2},{7,3},{8,12},{9,13},{10,... | collective-permute-start | bytes 589832 | tf_op jit(solution)/shard_map/ppermute | solution.py:305
  69.0 17.4 %collective-permute-start.12 = (bf16[4,32,768]{2,1,0:T(8,128)(2,1)S(1)}, bf16[4,32,768]{2,1,0:T(8,128)(2,1)S(1)}, u32[]{:S(2)}, u32[]{:S(2)}) collective-permute-start(bf16[4,32,768]{2,1,0:T(8,128)(2,1)S(1)} %get-tuple-element.58), channel_id=1, source_target_pairs={{0,8},{1,9},{2,10},{3,11},{4,12},{5,13},{6,14},{7,15},{8,0},{9,1},... | collective-permute-start | bytes 589832 | tf_op jit(solution)/shard_map/ppermute | solution.py:305
  72.2 14.3 %collective-permute-start.13 = (bf16[4,32,768]{2,1,0:T(8,128)(2,1)S(1)}, bf16[4,32,768]{2,1,0:T(8,128)(2,1)S(1)}, u32[]{:S(2)}, u32[]{:S(2)}) collective-permute-start(bf16[4,32,768]{2,1,0:T(8,128)(2,1)S(1)} %get-tuple-element.59), channel_id=1, source_target_pairs={{0,12},{1,13},{2,14},{3,15},{4,8},{5,9},{6,10},{7,11},{8,4},{9,5},... | collective-permute-start | bytes 589832 | tf_op jit(solution)/shard_map/ppermute | solution.py:305
  74.8 11.7 %collective-permute-start.14 = (bf16[4,32,768]{2,1,0:T(8,128)(2,1)S(1)}, bf16[4,32,768]{2,1,0:T(8,128)(2,1)S(1)}, u32[]{:S(2)}, u32[]{:S(2)}) collective-permute-start(bf16[4,32,768]{2,1,0:T(8,128)(2,1)S(1)} %get-tuple-element.60), channel_id=1, source_target_pairs={{0,4},{1,5},{2,6},{3,7},{4,0},{5,1},{6,2},{7,3},{8,12},{9,13},{10,... | collective-permute-start | bytes 589832 | tf_op jit(solution)/shard_map/ppermute | solution.py:305
  83.3 8.8 %collective-permute-start.18 = (bf16[4,32,768]{2,1,0:T(8,128)(2,1)}, bf16[4,32,768]{2,1,0:T(8,128)(2,1)S(1)}, u32[]{:S(2)}, u32[]{:S(2)}) collective-permute-start(bf16[4,32,768]{2,1,0:T(8,128)(2,1)} %get-tuple-element.66), channel_id=1, source_target_pairs={{0,1},{1,0},{2,3},{3,2},{4,5},{5,4},{6,7},{7,6},{8,9},{9,8},{10,11... | collective-permute-start | bytes 589832 | tf_op jit(solution)/shard_map/ppermute | solution.py:305
  83.3 9.6 %collective-permute-start.19 = (bf16[4,32,768]{2,1,0:T(8,128)(2,1)}, bf16[4,32,768]{2,1,0:T(8,128)(2,1)S(1)}, u32[]{:S(2)}, u32[]{:S(2)}) collective-permute-start(bf16[4,32,768]{2,1,0:T(8,128)(2,1)} %get-tuple-element.67), channel_id=1, source_target_pairs={{0,2},{1,3},{2,0},{3,1},{4,6},{5,7},{6,4},{7,5},{8,10},{9,11},{10,... | collective-permute-start | bytes 589832 | tf_op jit(solution)/shard_map/ppermute | solution.py:305
  86.4 8.2 %collective-permute-start.20 = (bf16[4,32,768]{2,1,0:T(8,128)(2,1)}, bf16[4,32,768]{2,1,0:T(8,128)(2,1)S(1)}, u32[]{:S(2)}, u32[]{:S(2)}) collective-permute-start(bf16[4,32,768]{2,1,0:T(8,128)(2,1)} %get-tuple-element.68), channel_id=1, source_target_pairs={{0,3},{1,2},{2,1},{3,0},{4,7},{5,6},{6,5},{7,4},{8,11},{9,10},{10,... | collective-permute-start | bytes 589832 | tf_op jit(solution)/shard_map/ppermute | solution.py:305
  90.0 11.9 %collective-permute-start.15 = (bf16[4,32,768]{2,1,0:T(8,128)(2,1)}, bf16[4,32,768]{2,1,0:T(8,128)(2,1)S(1)}, u32[]{:S(2)}, u32[]{:S(2)}) collective-permute-start(bf16[4,32,768]{2,1,0:T(8,128)(2,1)} %get-tuple-element.62), channel_id=1, source_target_pairs={{0,1},{1,0},{2,3},{3,2},{4,5},{5,4},{6,7},{7,6},{8,9},{9,8},{10,11... | collective-permute-start | bytes 589832 | tf_op jit(solution)/shard_map/ppermute | solution.py:305
  91.6 10.3 %collective-permute-start.16 = (bf16[4,32,768]{2,1,0:T(8,128)(2,1)}, bf16[4,32,768]{2,1,0:T(8,128)(2,1)S(1)}, u32[]{:S(2)}, u32[]{:S(2)}) collective-permute-start(bf16[4,32,768]{2,1,0:T(8,128)(2,1)} %get-tuple-element.63), channel_id=1, source_target_pairs={{0,2},{1,3},{2,0},{3,1},{4,6},{5,7},{6,4},{7,5},{8,10},{9,11},{10,... | collective-permute-start | bytes 589832 | tf_op jit(solution)/shard_map/ppermute | solution.py:305
  92.1 2.6 %copy-start.19 = (bf16[4,32,768]{2,1,0:T(8,128)(2,1)}, bf16[4,32,768]{2,1,0:T(8,128)(2,1)S(1)}, u32[]{:S(2)}) copy-start(bf16[4,32,768]{2,1,0:T(8,128)(2,1)S(1)} %collective-permute-done.18.refs_1_) | copy-start | bytes 589828
  92.1 11.0 %collective-permute-start.17 = (bf16[4,32,768]{2,1,0:T(8,128)(2,1)}, bf16[4,32,768]{2,1,0:T(8,128)(2,1)S(1)}, u32[]{:S(2)}, u32[]{:S(2)}) collective-permute-start(bf16[4,32,768]{2,1,0:T(8,128)(2,1)} %get-tuple-element.64), channel_id=1, source_target_pairs={{0,3},{1,2},{2,1},{3,0},{4,7},{5,6},{6,5},{7,4},{8,11},{9,10},{10,... | collective-permute-start | bytes 589832 | tf_op jit(solution)/shard_map/ppermute | solution.py:305
  97.5 17.3 %collective-permute-start.21 = (bf16[4,32,768]{2,1,0:T(8,128)(2,1)}, bf16[4,32,768]{2,1,0:T(8,128)(2,1)S(1)}, u32[]{:S(2)}, u32[]{:S(2)}) collective-permute-start(bf16[4,32,768]{2,1,0:T(8,128)(2,1)} %get-tuple-element.70), channel_id=1, source_target_pairs={{0,8},{1,9},{2,10},{3,11},{4,12},{5,13},{6,14},{7,15},{8,0},{9,1},... | collective-permute-start | bytes 589832 | tf_op jit(solution)/shard_map/ppermute | solution.py:305
  99.9 14.8 %collective-permute-start.22 = (bf16[4,32,768]{2,1,0:T(8,128)(2,1)}, bf16[4,32,768]{2,1,0:T(8,128)(2,1)S(1)}, u32[]{:S(2)}, u32[]{:S(2)}) collective-permute-start(bf16[4,32,768]{2,1,0:T(8,128)(2,1)} %get-tuple-element.71), channel_id=1, source_target_pairs={{0,12},{1,13},{2,14},{3,15},{4,8},{5,9},{6,10},{7,11},{8,4},{9,5},... | collective-permute-start | bytes 589832 | tf_op jit(solution)/shard_map/ppermute | solution.py:305
  101.9 13.9 %copy-start.13 = (bf16[4,32,768]{2,1,0:T(8,128)(2,1)}, bf16[4,32,768]{2,1,0:T(8,128)(2,1)S(1)}, u32[]{:S(2)}) copy-start(bf16[4,32,768]{2,1,0:T(8,128)(2,1)S(1)} %collective-permute-done.15.refs_1_) | copy-start | bytes 589828
  101.9 13.9 %collective-permute-start.23 = (bf16[4,32,768]{2,1,0:T(8,128)(2,1)}, bf16[4,32,768]{2,1,0:T(8,128)(2,1)S(1)}, u32[]{:S(2)}, u32[]{:S(2)}) collective-permute-start(bf16[4,32,768]{2,1,0:T(8,128)(2,1)} %get-tuple-element.72), channel_id=1, source_target_pairs={{0,4},{1,5},{2,6},{3,7},{4,0},{5,1},{6,2},{7,3},{8,12},{9,13},{10,... | collective-permute-start | bytes 589832 | tf_op jit(solution)/shard_map/ppermute | solution.py:305
  101.9 13.9 %copy-start.14 = (bf16[4,32,768]{2,1,0:T(8,128)(2,1)}, bf16[4,32,768]{2,1,0:T(8,128)(2,1)S(1)}, u32[]{:S(2)}) copy-start(bf16[4,32,768]{2,1,0:T(8,128)(2,1)S(1)} %collective-permute-done.16.refs_2_) | copy-start | bytes 589828
  103.1 12.7 %copy-start.15 = (bf16[4,32,768]{2,1,0:T(8,128)(2,1)}, bf16[4,32,768]{2,1,0:T(8,128)(2,1)S(1)}, u32[]{:S(2)}) copy-start(bf16[4,32,768]{2,1,0:T(8,128)(2,1)S(1)} %collective-permute-done.17.refs_3_) | copy-start | bytes 589828
  (20 other events, 17.1 us)

commit v2 on v1

--- a/solution.py
+++ b/solution.py
@@ -16,6 +16,7 @@
 F32 = jnp.float32
 VMEM = pl.BlockSpec(memory_space=pltpu.VMEM)
 SMEM = pl.BlockSpec(memory_space=pltpu.SMEM)
+HBM = pl.BlockSpec(memory_space=pltpu.HBM)
 
 OUTER = (0, 8, 12, 4)
 INNER = (0, 1, 2, 3)
@@ -123,13 +124,34 @@
             )
 
 
-def spatial_kernel(outer_first, me, x, wqkv, wo, middle, o0, o1, o2, o3, a, qkv, mixed, second):
+def spatial_kernel(outer_first, begin, me, x_in, wqkv_in, wo_in, middle, o0, o1, o2, o3, x, a, qkv, mixed, second, sems, *held):
     frames, patches, d = x.shape
     outs = (o0, o1, o2, o3)
     number = me[0]
+    x_copies = [pltpu.make_async_copy(x_in.at[begin + f], x.at[f], sems.at[f]) for f in range(frames)]
+    for copy in x_copies:
+        copy.start()
+    wqkv, wo = wqkv_in, wo_in
+    if held:
+        wqkv, wo = held
+        parts = [pl.ds(c, 192) for c in range(0, d, 192)]
+        copies = [
+            pltpu.make_async_copy(wqkv_in.at[c], wqkv.at[c], sems.at[frames + j])
+            for j, c in enumerate(parts)
+        ]
+        wo_copy = pltpu.make_async_copy(wo_in, wo, sems.at[frames + len(copies)])
+        for copy in copies:
+            copy.start()
+        wo_copy.start()
     for f in range(frames):
+        x_copies[f].wait()
         a[f * patches : (f + 1) * patches, :] = normalize(x[f].astype(F32))
+    if held:
+        for copy in copies:
+            copy.wait()
     layer_rows(a, wqkv, qkv, mixed, patches, patches)
+    if held:
+        wo_copy.wait()
     for f in range(frames):
         r = slice(f * patches, (f + 1) * patches)
         update = jnp.dot(mixed[r, :], wo[...], preferred_element_type=F32)
@@ -146,22 +168,25 @@
                     outs[i][f, p] = rows
 
 
-def spatial(me, x, wqkv, wo, outer_first):
-    frames, patches, d = x.shape
+def spatial(me, x, begin, frames, wqkv, wo, outer_first, fetch):
+    _, patches, d = x.shape
     rows = frames * patches
     block = jax.ShapeDtypeStruct((frames, 4, TILE, d), BF16)
     return pl.pallas_call(
-        functools.partial(spatial_kernel, outer_first),
-        in_specs=[SMEM, VMEM, VMEM, VMEM],
+        functools.partial(spatial_kernel, outer_first, begin),
+        in_specs=[SMEM, HBM] + [HBM if fetch else VMEM] * 2,
         out_specs=[VMEM] * 5,
-        out_shape=[jax.ShapeDtypeStruct(x.shape, BF16)] + [block] * 4,
+        out_shape=[jax.ShapeDtypeStruct((frames, patches, d), BF16)] + [block] * 4,
         scratch_shapes=[
+            pltpu.VMEM((frames, patches, d), BF16),
             pltpu.VMEM((rows, d), BF16),
             pltpu.VMEM((rows, 3 * d), BF16),
             pltpu.VMEM((rows, d), BF16),
             pltpu.VMEM((patches, d), BF16),
-        ],
-        compiler_params=pltpu.CompilerParams(vmem_limit_bytes=32 << 20),
+            pltpu.SemaphoreType.DMA((frames + 3 * d // 256 + 1,)),
+        ]
+        + ([pltpu.VMEM(wqkv.shape, BF16), pltpu.VMEM(wo.shape, BF16)] if fetch else []),
+        compiler_params=pltpu.CompilerParams(vmem_limit_bytes=(58 if fetch else 32) << 20),
         cost_estimate=pl.CostEstimate(
             flops=8 * rows * d * d + 16 * rows * patches * d,
             bytes_accessed=8 * d * d,
@@ -189,6 +214,7 @@
         in_specs=[VMEM] * 4,
         out_specs=[VMEM] * 4,
         out_shape=[jax.ShapeDtypeStruct(shape, BF16)] * 4,
+        compiler_params=pltpu.CompilerParams(vmem_limit_bytes=4 << 20),
         cost_estimate=pl.CostEstimate(flops=0, bytes_accessed=1 << 20, transcendentals=0),
         name="regroup",
     )(*pieces)
@@ -292,6 +318,7 @@
         in_specs=[SMEM] + [VMEM] * 10,
         out_specs=pl.BlockSpec((1, patches, d), lambda f: (f, 0, 0)),
         out_shape=jax.ShapeDtypeStruct((4, patches, d), BF16),
+        compiler_params=pltpu.CompilerParams(vmem_limit_bytes=16 << 20),
         cost_estimate=pl.CostEstimate(
             flops=patches * d * 4, bytes_accessed=patches * d * 8, transcendentals=0
         ),
@@ -309,9 +336,9 @@
 
 def shards(frames_in, qkv_spatial, out_spatial, qkv_temporal, out_temporal):
     me = lax.axis_index("wide").astype(jnp.int32).reshape(1)
-    mid01, *pieces = spatial(me, frames_in[:2], qkv_spatial, out_spatial, True)
+    mid01, *pieces = spatial(me, frames_in, 0, 2, qkv_spatial, out_spatial, True, True)
     z_parts = exchange(regroup(exchange(pieces, OUTER)), INNER)
-    mid23, *pieces = spatial(me, frames_in[2:], qkv_spatial, out_spatial, False)
+    mid23, *pieces = spatial(me, frames_in, 2, 2, qkv_spatial, out_spatial, False, False)
     y_parts = exchange(regroup(exchange(pieces, INNER)), OUTER)
     pieces = temporal(0, z_parts, y_parts, qkv_temporal, out_temporal, True)
     early = exchange(regroup(exchange(pieces, OUTER)), INNER)

time: 121 us -> 105 us (0.87)
  local copies, waits for them, and re-layouts: 15 us -> 1.3 us
  waiting for transfers between devices: 36.3 us -> 45 us
  Pallas kernels: 38.8 us -> 30.9 us
  starting transfers between devices: 29.8 us -> 27 us
    unnamed x56 -> x14, local copies, waits for them, and re-layouts: 13.4 us -> 1.3 us
    ppermute x24, waiting for transfers between devices: 36.3 us -> 45 us  [exchange(): lax.ppermute(piece, 'wide', [(w, w ^ mask) for w in range(size)])]
    pallas_call x4, Pallas kernels: 8.52 us -> 0.21 us  [regroup(): pl.pallas_call(regroup_kernel, in_specs=[VMEM] * 4, out_specs=[VMEM] * 4,...]
    pallas_call x2, Pallas kernels: 11.7 us -> 17 us  [spatial(): pl.pallas_call(functools.partial(spatial_kernel, outer_first, begin), in_...]
    pallas_call x2, Pallas kernels: 14.9 us -> 11.9 us  [temporal(): pl.pallas_call(functools.partial(temporal_kernel, half, outer_first), in_...]
    ppermute x24, starting transfers between devices: 29.8 us -> 27 us  [exchange(): lax.ppermute(piece, 'wide', [(w, w ^ mask) for w in range(size)])]
    pallas_call x1, Pallas kernels: 3.66 us -> 1.82 us  [last(): pl.pallas_call(last_kernel, grid=(4,), in_specs=[SMEM] + [VMEM] * 10, out...]
    slice x1 -> x0, local copies, waits for them, and re-layouts: 1.57 us -> none  [shards(): mid23, *pieces = spatial(me, frames_in[2:], qkv_spatial, out_spatial, False)]
  transfers between devices with their start and end apart: 24 -> 24, of which waited for: 12 -> 13; matrix products, arithmetic and copies ran while one was open for 0% -> 0% of each run, Pallas kernels for 19% -> 12%
where the time goes in v2:
time: 105 us; the launch traced here: 104 us
  waiting for transfers between devices  45 us (43%)
  Pallas kernels  30.9 us (29%)
  starting transfers between devices  27 us (26%)
  local copies, waits for them, and re-layouts  1.3 us (1%)
    ppermute x24, waiting for transfers between devices, exchange(): lax.ppermute(piece, 'wide', [(w, w ^ mask) for w in range(size)])  45 us
    ppermute x24, starting transfers between devices, exchange(): lax.ppermute(piece, 'wide', [(w, w ^ mask) for w in range(size)])  27 us
    pallas_call x2, Pallas kernels, spatial(): pl.pallas_call(functools.partial(spatial_kernel, outer_first, begin), in_...  17 us
    pallas_call x2, Pallas kernels, temporal(): pl.pallas_call(functools.partial(temporal_kernel, half, outer_first), in_...  11.9 us
  transfers between devices with their start and end apart: 24, of which 13 were waited for; matrix products, arithmetic and copies ran while one was open for 0% of the time, Pallas kernels for 12%

profile of v2, /device:TPU:0, one launch (start us, length us, event | category | flops | bytes accessed | tf_op | source)
XLA Modules:
  0.0 104.3 jit_solution(8193862992510087576)
XLA Ops:
  0.0 10.6 %spatial_outer.1 = (bf16[2,256,768]{2,1,0:T(8,128)(2,1)}, bf16[2,4,16,768]{3,2,1,0:T(8,128)(2,1)}, bf16[2,4,16,768]{3,2,1,0:T(8,128)(2,1)}, bf16[2,4,16,768]{3,2,1,0:T(8,128)(2,1)}, bf16[2,4,16,768]{3,2,1,0:T(8,128)(2,1)}) custom-call(s32[1]{0:T(128)} %bitcast.me, bf16[4,256,768]{2,1,0:T(8,128)(2,1)} %x_in.3, bf16[768,2304]{1,0:T(8,128)(2,1)} %wqkv_in.3, ...), custom_call_target="tpu_custom_call" | custom-call | flops 4026531840 | bytes 4718592 | tf_op jit(solution)/shard_map/spatial_outer/pallas_call | solution.py:175
  10.6 4.1 %collective-permute-start = (bf16[2,4,16,768]{3,2,1,0:T(8,128)(2,1)}, bf16[2,4,16,768]{3,2,1,0:T(8,128)(2,1)S(1)}, u32[]{:S(2)}, u32[]{:S(2)}) collective-permute-start(bf16[2,4,16,768]{3,2,1,0:T(8,128)(2,1)} %get-tuple-element.42), channel_id=1, source_target_pairs={{0,8},{1,9},{2,10},{3,11},{4,12},{5,13},{6,14},{7,15},{8,0},{9,1},... | collective-permute-start | bytes 589832 | tf_op jit(solution)/shard_map/ppermute | solution.py:332
  14.7 1.3 %collective-permute-start.1 = (bf16[2,4,16,768]{3,2,1,0:T(8,128)(2,1)}, bf16[2,4,16,768]{3,2,1,0:T(8,128)(2,1)S(1)}, u32[]{:S(2)}, u32[]{:S(2)}) collective-permute-start(bf16[2,4,16,768]{3,2,1,0:T(8,128)(2,1)} %get-tuple-element.43), channel_id=1, source_target_pairs={{0,12},{1,13},{2,14},{3,15},{4,8},{5,9},{6,10},{7,11},{8,4},{9,5},... | collective-permute-start | bytes 589832 | tf_op jit(solution)/shard_map/ppermute | solution.py:332
  16.3 1.3 %copy-done.5 = bf16[768,768]{1,0:T(8,128)(2,1)S(1)} copy-done((bf16[768,768]{1,0:T(8,128)(2,1)S(1)}, bf16[768,768]{1,0:T(8,128)(2,1)}, u32[]{:S(2)}) %copy-start.5) | copy-done | bytes 1179672
  17.6 6.4 %spatial_inner.1 = (bf16[2,256,768]{2,1,0:T(8,128)(2,1)S(1)}, bf16[2,4,16,768]{3,2,1,0:T(8,128)(2,1)S(1)}, bf16[2,4,16,768]{3,2,1,0:T(8,128)(2,1)S(1)}, bf16[2,4...) custom-call(s32[1]{0:T(128)} %bitcast.me, bf16[4,256,768]{2,1,0:T(8,128)(2,1)S(1)} %copy-done.4, ...), custom_call_target="tpu_custom_call" | custom-call | flops 4026531840 | bytes 4718592 | tf_op jit(solution)/shard_map/spatial_inner/pallas_call | solution.py:175
  24.0 1.6 %collective-permute-start.7 = (bf16[2,4,16,768]{3,2,1,0:T(8,128)(2,1)S(1)}, bf16[2,4,16,768]{3,2,1,0:T(8,128)(2,1)S(1)}, u32[]{:S(2)}, u32[]{:S(2)}) collective-permute-start(bf16[2,4,16,768]{3,2,1,0:T(8,128)(2,1)S(1)} %get-tuple-element.51), channel_id=1, source_target_pairs={{0,2},{1,3},{2,0},{3,1},{4,6},{5,7},{6,4},{7,5},{8,10},{9,11},{10,... | collective-permute-start | bytes 589832 | tf_op jit(solution)/shard_map/ppermute | solution.py:332
  25.6 3.5 %collective-permute-done.refs_1_ = bf16[2,4,16,768]{3,2,1,0:T(8,128)(2,1)S(1)} collective-permute-done((bf16[2,4,16,768]{3,2,1,0:T(8,128)(2,1)}, bf16[2,4,16,768]{3,2,1,0:T(8,128)(2,1)S(1)}, u32[]{:S(2)}, u32[]{:S(2)}) %collective-permute-start) | collective-permute-done | bytes 196640 | tf_op jit(solution)/shard_map/ppermute | solution.py:332
  29.1 0.5 collective-permute-done.2.refs_3_
  29.7 1.5 %collective-permute-start.3 = (bf16[4,2,16,768]{3,2,1,0:T(8,128)(2,1)S(1)}, bf16[4,2,16,768]{3,2,1,0:T(8,128)(2,1)S(1)}, u32[]{:S(2)}, u32[]{:S(2)}) collective-permute-start(bf16[4,2,16,768]{3,2,1,0:T(8,128)(2,1)S(1)} %get-tuple-element.46), channel_id=1, source_target_pairs={{0,1},{1,0},{2,3},{3,2},{4,5},{5,4},{6,7},{7,6},{8,9},{9,8},{10,11... | collective-permute-start | bytes 589832 | tf_op jit(solution)/shard_map/ppermute | solution.py:332
  31.4 1.3 %collective-permute-start.5 = (bf16[4,2,16,768]{3,2,1,0:T(8,128)(2,1)S(1)}, bf16[4,2,16,768]{3,2,1,0:T(8,128)(2,1)S(1)}, u32[]{:S(2)}, u32[]{:S(2)}) collective-permute-start(bf16[4,2,16,768]{3,2,1,0:T(8,128)(2,1)S(1)} %get-tuple-element.48), channel_id=1, source_target_pairs={{0,3},{1,2},{2,1},{3,0},{4,7},{5,6},{6,5},{7,4},{8,11},{9,10},{10,... | collective-permute-start | bytes 589832 | tf_op jit(solution)/shard_map/ppermute | solution.py:332
  32.7 3.3 %collective-permute-done.8.refs_3_ = bf16[2,4,16,768]{3,2,1,0:T(8,128)(2,1)S(1)} collective-permute-done((bf16[2,4,16,768]{3,2,1,0:T(8,128)(2,1)S(1)}, bf16[2,4,16,768]{3,2,1,0:T(8,128)(2,1)S(1)}, u32[]{:S(2)}, u32[]{:S(2)}) %collective-permute-start.8) | collective-permute-done | bytes 196640 | tf_op jit(solution)/shard_map/ppermute | solution.py:332
  36.0 2.0 %collective-permute-start.9 = (bf16[4,2,16,768]{3,2,1,0:T(8,128)(2,1)S(1)}, bf16[4,2,16,768]{3,2,1,0:T(8,128)(2,1)S(1)}, u32[]{:S(2)}, u32[]{:S(2)}) collective-permute-start(bf16[4,2,16,768]{3,2,1,0:T(8,128)(2,1)S(1)} %get-tuple-element.54), channel_id=1, source_target_pairs={{0,8},{1,9},{2,10},{3,11},{4,12},{5,13},{6,14},{7,15},{8,0},{9,1},... | collective-permute-start | bytes 589832 | tf_op jit(solution)/shard_map/ppermute | solution.py:332
  38.0 1.3 %collective-permute-start.10 = (bf16[4,2,16,768]{3,2,1,0:T(8,128)(2,1)S(1)}, bf16[4,2,16,768]{3,2,1,0:T(8,128)(2,1)S(1)}, u32[]{:S(2)}, u32[]{:S(2)}) collective-permute-start(bf16[4,2,16,768]{3,2,1,0:T(8,128)(2,1)S(1)} %get-tuple-element.55), channel_id=1, source_target_pairs={{0,12},{1,13},{2,14},{3,15},{4,8},{5,9},{6,10},{7,11},{8,4},{9,5},... | collective-permute-start | bytes 589832 | tf_op jit(solution)/shard_map/ppermute | solution.py:332
  39.7 1.2 %collective-permute-done.4.refs_2_ = bf16[4,2,16,768]{3,2,1,0:T(8,128)(2,1)S(1)} collective-permute-done((bf16[4,2,16,768]{3,2,1,0:T(8,128)(2,1)S(1)}, bf16[4,2,16,768]{3,2,1,0:T(8,128)(2,1)S(1)}, u32[]{:S(2)}, u32[]{:S(2)}) %collective-permute-start.4) | collective-permute-done | bytes 196640 | tf_op jit(solution)/shard_map/ppermute | solution.py:332
  40.9 3.5 %collective-permute-done.5.refs_3_ = bf16[4,2,16,768]{3,2,1,0:T(8,128)(2,1)S(1)} collective-permute-done((bf16[4,2,16,768]{3,2,1,0:T(8,128)(2,1)S(1)}, bf16[4,2,16,768]{3,2,1,0:T(8,128)(2,1)S(1)}, u32[]{:S(2)}, u32[]{:S(2)}) %collective-permute-start.5) | collective-permute-done | bytes 196640 | tf_op jit(solution)/shard_map/ppermute | solution.py:332
  44.4 8.8 %collective-permute-done.9.refs_5_ = bf16[4,2,16,768]{3,2,1,0:T(8,128)(2,1)S(1)} collective-permute-done((bf16[4,2,16,768]{3,2,1,0:T(8,128)(2,1)S(1)}, bf16[4,2,16,768]{3,2,1,0:T(8,128)(2,1)S(1)}, u32[]{:S(2)}, u32[]{:S(2)}) %collective-permute-start.9) | collective-permute-done | bytes 196640 | tf_op jit(solution)/shard_map/ppermute | solution.py:332
  53.2 0.9 collective-permute-done.11.refs_7_
  54.1 5.8 %temporal.2 = (bf16[4,32,768]{2,1,0:T(8,128)(2,1)S(1)}, bf16[4,32,768]{2,1,0:T(8,128)(2,1)S(1)}, bf16[4,32,768]{2,1,0:T(8,128)(2,1)S(1)}, bf16[4,32,768]{2,1,0:T(8,128)(2,1)S(1)}) custom-call(bf16[4,2,16,768]{3,2,1,0:T(8,128)(2,1)S(1)} %get-tuple-element.45.refs_0_, bf16[4,2,16,768]{3,2,1,0:T(8,128)(2,1)S(1)} %collective-permute-done.3.refs_1_, ...), custom_call_target="tpu_custom_call" | custom-call | flops 4026531840 | bytes 4718592 | tf_op jit(solution)/shard_map/temporal/pallas_call | solution.py:269
  59.9 4.7 %collective-permute-start.12 = (bf16[4,32,768]{2,1,0:T(8,128)(2,1)S(1)}, bf16[4,32,768]{2,1,0:T(8,128)(2,1)S(1)}, u32[]{:S(2)}, u32[]{:S(2)}) collective-permute-start(bf16[4,32,768]{2,1,0:T(8,128)(2,1)S(1)} %get-tuple-element.58), channel_id=1, source_target_pairs={{0,8},{1,9},{2,10},{3,11},{4,12},{5,13},{6,14},{7,15},{8,0},{9,1},... | collective-permute-start | bytes 589832 | tf_op jit(solution)/shard_map/ppermute | solution.py:332
  64.6 1.2 %collective-permute-start.13 = (bf16[4,32,768]{2,1,0:T(8,128)(2,1)S(1)}, bf16[4,32,768]{2,1,0:T(8,128)(2,1)S(1)}, u32[]{:S(2)}, u32[]{:S(2)}) collective-permute-start(bf16[4,32,768]{2,1,0:T(8,128)(2,1)S(1)} %get-tuple-element.59), channel_id=1, source_target_pairs={{0,12},{1,13},{2,14},{3,15},{4,8},{5,9},{6,10},{7,11},{8,4},{9,5},... | collective-permute-start | bytes 589832 | tf_op jit(solution)/shard_map/ppermute | solution.py:332
  65.8 6.1 %temporal.3 = (bf16[4,32,768]{2,1,0:T(8,128)(2,1)S(1)}, bf16[4,32,768]{2,1,0:T(8,128)(2,1)S(1)}, bf16[4,32,768]{2,1,0:T(8,128)(2,1)S(1)}, bf16[4,32,768]{2,1,0:T(8,128)(2,1)S(1)}) custom-call(bf16[4,2,16,768]{3,2,1,0:T(8,128)(2,1)S(1)} %get-tuple-element.45.refs_0_, bf16[4,2,16,768]{3,2,1,0:T(8,128)(2,1)S(1)} %collective-permute-done.3.refs_1_, ...), custom_call_target="tpu_custom_call" | custom-call | flops 4026531840 | bytes 4718592 | tf_op jit(solution)/shard_map/temporal/pallas_call | solution.py:269
  72.0 1.0 collective-permute-start.19
  73.1 5.8 %collective-permute-done.12.refs_1_ = bf16[4,32,768]{2,1,0:T(8,128)(2,1)S(1)} collective-permute-done((bf16[4,32,768]{2,1,0:T(8,128)(2,1)S(1)}, bf16[4,32,768]{2,1,0:T(8,128)(2,1)S(1)}, u32[]{:S(2)}, u32[]{:S(2)}) %collective-permute-start.12) | collective-permute-done | bytes 196640 | tf_op jit(solution)/shard_map/ppermute | solution.py:332
  79.6 0.6 collective-permute-start.15
  80.2 1.0 collective-permute-start.16
  81.7 4.3 %collective-permute-done.20.refs_3_ = bf16[4,32,768]{2,1,0:T(8,128)(2,1)S(1)} collective-permute-done((bf16[4,32,768]{2,1,0:T(8,128)(2,1)S(1)}, bf16[4,32,768]{2,1,0:T(8,128)(2,1)S(1)}, u32[]{:S(2)}, u32[]{:S(2)}) %collective-permute-start.20) | collective-permute-done | bytes 196640 | tf_op jit(solution)/shard_map/ppermute | solution.py:332
  86.4 1.2 %collective-permute-start.22 = (bf16[4,32,768]{2,1,0:T(8,128)(2,1)S(1)}, bf16[4,32,768]{2,1,0:T(8,128)(2,1)S(1)}, u32[]{:S(2)}, u32[]{:S(2)}) collective-permute-start(bf16[4,32,768]{2,1,0:T(8,128)(2,1)S(1)} %get-tuple-element.71), channel_id=1, source_target_pairs={{0,12},{1,13},{2,14},{3,15},{4,8},{5,9},{6,10},{7,11},{8,4},{9,5},... | collective-permute-start | bytes 589832 | tf_op jit(solution)/shard_map/ppermute | solution.py:332
  87.6 2.0 %collective-permute-start.23 = (bf16[4,32,768]{2,1,0:T(8,128)(2,1)S(1)}, bf16[4,32,768]{2,1,0:T(8,128)(2,1)S(1)}, u32[]{:S(2)}, u32[]{:S(2)}) collective-permute-start(bf16[4,32,768]{2,1,0:T(8,128)(2,1)S(1)} %get-tuple-element.72), channel_id=1, source_target_pairs={{0,4},{1,5},{2,6},{3,7},{4,0},{5,1},{6,2},{7,3},{8,12},{9,13},{10,... | collective-permute-start | bytes 589832 | tf_op jit(solution)/shard_map/ppermute | solution.py:332
  89.7 4.5 %collective-permute-done.17.refs_3_ = bf16[4,32,768]{2,1,0:T(8,128)(2,1)S(1)} collective-permute-done((bf16[4,32,768]{2,1,0:T(8,128)(2,1)S(1)}, bf16[4,32,768]{2,1,0:T(8,128)(2,1)S(1)}, u32[]{:S(2)}, u32[]{:S(2)}) %collective-permute-start.17) | collective-permute-done | bytes 196640 | tf_op jit(solution)/shard_map/ppermute | solution.py:332
  94.2 7.1 %collective-permute-done.21.refs_5_ = bf16[4,32,768]{2,1,0:T(8,128)(2,1)S(1)} collective-permute-done((bf16[4,32,768]{2,1,0:T(8,128)(2,1)S(1)}, bf16[4,32,768]{2,1,0:T(8,128)(2,1)S(1)}, u32[]{:S(2)}, u32[]{:S(2)}) %collective-permute-start.21) | collective-permute-done | bytes 196640 | tf_op jit(solution)/shard_map/ppermute | solution.py:332
  101.2 1.3 %collective-permute-done.23.refs_7_ = bf16[4,32,768]{2,1,0:T(8,128)(2,1)S(1)} collective-permute-done((bf16[4,32,768]{2,1,0:T(8,128)(2,1)S(1)}, bf16[4,32,768]{2,1,0:T(8,128)(2,1)S(1)}, u32[]{:S(2)}, u32[]{:S(2)}) %collective-permute-start.23) | collective-permute-done | bytes 196640 | tf_op jit(solution)/shard_map/ppermute | solution.py:332
  102.5 1.8 %last.1 = bf16[4,256,768]{2,1,0:T(8,128)(2,1)} custom-call(s32[1]{0:T(128)} %bitcast.me, bf16[2,256,768]{2,1,0:T(8,128)(2,1)S(1)} %copy-done, bf16[2,256,768]{2,1,0:T(8,128)(2,1)S(1)} %get-tuple-element.40.mid23, bf16[4,32,768]{2,1,0:T(8,128)(2,1)S(1)} %get-tuple-element.61.refs_0_, bf16[4,32,768]{2,1,0:T(8,128)(2,1)S(1)} %collective-permute-done.15.refs_1_, ...), custom_call_target="tpu_custom_call" | custom-call | flops 786432 | bytes 1572864 | tf_op jit(solution)/shard_map/last/pallas_call | solution.py:315
  (39 shorter events, 2.6 us)
Async XLA Ops:
  0.0 16.3 %copy-start.2 = (bf16[768,2304]{1,0:T(8,128)(2,1)S(1)}, bf16[768,2304]{1,0:T(8,128)(2,1)}, u32[]{:S(2)}) copy-start(bf16[768,2304]{1,0:T(8,128)(2,1)} %wqkv_in.3) | copy-start | bytes 10616836
  0.0 16.3 %copy-start.4 = (bf16[4,256,768]{2,1,0:T(8,128)(2,1)S(1)}, bf16[4,256,768]{2,1,0:T(8,128)(2,1)}, u32[]{:S(2)}) copy-start(bf16[4,256,768]{2,1,0:T(8,128)(2,1)} %x_in.3) | copy-start | bytes 4718596
  10.6 18.5 %collective-permute-start = (bf16[2,4,16,768]{3,2,1,0:T(8,128)(2,1)}, bf16[2,4,16,768]{3,2,1,0:T(8,128)(2,1)S(1)}, u32[]{:S(2)}, u32[]{:S(2)}) collective-permute-start(bf16[2,4,16,768]{3,2,1,0:T(8,128)(2,1)} %get-tuple-element.42), channel_id=1, source_target_pairs={{0,8},{1,9},{2,10},{3,11},{4,12},{5,13},{6,14},{7,15},{8,0},{9,1},... | collective-permute-start | bytes 589832 | tf_op jit(solution)/shard_map/ppermute | solution.py:332
  14.7 14.4 %collective-permute-start.1 = (bf16[2,4,16,768]{3,2,1,0:T(8,128)(2,1)}, bf16[2,4,16,768]{3,2,1,0:T(8,128)(2,1)S(1)}, u32[]{:S(2)}, u32[]{:S(2)}) collective-permute-start(bf16[2,4,16,768]{3,2,1,0:T(8,128)(2,1)} %get-tuple-element.43), channel_id=1, source_target_pairs={{0,12},{1,13},{2,14},{3,15},{4,8},{5,9},{6,10},{7,11},{8,4},{9,5},... | collective-permute-start | bytes 589832 | tf_op jit(solution)/shard_map/ppermute | solution.py:332
  16.0 13.6 %copy-start.1 = (bf16[2,4,16,768]{3,2,1,0:T(8,128)(2,1)S(1)}, bf16[2,4,16,768]{3,2,1,0:T(8,128)(2,1)}, u32[]{:S(2)}) copy-start(bf16[2,4,16,768]{3,2,1,0:T(8,128)(2,1)} %get-tuple-element.41.refs_0_) | copy-start | bytes 589828
  16.0 13.6 %collective-permute-start.2 = (bf16[2,4,16,768]{3,2,1,0:T(8,128)(2,1)}, bf16[2,4,16,768]{3,2,1,0:T(8,128)(2,1)S(1)}, u32[]{:S(2)}, u32[]{:S(2)}) collective-permute-start(bf16[2,4,16,768]{3,2,1,0:T(8,128)(2,1)} %get-tuple-element.44), channel_id=1, source_target_pairs={{0,4},{1,5},{2,6},{3,7},{4,0},{5,1},{6,2},{7,3},{8,12},{9,13},{10,... | collective-permute-start | bytes 589832 | tf_op jit(solution)/shard_map/ppermute | solution.py:332
  16.3 1.3 %copy-start.5 = (bf16[768,768]{1,0:T(8,128)(2,1)S(1)}, bf16[768,768]{1,0:T(8,128)(2,1)}, u32[]{:S(2)}) copy-start(bf16[768,768]{1,0:T(8,128)(2,1)} %wo_in.3) | copy-start | bytes 3538948
  17.6 36.5 %copy-start.3 = (bf16[768,2304]{1,0:T(8,128)(2,1)S(1)}, bf16[768,2304]{1,0:T(8,128)(2,1)}, u32[]{:S(2)}) copy-start(bf16[768,2304]{1,0:T(8,128)(2,1)} %refs_8_.3) | copy-start | bytes 10616836
  24.0 30.1 %copy-start.6 = (bf16[768,768]{1,0:T(8,128)(2,1)S(1)}, bf16[768,768]{1,0:T(8,128)(2,1)}, u32[]{:S(2)}) copy-start(bf16[768,768]{1,0:T(8,128)(2,1)} %refs_9_.3) | copy-start | bytes 3538948
  24.0 7.4 %collective-permute-start.6 = (bf16[2,4,16,768]{3,2,1,0:T(8,128)(2,1)S(1)}, bf16[2,4,16,768]{3,2,1,0:T(8,128)(2,1)S(1)}, u32[]{:S(2)}, u32[]{:S(2)}) collective-permute-start(bf16[2,4,16,768]{3,2,1,0:T(8,128)(2,1)S(1)} %get-tuple-element.50), channel_id=1, source_target_pairs={{0,1},{1,0},{2,3},{3,2},{4,5},{5,4},{6,7},{7,6},{8,9},{9,8},{10,11... | collective-permute-start | bytes 589832 | tf_op jit(solution)/shard_map/ppermute | solution.py:332
  24.0 8.6 %collective-permute-start.7 = (bf16[2,4,16,768]{3,2,1,0:T(8,128)(2,1)S(1)}, bf16[2,4,16,768]{3,2,1,0:T(8,128)(2,1)S(1)}, u32[]{:S(2)}, u32[]{:S(2)}) collective-permute-start(bf16[2,4,16,768]{3,2,1,0:T(8,128)(2,1)S(1)} %get-tuple-element.51), channel_id=1, source_target_pairs={{0,2},{1,3},{2,0},{3,1},{4,6},{5,7},{6,4},{7,5},{8,10},{9,11},{10,... | collective-permute-start | bytes 589832 | tf_op jit(solution)/shard_map/ppermute | solution.py:332
  29.1 6.9 %collective-permute-start.8 = (bf16[2,4,16,768]{3,2,1,0:T(8,128)(2,1)S(1)}, bf16[2,4,16,768]{3,2,1,0:T(8,128)(2,1)S(1)}, u32[]{:S(2)}, u32[]{:S(2)}) collective-permute-start(bf16[2,4,16,768]{3,2,1,0:T(8,128)(2,1)S(1)} %get-tuple-element.52), channel_id=1, source_target_pairs={{0,3},{1,2},{2,1},{3,0},{4,7},{5,6},{6,5},{7,4},{8,11},{9,10},{10,... | collective-permute-start | bytes 589832 | tf_op jit(solution)/shard_map/ppermute | solution.py:332
  29.7 9.7 %collective-permute-start.3 = (bf16[4,2,16,768]{3,2,1,0:T(8,128)(2,1)S(1)}, bf16[4,2,16,768]{3,2,1,0:T(8,128)(2,1)S(1)}, u32[]{:S(2)}, u32[]{:S(2)}) collective-permute-start(bf16[4,2,16,768]{3,2,1,0:T(8,128)(2,1)S(1)} %get-tuple-element.46), channel_id=1, source_target_pairs={{0,1},{1,0},{2,3},{3,2},{4,5},{5,4},{6,7},{7,6},{8,9},{9,8},{10,11... | collective-permute-start | bytes 589832 | tf_op jit(solution)/shard_map/ppermute | solution.py:332
  31.2 9.6 %collective-permute-start.4 = (bf16[4,2,16,768]{3,2,1,0:T(8,128)(2,1)S(1)}, bf16[4,2,16,768]{3,2,1,0:T(8,128)(2,1)S(1)}, u32[]{:S(2)}, u32[]{:S(2)}) collective-permute-start(bf16[4,2,16,768]{3,2,1,0:T(8,128)(2,1)S(1)} %get-tuple-element.47), channel_id=1, source_target_pairs={{0,2},{1,3},{2,0},{3,1},{4,6},{5,7},{6,4},{7,5},{8,10},{9,11},{10,... | collective-permute-start | bytes 589832 | tf_op jit(solution)/shard_map/ppermute | solution.py:332
  31.4 13.0 %collective-permute-start.5 = (bf16[4,2,16,768]{3,2,1,0:T(8,128)(2,1)S(1)}, bf16[4,2,16,768]{3,2,1,0:T(8,128)(2,1)S(1)}, u32[]{:S(2)}, u32[]{:S(2)}) collective-permute-start(bf16[4,2,16,768]{3,2,1,0:T(8,128)(2,1)S(1)} %get-tuple-element.48), channel_id=1, source_target_pairs={{0,3},{1,2},{2,1},{3,0},{4,7},{5,6},{6,5},{7,4},{8,11},{9,10},{10,... | collective-permute-start | bytes 589832 | tf_op jit(solution)/shard_map/ppermute | solution.py:332
  36.0 17.1 %collective-permute-start.9 = (bf16[4,2,16,768]{3,2,1,0:T(8,128)(2,1)S(1)}, bf16[4,2,16,768]{3,2,1,0:T(8,128)(2,1)S(1)}, u32[]{:S(2)}, u32[]{:S(2)}) collective-permute-start(bf16[4,2,16,768]{3,2,1,0:T(8,128)(2,1)S(1)} %get-tuple-element.54), channel_id=1, source_target_pairs={{0,8},{1,9},{2,10},{3,11},{4,12},{5,13},{6,14},{7,15},{8,0},{9,1},... | collective-permute-start | bytes 589832 | tf_op jit(solution)/shard_map/ppermute | solution.py:332
  38.0 15.1 %collective-permute-start.10 = (bf16[4,2,16,768]{3,2,1,0:T(8,128)(2,1)S(1)}, bf16[4,2,16,768]{3,2,1,0:T(8,128)(2,1)S(1)}, u32[]{:S(2)}, u32[]{:S(2)}) collective-permute-start(bf16[4,2,16,768]{3,2,1,0:T(8,128)(2,1)S(1)} %get-tuple-element.55), channel_id=1, source_target_pairs={{0,12},{1,13},{2,14},{3,15},{4,8},{5,9},{6,10},{7,11},{8,4},{9,5},... | collective-permute-start | bytes 589832 | tf_op jit(solution)/shard_map/ppermute | solution.py:332
  39.4 14.7 %collective-permute-start.11 = (bf16[4,2,16,768]{3,2,1,0:T(8,128)(2,1)S(1)}, bf16[4,2,16,768]{3,2,1,0:T(8,128)(2,1)S(1)}, u32[]{:S(2)}, u32[]{:S(2)}) collective-permute-start(bf16[4,2,16,768]{3,2,1,0:T(8,128)(2,1)S(1)} %get-tuple-element.56), channel_id=1, source_target_pairs={{0,4},{1,5},{2,6},{3,7},{4,0},{5,1},{6,2},{7,3},{8,12},{9,13},{10,... | collective-permute-start | bytes 589832 | tf_op jit(solution)/shard_map/ppermute | solution.py:332
  59.9 18.9 %collective-permute-start.12 = (bf16[4,32,768]{2,1,0:T(8,128)(2,1)S(1)}, bf16[4,32,768]{2,1,0:T(8,128)(2,1)S(1)}, u32[]{:S(2)}, u32[]{:S(2)}) collective-permute-start(bf16[4,32,768]{2,1,0:T(8,128)(2,1)S(1)} %get-tuple-element.58), channel_id=1, source_target_pairs={{0,8},{1,9},{2,10},{3,11},{4,12},{5,13},{6,14},{7,15},{8,0},{9,1},... | collective-permute-start | bytes 589832 | tf_op jit(solution)/shard_map/ppermute | solution.py:332
  64.6 14.6 %collective-permute-start.13 = (bf16[4,32,768]{2,1,0:T(8,128)(2,1)S(1)}, bf16[4,32,768]{2,1,0:T(8,128)(2,1)S(1)}, u32[]{:S(2)}, u32[]{:S(2)}) collective-permute-start(bf16[4,32,768]{2,1,0:T(8,128)(2,1)S(1)} %get-tuple-element.59), channel_id=1, source_target_pairs={{0,12},{1,13},{2,14},{3,15},{4,8},{5,9},{6,10},{7,11},{8,4},{9,5},... | collective-permute-start | bytes 589832 | tf_op jit(solution)/shard_map/ppermute | solution.py:332
  65.8 13.7 %collective-permute-start.14 = (bf16[4,32,768]{2,1,0:T(8,128)(2,1)S(1)}, bf16[4,32,768]{2,1,0:T(8,128)(2,1)S(1)}, u32[]{:S(2)}, u32[]{:S(2)}) collective-permute-start(bf16[4,32,768]{2,1,0:T(8,128)(2,1)S(1)} %get-tuple-element.60), channel_id=1, source_target_pairs={{0,4},{1,5},{2,6},{3,7},{4,0},{5,1},{6,2},{7,3},{8,12},{9,13},{10,... | collective-permute-start | bytes 589832 | tf_op jit(solution)/shard_map/ppermute | solution.py:332
  71.9 30.6 %copy-start = (bf16[2,256,768]{2,1,0:T(8,128)(2,1)S(1)}, bf16[2,256,768]{2,1,0:T(8,128)(2,1)}, u32[]{:S(2)}) copy-start(bf16[2,256,768]{2,1,0:T(8,128)(2,1)} %get-tuple-element.39.mid01) | copy-start | bytes 2359300
  72.0 9.3 %collective-permute-start.18 = (bf16[4,32,768]{2,1,0:T(8,128)(2,1)S(1)}, bf16[4,32,768]{2,1,0:T(8,128)(2,1)S(1)}, u32[]{:S(2)}, u32[]{:S(2)}) collective-permute-start(bf16[4,32,768]{2,1,0:T(8,128)(2,1)S(1)} %get-tuple-element.66), channel_id=1, source_target_pairs={{0,1},{1,0},{2,3},{3,2},{4,5},{5,4},{6,7},{7,6},{8,9},{9,8},{10,11... | collective-permute-start | bytes 589832 | tf_op jit(solution)/shard_map/ppermute | solution.py:332
  72.0 9.6 %collective-permute-start.19 = (bf16[4,32,768]{2,1,0:T(8,128)(2,1)S(1)}, bf16[4,32,768]{2,1,0:T(8,128)(2,1)S(1)}, u32[]{:S(2)}, u32[]{:S(2)}) collective-permute-start(bf16[4,32,768]{2,1,0:T(8,128)(2,1)S(1)} %get-tuple-element.67), channel_id=1, source_target_pairs={{0,2},{1,3},{2,0},{3,1},{4,6},{5,7},{6,4},{7,5},{8,10},{9,11},{10,... | collective-permute-start | bytes 589832 | tf_op jit(solution)/shard_map/ppermute | solution.py:332
  78.8 7.2 %collective-permute-start.20 = (bf16[4,32,768]{2,1,0:T(8,128)(2,1)S(1)}, bf16[4,32,768]{2,1,0:T(8,128)(2,1)S(1)}, u32[]{:S(2)}, u32[]{:S(2)}) collective-permute-start(bf16[4,32,768]{2,1,0:T(8,128)(2,1)S(1)} %get-tuple-element.68), channel_id=1, source_target_pairs={{0,3},{1,2},{2,1},{3,0},{4,7},{5,6},{6,5},{7,4},{8,11},{9,10},{10,... | collective-permute-start | bytes 589832 | tf_op jit(solution)/shard_map/ppermute | solution.py:332
  79.6 8.0 %collective-permute-start.15 = (bf16[4,32,768]{2,1,0:T(8,128)(2,1)S(1)}, bf16[4,32,768]{2,1,0:T(8,128)(2,1)S(1)}, u32[]{:S(2)}, u32[]{:S(2)}) collective-permute-start(bf16[4,32,768]{2,1,0:T(8,128)(2,1)S(1)} %get-tuple-element.62), channel_id=1, source_target_pairs={{0,1},{1,0},{2,3},{3,2},{4,5},{5,4},{6,7},{7,6},{8,9},{9,8},{10,11... | collective-permute-start | bytes 589832 | tf_op jit(solution)/shard_map/ppermute | solution.py:332
  80.2 9.4 %collective-permute-start.16 = (bf16[4,32,768]{2,1,0:T(8,128)(2,1)S(1)}, bf16[4,32,768]{2,1,0:T(8,128)(2,1)S(1)}, u32[]{:S(2)}, u32[]{:S(2)}) collective-permute-start(bf16[4,32,768]{2,1,0:T(8,128)(2,1)S(1)} %get-tuple-element.63), channel_id=1, source_target_pairs={{0,2},{1,3},{2,0},{3,1},{4,6},{5,7},{6,4},{7,5},{8,10},{9,11},{10,... | collective-permute-start | bytes 589832 | tf_op jit(solution)/shard_map/ppermute | solution.py:332
  81.3 12.9 %collective-permute-start.17 = (bf16[4,32,768]{2,1,0:T(8,128)(2,1)S(1)}, bf16[4,32,768]{2,1,0:T(8,128)(2,1)S(1)}, u32[]{:S(2)}, u32[]{:S(2)}) collective-permute-start(bf16[4,32,768]{2,1,0:T(8,128)(2,1)S(1)} %get-tuple-element.64), channel_id=1, source_target_pairs={{0,3},{1,2},{2,1},{3,0},{4,7},{5,6},{6,5},{7,4},{8,11},{9,10},{10,... | collective-permute-start | bytes 589832 | tf_op jit(solution)/shard_map/ppermute | solution.py:332
  86.1 15.2 %collective-permute-start.21 = (bf16[4,32,768]{2,1,0:T(8,128)(2,1)S(1)}, bf16[4,32,768]{2,1,0:T(8,128)(2,1)S(1)}, u32[]{:S(2)}, u32[]{:S(2)}) collective-permute-start(bf16[4,32,768]{2,1,0:T(8,128)(2,1)S(1)} %get-tuple-element.70), channel_id=1, source_target_pairs={{0,8},{1,9},{2,10},{3,11},{4,12},{5,13},{6,14},{7,15},{8,0},{9,1},... | collective-permute-start | bytes 589832 | tf_op jit(solution)/shard_map/ppermute | solution.py:332
  86.4 14.8 %collective-permute-start.22 = (bf16[4,32,768]{2,1,0:T(8,128)(2,1)S(1)}, bf16[4,32,768]{2,1,0:T(8,128)(2,1)S(1)}, u32[]{:S(2)}, u32[]{:S(2)}) collective-permute-start(bf16[4,32,768]{2,1,0:T(8,128)(2,1)S(1)} %get-tuple-element.71), channel_id=1, source_target_pairs={{0,12},{1,13},{2,14},{3,15},{4,8},{5,9},{6,10},{7,11},{8,4},{9,5},... | collective-permute-start | bytes 589832 | tf_op jit(solution)/shard_map/ppermute | solution.py:332
  87.6 14.9 %collective-permute-start.23 = (bf16[4,32,768]{2,1,0:T(8,128)(2,1)S(1)}, bf16[4,32,768]{2,1,0:T(8,128)(2,1)S(1)}, u32[]{:S(2)}, u32[]{:S(2)}) collective-permute-start(bf16[4,32,768]{2,1,0:T(8,128)(2,1)S(1)} %get-tuple-element.72), channel_id=1, source_target_pairs={{0,4},{1,5},{2,6},{3,7},{4,0},{5,1},{6,2},{7,3},{8,12},{9,13},{10,... | collective-permute-start | bytes 589832 | tf_op jit(solution)/shard_map/ppermute | solution.py:332

commit v3 on v1

v3 whole, which is shorter than its diff:
```python
import functools

import jax
import jax.numpy as jnp
from jax import lax
from jax.experimental import pallas as pl
from jax.experimental.pallas import tpu as pltpu
from jax.sharding import PartitionSpec as P

HEADS = 12
HEAD_DIM = 64
LANES = 128
TILE = 16
HALF = TILE // 2
GROUP = 256
LAG = 1
BF16 = jnp.bfloat16
F32 = jnp.float32
VMEM = pl.BlockSpec(memory_space=pltpu.VMEM)
SMEM = pl.BlockSpec(memory_space=pltpu.SMEM)
HBM = pl.BlockSpec(memory_space=pltpu.HBM)

OUTER = (0, 8, 12, 4)
INNER = (0, 1, 2, 3)


def normalize(floats):
    average = jnp.mean(floats, axis=-1, keepdims=True)
    centred = floats - average
    spread = jnp.mean(centred * centred, axis=-1, keepdims=True)
    return (centred * lax.rsqrt(spread + 1e-06)).astype(BF16)


def project(flat_rows, matrix):
    return jnp.dot(flat_rows, matrix, preferred_element_type=F32)


def plain_attend(projected, score_form, mix_form):
    leading = projected.shape[:-1]
    split = projected.reshape(leading + (3, HEADS, HEAD_DIM))
    queries = split[..., 0, :, :]
    key_part = split[..., 1, :, :]
    values = split[..., 2, :, :]
    scores = jnp.einsum(
        score_form, queries, key_part, preferred_element_type=F32
    ) * HEAD_DIM ** (-0.5)
    weights = jax.nn.softmax(scores, axis=-1).astype(BF16)
    mixed = jnp.einsum(mix_form, weights, values, preferred_element_type=F32)
    return mixed.reshape(leading + (HEADS * HEAD_DIM,)).astype(BF16)


def attend_time(received):
    frame_total, single, item_count, columns = received.shape
    sequences = received.reshape(frame_total, item_count, columns)
    result = plain_attend(sequences, "qbhd,kbhd->bhqk", "bhqk,kbhd->qbhd")
    return result.reshape(frame_total, single, item_count, HEADS * HEAD_DIM)


def plain_shards(frames_in, qkv_spatial, out_spatial, qkv_temporal, out_temporal):
    frame_count, patch_count, features = frames_in.shape
    wide_count = lax.axis_size("wide")
    per_group = patch_count // wide_count
    first = normalize(frames_in.astype(F32))
    proj_one = project(first.reshape(-1, features), qkv_spatial).astype(BF16)
    proj_one = proj_one.reshape(frame_count, patch_count, 3 * features)
    spatial = plain_attend(proj_one, "bqhd,bkhd->bhqk", "bhqk,bkhd->bqhd")
    update = project(spatial.reshape(-1, features), out_spatial).reshape(
        frame_count, patch_count, features
    )
    middle = (frames_in.astype(F32) + update).astype(BF16)
    second = normalize(middle.astype(F32))
    grouped = second.reshape(frame_count, wide_count, per_group, features)
    received = lax.all_to_all(grouped, "wide", split_axis=1, concat_axis=0, tiled=True)
    frame_total, single, item_count, columns = received.shape
    local_proj = project(received.reshape(-1, columns), qkv_temporal).astype(BF16)
    local_proj = local_proj.reshape(frame_total, single, item_count, 3 * columns)
    temporal = attend_time(local_proj)
    returned = lax.all_to_all(temporal, "wide", split_axis=0, concat_axis=1, tiled=True)
    change = project(returned.reshape(-1, features), out_temporal).reshape(
        frame_count, patch_count, features
    )
    return (middle.astype(F32) + change).astype(BF16)


def project_rows(a, wqkv, qkv, places, j):
    d = a.shape[1]
    for start in range(j * d, (j + 1) * d, GROUP):
        cols = slice(start, start + GROUP)
        part = jnp.dot(a[...], wqkv[:, cols], preferred_element_type=F32).astype(BF16)
        part = part * BF16(HEAD_DIM**-0.5) if j == 0 else part
        size = a.shape[0] // len(places)
        for n, place in enumerate(places):
            qkv[place : place + size, cols] = part[n * size : (n + 1) * size]


def attend(qkv, mixed, blocks, bias=None):
    d = mixed.shape[1]
    units = [(r, c, half) for r in blocks for c in range(0, d, LANES) for half in range(2)]
    size = blocks[0].stop - blocks[0].start
    low = lax.broadcasted_iota(jnp.int32, (size, LANES), 1) < HEAD_DIM
    begun, sums = {}, {}

    def begin(n):
        r, c, half = units[n]
        q = qkv[r, c : c + LANES]
        one = jnp.where(low if half == 0 else ~low, q, jnp.zeros_like(q))
        scores = lax.dot_general(
            one,
            qkv[r, d + c : d + c + LANES],
            (((1,), (1,)), ((), ())),
            preferred_element_type=F32,
        )
        if bias is not None:
            scores = scores + bias[...]
        begun[n] = scores, jnp.max(scores, axis=-1, keepdims=True)

    def end(n):
        r, c, half = units[n]
        scores, top = begun.pop(n)
        weights = jnp.exp(scores - top).astype(BF16)
        v = qkv[r, 2 * d + c : 2 * d + c + LANES]
        values = jnp.where(low if half == 0 else ~low, v, jnp.ones_like(v))
        sums[half] = jnp.dot(weights, values, preferred_element_type=F32)
        if half == 1:
            total = pltpu.roll(jnp.where(low, sums[1], sums[0]), HEAD_DIM, 1)
            mixed[r, c : c + LANES] = (jnp.where(low, sums[0], sums[1]) / total).astype(BF16)

    for n in range(len(units) + LAG):
        if n < len(units):
            begin(n)
        if n >= LAG:
            end(n - LAG)


def spatial_kernel(outer_first, begin, fetch, me, x_in, wqkv_in, wo_in, middle, *refs):
    frames, patches, d = middle.shape
    outs, (a, qkv, mixed, second, *held) = refs[:4], refs[4:]
    number = me[0]
    if fetch:
        x, wqkv, wo, sems = held
        pairs = [(x_in.at[pl.ds(begin, frames)], x)]
        pairs += [(wqkv_in.at[:, pl.ds(j * d, d)], wqkv.at[:, pl.ds(j * d, d)]) for j in range(3)]
        pairs += [(wo_in, wo)]
        copies = [pltpu.make_async_copy(*pair, sems.at[n]) for n, pair in enumerate(pairs)]
        for copy in copies:
            copy.start()
        copies[0].wait()
    else:
        x, wqkv, wo = x_in.at[pl.ds(begin, frames)], wqkv_in, wo_in
    for f in range(frames):
        a[f * patches : (f + 1) * patches, :] = normalize(x[f].astype(F32))
    for j in range(3):
        if fetch:
            copies[1 + j].wait()
        project_rows(a, wqkv, qkv, (0,), j)
    if fetch:
        copies[4].wait()
    attend(qkv, mixed, [slice(f * patches, (f + 1) * patches) for f in range(frames)])
    for f in range(frames):
        r = slice(f * patches, (f + 1) * patches)
        update = jnp.dot(mixed[r, :], wo[...], preferred_element_type=F32)
        mid = (x[f].astype(F32) + update).astype(BF16)
        middle[f] = mid
        second[...] = normalize(mid.astype(F32))
        for p in range(4):
            for i in range(4):
                owner = number ^ (OUTER[p] ^ INNER[i])
                rows = second[pl.ds(pl.multiple_of(owner * TILE, TILE), TILE), :]
                if outer_first:
                    outs[p][f, i] = rows
                else:
                    outs[i][f, p] = rows


def spatial(me, x, begin, frames, wqkv, wo, outer_first, fetch):
    _, patches, d = x.shape
    rows = frames * patches
    block = jax.ShapeDtypeStruct((frames, 4, TILE, d), BF16)
    held = [
        pltpu.VMEM((frames, patches, d), BF16),
        pltpu.VMEM(wqkv.shape, BF16),
        pltpu.VMEM(wo.shape, BF16),
        pltpu.SemaphoreType.DMA((5,)),
    ]
    return pl.pallas_call(
        functools.partial(spatial_kernel, outer_first, begin, fetch),
        in_specs=[SMEM] + [HBM if fetch else VMEM] * 3,
        out_specs=[VMEM] * 5,
        out_shape=[jax.ShapeDtypeStruct((frames, patches, d), BF16)] + [block] * 4,
        scratch_shapes=[
            pltpu.VMEM((rows, d), BF16),
            pltpu.VMEM((rows, 3 * d), BF16),
            pltpu.VMEM((rows, d), BF16),
            pltpu.VMEM((patches, d), BF16),
        ]
        + (held if fetch else []),
        compiler_params=pltpu.CompilerParams(vmem_limit_bytes=(52 if fetch else 24) << 20),
        cost_estimate=pl.CostEstimate(
            flops=8 * rows * d * d + 16 * rows * patches * d,
            bytes_accessed=8 * d * d,
            transcendentals=rows * patches * HEADS,
        ),
        name="spatial_outer" if outer_first else "spatial_inner",
    )(me, x, wqkv, wo)


def regroup_kernel(*refs):
    ins, outs = refs[:4], refs[4:]
    for b in range(4):
        for a in range(4):
            if len(ins[0].shape) == 4:
                outs[b][a] = ins[a][:, b]
            else:
                outs[b][a] = ins[a][b]


def regroup(pieces):
    shape = pieces[0].shape
    shape = (4, shape[0]) + shape[2:] if len(shape) == 4 else shape
    return pl.pallas_call(
        regroup_kernel,
        in_specs=[VMEM] * 4,
        out_specs=[VMEM] * 4,
        out_shape=[jax.ShapeDtypeStruct(shape, BF16)] * 4,
        compiler_params=pltpu.CompilerParams(vmem_limit_bytes=4 << 20),
        cost_estimate=pl.CostEstimate(flops=0, bytes_accessed=1 << 20, transcendentals=0),
        name="regroup",
    )(*pieces)


def chosen(rows, columns, source):
    r = lax.broadcasted_iota(jnp.int32, (rows, columns), 0)
    c = lax.broadcasted_iota(jnp.int32, (rows, columns), 1)
    return (c == source(r)).astype(F32).astype(BF16)


def gather(parts, tile, scratch, positions, length, a):
    count = positions.stop - positions.start
    pick = chosen(
        count * TILE, TILE * TILE, lambda r: (r % TILE) * TILE + positions.start + r // TILE
    )
    for block in range(2):
        for n in range(TILE):
            p, i, f = 2 * block + n // 8, n // 2 % 4, n % 2
            scratch[n * TILE : (n + 1) * TILE, :] = tile(parts, p, i, f)
        taken = jnp.dot(pick, scratch[...], preferred_element_type=F32).astype(BF16)
        for q in range(count):
            start = q * length + block * TILE
            a[start : start + TILE, :] = taken[q * TILE : (q + 1) * TILE]


def project_kernel(*refs):
    parts, wqkv, qkv, scratch, a = refs[:4], *refs[4:]
    gather(parts, lambda z, p, i, f: z[i][p, f], scratch, slice(0, TILE), 2 * TILE, a)
    for j in range(3):
        project_rows(a, wqkv, qkv, (0,), j)


def project_early(parts, wqkv):
    d = wqkv.shape[0]
    rows = TILE * 2 * TILE
    return pl.pallas_call(
        project_kernel,
        in_specs=[VMEM] * 5,
        out_specs=VMEM,
        out_shape=jax.ShapeDtypeStruct((rows, 3 * d), BF16),
        scratch_shapes=[pltpu.VMEM((TILE * TILE, d), BF16), pltpu.VMEM((rows, d), BF16)],
        compiler_params=pltpu.CompilerParams(vmem_limit_bytes=24 << 20),
        cost_estimate=pl.CostEstimate(
            flops=6 * rows * d * d, bytes_accessed=6 * d * d, transcendentals=0
        ),
        name="project_early",
    )(*parts, wqkv)


def temporal_kernel(half, outer_first, early, *refs):
    parts, wqkv, wo, outs = refs[:4], refs[4], refs[5], refs[6:10]
    scratch, a, qkv, mixed, change, bias = refs[10:]
    length = 2 * TILE
    run = 4 * length
    row, column = (lax.broadcasted_iota(jnp.int32, bias.shape, axis) for axis in range(2))
    other = ((row ^ column) & (run - length)) != 0
    bias[...] = jnp.where(other, -jnp.inf, 0.0)
    gather(
        parts,
        lambda y, p, i, f: y[p][i, f],
        scratch,
        slice(half * HALF, (half + 1) * HALF),
        length,
        a,
    )
    groups = range(HALF // 4)
    for g in groups:
        first = (half * HALF + 4 * g) * length
        qkv[2 * g * run : (2 * g + 1) * run, :] = early[first : first + run, :]
    for j in range(3):
        project_rows(a, wqkv, qkv, [(2 * g + 1) * run for g in groups], j)
    attend(qkv, mixed, [slice(2 * g * run, 2 * (g + 1) * run) for g in groups], bias)
    change[...] = jnp.dot(mixed[...], wo[...], preferred_element_type=F32).astype(BF16)
    back = chosen(HALF * TILE, HALF * TILE, lambda r: (r % HALF) * TILE + r // HALF)
    for chunk in range(2):
        for block in range(2):
            starts = [
                (q // 4 * 2 + chunk) * run + q % 4 * length + block * TILE for q in range(HALF)
            ]
            rows = jnp.concatenate([change[start : start + TILE, :] for start in starts], axis=0)
            rows = jnp.dot(back, rows, preferred_element_type=F32).astype(BF16)
            for n in range(8):
                p, i = 2 * block + n // 4, n % 4
                tile = rows[n * TILE : (n + 1) * TILE]
                at = slice(chunk * TILE, (chunk + 1) * TILE)
                if outer_first:
                    outs[p][i, at] = tile
                else:
                    outs[i][p, at] = tile


def temporal(half, early, parts, wqkv, wo, outer_first):
    d = wo.shape[0]
    rows = HALF * 2 * TILE
    block = jax.ShapeDtypeStruct((4, 2 * TILE, d), BF16)
    return pl.pallas_call(
        functools.partial(temporal_kernel, half, outer_first),
        in_specs=[VMEM] * 7,
        out_specs=[VMEM] * 4,
        out_shape=[block] * 4,
        scratch_shapes=[
            pltpu.VMEM((TILE * TILE, d), BF16),
            pltpu.VMEM((rows, d), BF16),
            pltpu.VMEM((2 * rows, 3 * d), BF16),
            pltpu.VMEM((2 * rows, d), BF16),
            pltpu.VMEM((2 * rows, d), BF16),
            pltpu.VMEM((16 * TILE, 16 * TILE), F32),
        ],
        compiler_params=pltpu.CompilerParams(vmem_limit_bytes=24 << 20),
        cost_estimate=pl.CostEstimate(
            flops=10 * rows * d * d + 32 * rows * GROUP * d,
            bytes_accessed=8 * d * d,
            transcendentals=2 * rows * GROUP * HEADS,
        ),
        name="temporal",
    )(early, *parts, wqkv, wo)


def last_kernel(me, mid01, mid23, *refs):
    early, late, out = refs[:4], refs[4:8], refs[8]
    number = me[0]
    f = pl.program_id(0)

    def add(mid, frame, at):
        for p in range(4):
            for i in range(4):
                owner = number ^ (OUTER[p] ^ INNER[i])
                rows = pl.ds(pl.multiple_of(owner * TILE, TILE), TILE)
                change = jnp.concatenate(
                    [
                        early[i][p].astype(F32)[at * HALF : (at + 1) * HALF],
                        late[p][i].astype(F32)[at * HALF : (at + 1) * HALF],
                    ],
                    axis=0,
                )
                out[0, rows, :] = (mid[frame, rows, :].astype(F32) + change).astype(BF16)

    for at in range(4):
        pl.when(f == at)(functools.partial(add, mid01 if at < 2 else mid23, at % 2, at))


def last(me, mid01, mid23, early, late):
    _, patches, d = mid01.shape
    return pl.pallas_call(
        last_kernel,
        grid=(4,),
        in_specs=[SMEM] + [VMEM] * 10,
        out_specs=pl.BlockSpec((1, patches, d), lambda f: (f, 0, 0)),
        out_shape=jax.ShapeDtypeStruct((4, patches, d), BF16),
        compiler_params=pltpu.CompilerParams(vmem_limit_bytes=16 << 20),
        cost_estimate=pl.CostEstimate(
            flops=patches * d * 4, bytes_accessed=patches * d * 8, transcendentals=0
        ),
        name="last",
    )(me, mid01, mid23, *early, *late)


def exchange(pieces, masks):
    size = lax.axis_size("wide")
    return [pieces[0]] + [
        lax.ppermute(piece, "wide", [(w, w ^ mask) for w in range(size)])
        for piece, mask in zip(pieces[1:], masks[1:])
    ]


def shards(frames_in, qkv_spatial, out_spatial, qkv_temporal, out_temporal):
    me = lax.axis_index("wide").astype(jnp.int32).reshape(1)
    mid01, *pieces = spatial(me, frames_in, 0, 2, qkv_spatial, out_spatial, True, True)
    z_parts = exchange(regroup(exchange(pieces, OUTER)), INNER)
    mid23, *pieces = spatial(me, frames_in, 2, 2, qkv_spatial, out_spatial, False, False)
    y_parts = exchange(regroup(exchange(pieces, INNER)), OUTER)
    projected = project_early(z_parts, qkv_temporal)
    pieces = temporal(0, projected, y_parts, qkv_temporal, out_temporal, True)
    early = exchange(regroup(exchange(pieces, OUTER)), INNER)
    pieces = temporal(1, projected, y_parts, qkv_temporal, out_temporal, False)
    late = exchange(regroup(exchange(pieces, INNER)), OUTER)
    return last(me, mid01, mid23, early, late)


def solution(mesh):
    wide = mesh.shape["wide"]

    def whole(frames_in, *weights):
        local = frames_in.shape[0] // (wide * mesh.shape["groups"])
        fits = wide == 16 and local == 4 and frames_in.shape[1] == wide * TILE
        return jax.shard_map(
            shards if fits else plain_shards,
            mesh=mesh,
            in_specs=(P(("groups", "wide"), None, None), P(), P(), P(), P()),
            out_specs=P(("groups", "wide"), None, None),
            check_vma=False,
        )(frames_in, *weights)

    return whole
```

time: 121 us -> 101 us (0.83)
  local copies, waits for them, and re-layouts: 15 us -> 0.02 us
  Pallas kernels: 38.8 us -> 29 us
  waiting for transfers between devices: 36.3 us -> 45.3 us
  starting transfers between devices: 29.8 us -> 26.2 us
    unnamed x56 -> x10, local copies, waits for them, and re-layouts: 13.4 us -> 0.02 us
    ppermute x24, waiting for transfers between devices: 36.3 us -> 45.3 us  [exchange(): lax.ppermute(piece, 'wide', [(w, w ^ mask) for w in range(size)])]
    pallas_call x4, Pallas kernels: 8.52 us -> 0.21 us  [regroup(): pl.pallas_call(regroup_kernel, in_specs=[VMEM] * 4, out_specs=[VMEM] * 4,...]
    pallas_call x2 -> x3, Pallas kernels: 11.7 us -> 15.8 us  [the longest x2 13.4 us: spatial(): pl.pallas_call(functools.partial(spatial_kernel, outer_first, begin, fetc...]
    pallas_call x2, Pallas kernels: 14.9 us -> 11.2 us  [temporal(): pl.pallas_call(functools.partial(temporal_kernel, half, outer_first), in_...]
    ppermute x24, starting transfers between devices: 29.8 us -> 26.2 us  [exchange(): lax.ppermute(piece, 'wide', [(w, w ^ mask) for w in range(size)])]
    pallas_call x1, Pallas kernels: 3.66 us -> 1.82 us  [last(): pl.pallas_call(last_kernel, grid=(4,), in_specs=[SMEM] + [VMEM] * 10, out...]
    slice x1 -> x0, local copies, waits for them, and re-layouts: 1.57 us -> none  [shards(): mid23, *pieces = spatial(me, frames_in[2:], qkv_spatial, out_spatial, False)]
  transfers between devices with their start and end apart: 24 -> 24, of which waited for: 12 -> 14; matrix products, arithmetic and copies ran while one was open for 0% -> 0% of each run, Pallas kernels for 19% -> 14%
where the time goes in v3:
time: 101 us
  waiting for transfers between devices  45.3 us (45%)
  Pallas kernels  29 us (29%)
  starting transfers between devices  26.2 us (26%)
    ppermute x24, waiting for transfers between devices, exchange(): lax.ppermute(piece, 'wide', [(w, w ^ mask) for w in range(size)])  45.3 us
    ppermute x24, starting transfers between devices, exchange(): lax.ppermute(piece, 'wide', [(w, w ^ mask) for w in range(size)])  26.2 us
    pallas_call x2, Pallas kernels, spatial(): pl.pallas_call(functools.partial(spatial_kernel, outer_first, begin, fetc...  13.4 us
    pallas_call x2, Pallas kernels, temporal(): pl.pallas_call(functools.partial(temporal_kernel, half, outer_first), in_...  11.2 us
    pallas_call x1, Pallas kernels, project_early(): pl.pallas_call(project_kernel, in_specs=[VMEM] * 5, out_specs=VMEM, out_s...  2.46 us
  transfers between devices with their start and end apart: 24, of which 14 were waited for; matrix products, arithmetic and copies ran while one was open for 0% of the time, Pallas kernels for 14%

profile of v3, /device:TPU:0, one launch (start us, length us, event | category | flops | bytes accessed | tf_op | source)
XLA Modules:
  0.0 100.7 jit_solution(17155797197719593850)
XLA Ops:
  0.0 8.0 %spatial_outer.1 = (bf16[2,256,768]{2,1,0:T(8,128)(2,1)S(1)}, bf16[2,4,16,768]{3,2,1,0:T(8,128)(2,1)S(1)}, bf16[2,4,16,768]{3,2,1,0:T(8,128)(2,1)S(1)}, bf16[2,4...) custom-call(s32[1]{0:T(128)} %bitcast.me, bf16[4,256,768]{2,1,0:T(8,128)(2,1)} %x_in.3, bf16[768,2304]{1,0:T(8,128)(2,1)} %wqkv_in.3, ...), custom_call_target="tpu_custom_call" | custom-call | flops 4026531840 | bytes 4718592 | tf_op jit(solution)/shard_map/spatial_outer/pallas_call | solution.py:185
  8.0 4.1 %collective-permute-start = (bf16[2,4,16,768]{3,2,1,0:T(8,128)(2,1)S(1)}, bf16[2,4,16,768]{3,2,1,0:T(8,128)(2,1)S(1)}, u32[]{:S(2)}, u32[]{:S(2)}) collective-permute-start(bf16[2,4,16,768]{3,2,1,0:T(8,128)(2,1)S(1)} %get-tuple-element.42), channel_id=1, source_target_pairs={{0,8},{1,9},{2,10},{3,11},{4,12},{5,13},{6,14},{7,15},{8,0},{9,1},... | collective-permute-start | bytes 589832 | tf_op jit(solution)/shard_map/ppermute | solution.py:387
  12.1 1.3 %collective-permute-start.1 = (bf16[2,4,16,768]{3,2,1,0:T(8,128)(2,1)S(1)}, bf16[2,4,16,768]{3,2,1,0:T(8,128)(2,1)S(1)}, u32[]{:S(2)}, u32[]{:S(2)}) collective-permute-start(bf16[2,4,16,768]{3,2,1,0:T(8,128)(2,1)S(1)} %get-tuple-element.43), channel_id=1, source_target_pairs={{0,12},{1,13},{2,14},{3,15},{4,8},{5,9},{6,10},{7,11},{8,4},{9,5},... | collective-permute-start | bytes 589832 | tf_op jit(solution)/shard_map/ppermute | solution.py:387
  13.7 5.4 %spatial_inner.1 = (bf16[2,256,768]{2,1,0:T(8,128)(2,1)S(1)}, bf16[2,4,16,768]{3,2,1,0:T(8,128)(2,1)S(1)}, bf16[2,4,16,768]{3,2,1,0:T(8,128)(2,1)S(1)}, bf16[2,4...) custom-call(s32[1]{0:T(128)} %bitcast.me, bf16[4,256,768]{2,1,0:T(8,128)(2,1)S(1)} %copy-done.2, ...), custom_call_target="tpu_custom_call" | custom-call | flops 4026531840 | bytes 4718592 | tf_op jit(solution)/shard_map/spatial_inner/pallas_call | solution.py:185
  19.2 1.6 %collective-permute-start.7 = (bf16[2,4,16,768]{3,2,1,0:T(8,128)(2,1)S(1)}, bf16[2,4,16,768]{3,2,1,0:T(8,128)(2,1)S(1)}, u32[]{:S(2)}, u32[]{:S(2)}) collective-permute-start(bf16[2,4,16,768]{3,2,1,0:T(8,128)(2,1)S(1)} %get-tuple-element.51), channel_id=1, source_target_pairs={{0,2},{1,3},{2,0},{3,1},{4,6},{5,7},{6,4},{7,5},{8,10},{9,11},{10,... | collective-permute-start | bytes 589832 | tf_op jit(solution)/shard_map/ppermute | solution.py:387
  20.8 5.5 %collective-permute-done.refs_1_ = bf16[2,4,16,768]{3,2,1,0:T(8,128)(2,1)S(1)} collective-permute-done((bf16[2,4,16,768]{3,2,1,0:T(8,128)(2,1)S(1)}, bf16[2,4,16,768]{3,2,1,0:T(8,128)(2,1)S(1)}, u32[]{:S(2)}, u32[]{:S(2)}) %collective-permute-start) | collective-permute-done | bytes 196640 | tf_op jit(solution)/shard_map/ppermute | solution.py:387
  26.3 0.5 collective-permute-done.2.refs_3_
  26.8 1.5 %collective-permute-start.3 = (bf16[4,2,16,768]{3,2,1,0:T(8,128)(2,1)S(1)}, bf16[4,2,16,768]{3,2,1,0:T(8,128)(2,1)S(1)}, u32[]{:S(2)}, u32[]{:S(2)}) collective-permute-start(bf16[4,2,16,768]{3,2,1,0:T(8,128)(2,1)S(1)} %get-tuple-element.46), channel_id=1, source_target_pairs={{0,1},{1,0},{2,3},{3,2},{4,5},{5,4},{6,7},{7,6},{8,9},{9,8},{10,11... | collective-permute-start | bytes 589832 | tf_op jit(solution)/shard_map/ppermute | solution.py:387
  28.6 1.3 %collective-permute-start.5 = (bf16[4,2,16,768]{3,2,1,0:T(8,128)(2,1)S(1)}, bf16[4,2,16,768]{3,2,1,0:T(8,128)(2,1)S(1)}, u32[]{:S(2)}, u32[]{:S(2)}) collective-permute-start(bf16[4,2,16,768]{3,2,1,0:T(8,128)(2,1)S(1)} %get-tuple-element.48), channel_id=1, source_target_pairs={{0,3},{1,2},{2,1},{3,0},{4,7},{5,6},{6,5},{7,4},{8,11},{9,10},{10,... | collective-permute-start | bytes 589832 | tf_op jit(solution)/shard_map/ppermute | solution.py:387
  29.8 3.3 %collective-permute-done.8.refs_3_ = bf16[2,4,16,768]{3,2,1,0:T(8,128)(2,1)S(1)} collective-permute-done((bf16[2,4,16,768]{3,2,1,0:T(8,128)(2,1)S(1)}, bf16[2,4,16,768]{3,2,1,0:T(8,128)(2,1)S(1)}, u32[]{:S(2)}, u32[]{:S(2)}) %collective-permute-start.8) | collective-permute-done | bytes 196640 | tf_op jit(solution)/shard_map/ppermute | solution.py:387
  33.2 1.2 %collective-permute-start.9 = (bf16[4,2,16,768]{3,2,1,0:T(8,128)(2,1)S(1)}, bf16[4,2,16,768]{3,2,1,0:T(8,128)(2,1)S(1)}, u32[]{:S(2)}, u32[]{:S(2)}) collective-permute-start(bf16[4,2,16,768]{3,2,1,0:T(8,128)(2,1)S(1)} %get-tuple-element.54), channel_id=1, source_target_pairs={{0,8},{1,9},{2,10},{3,11},{4,12},{5,13},{6,14},{7,15},{8,0},{9,1},... | collective-permute-start | bytes 589832 | tf_op jit(solution)/shard_map/ppermute | solution.py:387
  34.4 1.9 %collective-permute-start.10 = (bf16[4,2,16,768]{3,2,1,0:T(8,128)(2,1)S(1)}, bf16[4,2,16,768]{3,2,1,0:T(8,128)(2,1)S(1)}, u32[]{:S(2)}, u32[]{:S(2)}) collective-permute-start(bf16[4,2,16,768]{3,2,1,0:T(8,128)(2,1)S(1)} %get-tuple-element.55), channel_id=1, source_target_pairs={{0,12},{1,13},{2,14},{3,15},{4,8},{5,9},{6,10},{7,11},{8,4},{9,5},... | collective-permute-start | bytes 589832 | tf_op jit(solution)/shard_map/ppermute | solution.py:387
  36.4 0.5 collective-permute-start.11
  36.9 1.2 %collective-permute-done.4.refs_2_ = bf16[4,2,16,768]{3,2,1,0:T(8,128)(2,1)S(1)} collective-permute-done((bf16[4,2,16,768]{3,2,1,0:T(8,128)(2,1)S(1)}, bf16[4,2,16,768]{3,2,1,0:T(8,128)(2,1)S(1)}, u32[]{:S(2)}, u32[]{:S(2)}) %collective-permute-start.4) | collective-permute-done | bytes 196640 | tf_op jit(solution)/shard_map/ppermute | solution.py:387
  38.0 3.5 %collective-permute-done.5.refs_3_ = bf16[4,2,16,768]{3,2,1,0:T(8,128)(2,1)S(1)} collective-permute-done((bf16[4,2,16,768]{3,2,1,0:T(8,128)(2,1)S(1)}, bf16[4,2,16,768]{3,2,1,0:T(8,128)(2,1)S(1)}, u32[]{:S(2)}, u32[]{:S(2)}) %collective-permute-start.5) | collective-permute-done | bytes 196640 | tf_op jit(solution)/shard_map/ppermute | solution.py:387
  41.6 2.5 %project_early.1.early = bf16[512,2304]{1,0:T(8,128)(2,1)S(1)} custom-call(bf16[4,2,16,768]{3,2,1,0:T(8,128)(2,1)S(1)} %get-tuple-element.45.refs_0_, bf16[4,2,16,768]{3,2,1,0:T(8,128)(2,1)S(1)} %collective-permute-done.3.refs_1_, bf16[4,2,16,768]{3,2,1,0:T(8,128)(2,1)S(1)} %collective-permute-done.4.refs_2_, ...), custom_call_target="tpu_custom_call" | custom-call | flops 1811939328 | bytes 3538944 | tf_op jit(solution)/shard_map/project_early/pallas_call | solution.py:262
  44.0 6.0 %collective-permute-done.9.refs_1_ = bf16[4,2,16,768]{3,2,1,0:T(8,128)(2,1)S(1)} collective-permute-done((bf16[4,2,16,768]{3,2,1,0:T(8,128)(2,1)S(1)}, bf16[4,2,16,768]{3,2,1,0:T(8,128)(2,1)S(1)}, u32[]{:S(2)}, u32[]{:S(2)}) %collective-permute-start.9) | collective-permute-done | bytes 196640 | tf_op jit(solution)/shard_map/ppermute | solution.py:387
  50.1 1.3 %collective-permute-done.11.refs_3_ = bf16[4,2,16,768]{3,2,1,0:T(8,128)(2,1)S(1)} collective-permute-done((bf16[4,2,16,768]{3,2,1,0:T(8,128)(2,1)S(1)}, bf16[4,2,16,768]{3,2,1,0:T(8,128)(2,1)S(1)}, u32[]{:S(2)}, u32[]{:S(2)}) %collective-permute-start.11) | collective-permute-done | bytes 196640 | tf_op jit(solution)/shard_map/ppermute | solution.py:387
  51.3 5.6 %temporal.2 = (bf16[4,32,768]{2,1,0:T(8,128)(2,1)S(1)}, bf16[4,32,768]{2,1,0:T(8,128)(2,1)S(1)}, bf16[4,32,768]{2,1,0:T(8,128)(2,1)S(1)}, bf16[4,32,768]{2,1,0:T(8,128)(2,1)S(1)}) custom-call(bf16[512,2304]{1,0:T(8,128)(2,1)S(1)} %project_early.1.early, bf16[4,2,16,768]{3,2,1,0:T(8,128)(2,1)S(1)} %get-tuple-element.53.refs_0_, ...), custom_call_target="tpu_custom_call" | custom-call | flops 3120562176 | bytes 4718592 | tf_op jit(solution)/shard_map/temporal/pallas_call | solution.py:322
  56.9 3.9 %collective-permute-start.12 = (bf16[4,32,768]{2,1,0:T(8,128)(2,1)S(1)}, bf16[4,32,768]{2,1,0:T(8,128)(2,1)S(1)}, u32[]{:S(2)}, u32[]{:S(2)}) collective-permute-start(bf16[4,32,768]{2,1,0:T(8,128)(2,1)S(1)} %get-tuple-element.58), channel_id=1, source_target_pairs={{0,8},{1,9},{2,10},{3,11},{4,12},{5,13},{6,14},{7,15},{8,0},{9,1},... | collective-permute-start | bytes 589832 | tf_op jit(solution)/shard_map/ppermute | solution.py:387
  60.8 1.9 %collective-permute-start.13 = (bf16[4,32,768]{2,1,0:T(8,128)(2,1)S(1)}, bf16[4,32,768]{2,1,0:T(8,128)(2,1)S(1)}, u32[]{:S(2)}, u32[]{:S(2)}) collective-permute-start(bf16[4,32,768]{2,1,0:T(8,128)(2,1)S(1)} %get-tuple-element.59), channel_id=1, source_target_pairs={{0,12},{1,13},{2,14},{3,15},{4,8},{5,9},{6,10},{7,11},{8,4},{9,5},... | collective-permute-start | bytes 589832 | tf_op jit(solution)/shard_map/ppermute | solution.py:387
  62.7 5.6 %temporal.3 = (bf16[4,32,768]{2,1,0:T(8,128)(2,1)S(1)}, bf16[4,32,768]{2,1,0:T(8,128)(2,1)S(1)}, bf16[4,32,768]{2,1,0:T(8,128)(2,1)S(1)}, bf16[4,32,768]{2,1,0:T(8,128)(2,1)S(1)}) custom-call(bf16[512,2304]{1,0:T(8,128)(2,1)S(1)} %project_early.1.early, bf16[4,2,16,768]{3,2,1,0:T(8,128)(2,1)S(1)} %get-tuple-element.53.refs_0_, ...), custom_call_target="tpu_custom_call" | custom-call | flops 3120562176 | bytes 4718592 | tf_op jit(solution)/shard_map/temporal/pallas_call | solution.py:322
  68.7 6.3 %collective-permute-done.12.refs_1_ = bf16[4,32,768]{2,1,0:T(8,128)(2,1)S(1)} collective-permute-done((bf16[4,32,768]{2,1,0:T(8,128)(2,1)S(1)}, bf16[4,32,768]{2,1,0:T(8,128)(2,1)S(1)}, u32[]{:S(2)}, u32[]{:S(2)}) %collective-permute-start.12) | collective-permute-done | bytes 196640 | tf_op jit(solution)/shard_map/ppermute | solution.py:387
  75.8 0.6 collective-permute-start.15
  76.4 1.0 %collective-permute-start.16 = (bf16[4,32,768]{2,1,0:T(8,128)(2,1)S(1)}, bf16[4,32,768]{2,1,0:T(8,128)(2,1)S(1)}, u32[]{:S(2)}, u32[]{:S(2)}) collective-permute-start(bf16[4,32,768]{2,1,0:T(8,128)(2,1)S(1)} %get-tuple-element.63), channel_id=1, source_target_pairs={{0,2},{1,3},{2,0},{3,1},{4,6},{5,7},{6,4},{7,5},{8,10},{9,11},{10,... | collective-permute-start | bytes 589832 | tf_op jit(solution)/shard_map/ppermute | solution.py:387
  77.9 4.3 %collective-permute-done.20.refs_3_ = bf16[4,32,768]{2,1,0:T(8,128)(2,1)S(1)} collective-permute-done((bf16[4,32,768]{2,1,0:T(8,128)(2,1)S(1)}, bf16[4,32,768]{2,1,0:T(8,128)(2,1)S(1)}, u32[]{:S(2)}, u32[]{:S(2)}) %collective-permute-start.20) | collective-permute-done | bytes 196640 | tf_op jit(solution)/shard_map/ppermute | solution.py:387
  82.3 2.0 %collective-permute-start.22 = (bf16[4,32,768]{2,1,0:T(8,128)(2,1)S(1)}, bf16[4,32,768]{2,1,0:T(8,128)(2,1)S(1)}, u32[]{:S(2)}, u32[]{:S(2)}) collective-permute-start(bf16[4,32,768]{2,1,0:T(8,128)(2,1)S(1)} %get-tuple-element.71), channel_id=1, source_target_pairs={{0,12},{1,13},{2,14},{3,15},{4,8},{5,9},{6,10},{7,11},{8,4},{9,5},... | collective-permute-start | bytes 589832 | tf_op jit(solution)/shard_map/ppermute | solution.py:387
  84.3 1.5 %collective-permute-start.23 = (bf16[4,32,768]{2,1,0:T(8,128)(2,1)S(1)}, bf16[4,32,768]{2,1,0:T(8,128)(2,1)S(1)}, u32[]{:S(2)}, u32[]{:S(2)}) collective-permute-start(bf16[4,32,768]{2,1,0:T(8,128)(2,1)S(1)} %get-tuple-element.72), channel_id=1, source_target_pairs={{0,4},{1,5},{2,6},{3,7},{4,0},{5,1},{6,2},{7,3},{8,12},{9,13},{10,... | collective-permute-start | bytes 589832 | tf_op jit(solution)/shard_map/ppermute | solution.py:387
  85.9 4.5 %collective-permute-done.17.refs_3_ = bf16[4,32,768]{2,1,0:T(8,128)(2,1)S(1)} collective-permute-done((bf16[4,32,768]{2,1,0:T(8,128)(2,1)S(1)}, bf16[4,32,768]{2,1,0:T(8,128)(2,1)S(1)}, u32[]{:S(2)}, u32[]{:S(2)}) %collective-permute-start.17) | collective-permute-done | bytes 196640 | tf_op jit(solution)/shard_map/ppermute | solution.py:387
  90.4 7.2 %collective-permute-done.21.refs_5_ = bf16[4,32,768]{2,1,0:T(8,128)(2,1)S(1)} collective-permute-done((bf16[4,32,768]{2,1,0:T(8,128)(2,1)S(1)}, bf16[4,32,768]{2,1,0:T(8,128)(2,1)S(1)}, u32[]{:S(2)}, u32[]{:S(2)}) %collective-permute-start.21) | collective-permute-done | bytes 196640 | tf_op jit(solution)/shard_map/ppermute | solution.py:387
  97.6 1.2 %collective-permute-done.23.refs_7_ = bf16[4,32,768]{2,1,0:T(8,128)(2,1)S(1)} collective-permute-done((bf16[4,32,768]{2,1,0:T(8,128)(2,1)S(1)}, bf16[4,32,768]{2,1,0:T(8,128)(2,1)S(1)}, u32[]{:S(2)}, u32[]{:S(2)}) %collective-permute-start.23) | collective-permute-done | bytes 196640 | tf_op jit(solution)/shard_map/ppermute | solution.py:387
  98.9 1.8 %last.1 = bf16[4,256,768]{2,1,0:T(8,128)(2,1)} custom-call(s32[1]{0:T(128)} %bitcast.me, bf16[2,256,768]{2,1,0:T(8,128)(2,1)S(1)} %get-tuple-element.39.mid01, bf16[2,256,768]{2,1,0:T(8,128)(2,1)S(1)} %get-tuple-element.40.mid23, bf16[4,32,768]{2,1,0:T(8,128)(2,1)S(1)} %get-tuple-element.61.refs_0_, bf16[4,32,768]{2,1,0:T(8,128)(2,1)S(1)} %collective-permute-done.15.refs_1_, ...), custom_call_target="tpu_custom_call" | custom-call | flops 786432 | bytes 1572864 | tf_op jit(solution)/shard_map/last/pallas_call | solution.py:370
  (36 shorter events, 2.4 us)
Async XLA Ops:
  0.0 13.7 %copy-start = (bf16[768,2304]{1,0:T(8,128)(2,1)S(1)}, bf16[768,2304]{1,0:T(8,128)(2,1)}, u32[]{:S(2)}) copy-start(bf16[768,2304]{1,0:T(8,128)(2,1)} %wqkv_in.3) | copy-start | bytes 10616836
  0.0 13.7 %copy-start.2 = (bf16[4,256,768]{2,1,0:T(8,128)(2,1)S(1)}, bf16[4,256,768]{2,1,0:T(8,128)(2,1)}, u32[]{:S(2)}) copy-start(bf16[4,256,768]{2,1,0:T(8,128)(2,1)} %x_in.3) | copy-start | bytes 4718596
  0.0 13.7 %copy-start.3 = (bf16[768,768]{1,0:T(8,128)(2,1)S(1)}, bf16[768,768]{1,0:T(8,128)(2,1)}, u32[]{:S(2)}) copy-start(bf16[768,768]{1,0:T(8,128)(2,1)} %wo_in.3) | copy-start | bytes 3538948
  8.0 18.3 %collective-permute-start = (bf16[2,4,16,768]{3,2,1,0:T(8,128)(2,1)S(1)}, bf16[2,4,16,768]{3,2,1,0:T(8,128)(2,1)S(1)}, u32[]{:S(2)}, u32[]{:S(2)}) collective-permute-start(bf16[2,4,16,768]{3,2,1,0:T(8,128)(2,1)S(1)} %get-tuple-element.42), channel_id=1, source_target_pairs={{0,8},{1,9},{2,10},{3,11},{4,12},{5,13},{6,14},{7,15},{8,0},{9,1},... | collective-permute-start | bytes 589832 | tf_op jit(solution)/shard_map/ppermute | solution.py:387
  12.1 14.2 %collective-permute-start.1 = (bf16[2,4,16,768]{3,2,1,0:T(8,128)(2,1)S(1)}, bf16[2,4,16,768]{3,2,1,0:T(8,128)(2,1)S(1)}, u32[]{:S(2)}, u32[]{:S(2)}) collective-permute-start(bf16[2,4,16,768]{3,2,1,0:T(8,128)(2,1)S(1)} %get-tuple-element.43), channel_id=1, source_target_pairs={{0,12},{1,13},{2,14},{3,15},{4,8},{5,9},{6,10},{7,11},{8,4},{9,5},... | collective-permute-start | bytes 589832 | tf_op jit(solution)/shard_map/ppermute | solution.py:387
  13.4 13.4 %collective-permute-start.2 = (bf16[2,4,16,768]{3,2,1,0:T(8,128)(2,1)S(1)}, bf16[2,4,16,768]{3,2,1,0:T(8,128)(2,1)S(1)}, u32[]{:S(2)}, u32[]{:S(2)}) collective-permute-start(bf16[2,4,16,768]{3,2,1,0:T(8,128)(2,1)S(1)} %get-tuple-element.44), channel_id=1, source_target_pairs={{0,4},{1,5},{2,6},{3,7},{4,0},{5,1},{6,2},{7,3},{8,12},{9,13},{10,... | collective-permute-start | bytes 589832 | tf_op jit(solution)/shard_map/ppermute | solution.py:387
  13.7 27.9 %copy-start.1 = (bf16[768,2304]{1,0:T(8,128)(2,1)S(1)}, bf16[768,2304]{1,0:T(8,128)(2,1)}, u32[]{:S(2)}) copy-start(bf16[768,2304]{1,0:T(8,128)(2,1)} %refs_4_.5) | copy-start | bytes 10616836
  19.1 9.5 %collective-permute-start.6 = (bf16[2,4,16,768]{3,2,1,0:T(8,128)(2,1)S(1)}, bf16[2,4,16,768]{3,2,1,0:T(8,128)(2,1)S(1)}, u32[]{:S(2)}, u32[]{:S(2)}) collective-permute-start(bf16[2,4,16,768]{3,2,1,0:T(8,128)(2,1)S(1)} %get-tuple-element.50), channel_id=1, source_target_pairs={{0,1},{1,0},{2,3},{3,2},{4,5},{5,4},{6,7},{7,6},{8,9},{9,8},{10,11... | collective-permute-start | bytes 589832 | tf_op jit(solution)/shard_map/ppermute | solution.py:387
  19.2 10.7 %collective-permute-start.7 = (bf16[2,4,16,768]{3,2,1,0:T(8,128)(2,1)S(1)}, bf16[2,4,16,768]{3,2,1,0:T(8,128)(2,1)S(1)}, u32[]{:S(2)}, u32[]{:S(2)}) collective-permute-start(bf16[2,4,16,768]{3,2,1,0:T(8,128)(2,1)S(1)} %get-tuple-element.51), channel_id=1, source_target_pairs={{0,2},{1,3},{2,0},{3,1},{4,6},{5,7},{6,4},{7,5},{8,10},{9,11},{10,... | collective-permute-start | bytes 589832 | tf_op jit(solution)/shard_map/ppermute | solution.py:387
  26.3 6.9 %collective-permute-start.8 = (bf16[2,4,16,768]{3,2,1,0:T(8,128)(2,1)S(1)}, bf16[2,4,16,768]{3,2,1,0:T(8,128)(2,1)S(1)}, u32[]{:S(2)}, u32[]{:S(2)}) collective-permute-start(bf16[2,4,16,768]{3,2,1,0:T(8,128)(2,1)S(1)} %get-tuple-element.52), channel_id=1, source_target_pairs={{0,3},{1,2},{2,1},{3,0},{4,7},{5,6},{6,5},{7,4},{8,11},{9,10},{10,... | collective-permute-start | bytes 589832 | tf_op jit(solution)/shard_map/ppermute | solution.py:387
  26.8 9.5 %collective-permute-start.3 = (bf16[4,2,16,768]{3,2,1,0:T(8,128)(2,1)S(1)}, bf16[4,2,16,768]{3,2,1,0:T(8,128)(2,1)S(1)}, u32[]{:S(2)}, u32[]{:S(2)}) collective-permute-start(bf16[4,2,16,768]{3,2,1,0:T(8,128)(2,1)S(1)} %get-tuple-element.46), channel_id=1, source_target_pairs={{0,1},{1,0},{2,3},{3,2},{4,5},{5,4},{6,7},{7,6},{8,9},{9,8},{10,11... | collective-permute-start | bytes 589832 | tf_op jit(solution)/shard_map/ppermute | solution.py:387
  28.4 9.6 %collective-permute-start.4 = (bf16[4,2,16,768]{3,2,1,0:T(8,128)(2,1)S(1)}, bf16[4,2,16,768]{3,2,1,0:T(8,128)(2,1)S(1)}, u32[]{:S(2)}, u32[]{:S(2)}) collective-permute-start(bf16[4,2,16,768]{3,2,1,0:T(8,128)(2,1)S(1)} %get-tuple-element.47), channel_id=1, source_target_pairs={{0,2},{1,3},{2,0},{3,1},{4,6},{5,7},{6,4},{7,5},{8,10},{9,11},{10,... | collective-permute-start | bytes 589832 | tf_op jit(solution)/shard_map/ppermute | solution.py:387
  28.6 13.0 %collective-permute-start.5 = (bf16[4,2,16,768]{3,2,1,0:T(8,128)(2,1)S(1)}, bf16[4,2,16,768]{3,2,1,0:T(8,128)(2,1)S(1)}, u32[]{:S(2)}, u32[]{:S(2)}) collective-permute-start(bf16[4,2,16,768]{3,2,1,0:T(8,128)(2,1)S(1)} %get-tuple-element.48), channel_id=1, source_target_pairs={{0,3},{1,2},{2,1},{3,0},{4,7},{5,6},{6,5},{7,4},{8,11},{9,10},{10,... | collective-permute-start | bytes 589832 | tf_op jit(solution)/shard_map/ppermute | solution.py:387
  33.2 16.8 %collective-permute-start.9 = (bf16[4,2,16,768]{3,2,1,0:T(8,128)(2,1)S(1)}, bf16[4,2,16,768]{3,2,1,0:T(8,128)(2,1)S(1)}, u32[]{:S(2)}, u32[]{:S(2)}) collective-permute-start(bf16[4,2,16,768]{3,2,1,0:T(8,128)(2,1)S(1)} %get-tuple-element.54), channel_id=1, source_target_pairs={{0,8},{1,9},{2,10},{3,11},{4,12},{5,13},{6,14},{7,15},{8,0},{9,1},... | collective-permute-start | bytes 589832 | tf_op jit(solution)/shard_map/ppermute | solution.py:387
  34.4 15.6 %collective-permute-start.10 = (bf16[4,2,16,768]{3,2,1,0:T(8,128)(2,1)S(1)}, bf16[4,2,16,768]{3,2,1,0:T(8,128)(2,1)S(1)}, u32[]{:S(2)}, u32[]{:S(2)}) collective-permute-start(bf16[4,2,16,768]{3,2,1,0:T(8,128)(2,1)S(1)} %get-tuple-element.55), channel_id=1, source_target_pairs={{0,12},{1,13},{2,14},{3,15},{4,8},{5,9},{6,10},{7,11},{8,4},{9,5},... | collective-permute-start | bytes 589832 | tf_op jit(solution)/shard_map/ppermute | solution.py:387
  36.4 15.0 %collective-permute-start.11 = (bf16[4,2,16,768]{3,2,1,0:T(8,128)(2,1)S(1)}, bf16[4,2,16,768]{3,2,1,0:T(8,128)(2,1)S(1)}, u32[]{:S(2)}, u32[]{:S(2)}) collective-permute-start(bf16[4,2,16,768]{3,2,1,0:T(8,128)(2,1)S(1)} %get-tuple-element.56), channel_id=1, source_target_pairs={{0,4},{1,5},{2,6},{3,7},{4,0},{5,1},{6,2},{7,3},{8,12},{9,13},{10,... | collective-permute-start | bytes 589832 | tf_op jit(solution)/shard_map/ppermute | solution.py:387
  41.6 9.8 %copy-start.4 = (bf16[768,768]{1,0:T(8,128)(2,1)S(1)}, bf16[768,768]{1,0:T(8,128)(2,1)}, u32[]{:S(2)}) copy-start(bf16[768,768]{1,0:T(8,128)(2,1)} %refs_5_.3) | copy-start | bytes 3538948
  56.9 18.1 %collective-permute-start.12 = (bf16[4,32,768]{2,1,0:T(8,128)(2,1)S(1)}, bf16[4,32,768]{2,1,0:T(8,128)(2,1)S(1)}, u32[]{:S(2)}, u32[]{:S(2)}) collective-permute-start(bf16[4,32,768]{2,1,0:T(8,128)(2,1)S(1)} %get-tuple-element.58), channel_id=1, source_target_pairs={{0,8},{1,9},{2,10},{3,11},{4,12},{5,13},{6,14},{7,15},{8,0},{9,1},... | collective-permute-start | bytes 589832 | tf_op jit(solution)/shard_map/ppermute | solution.py:387
  60.8 14.6 %collective-permute-start.13 = (bf16[4,32,768]{2,1,0:T(8,128)(2,1)S(1)}, bf16[4,32,768]{2,1,0:T(8,128)(2,1)S(1)}, u32[]{:S(2)}, u32[]{:S(2)}) collective-permute-start(bf16[4,32,768]{2,1,0:T(8,128)(2,1)S(1)} %get-tuple-element.59), channel_id=1, source_target_pairs={{0,12},{1,13},{2,14},{3,15},{4,8},{5,9},{6,10},{7,11},{8,4},{9,5},... | collective-permute-start | bytes 589832 | tf_op jit(solution)/shard_map/ppermute | solution.py:387
  62.7 13.0 %collective-permute-start.14 = (bf16[4,32,768]{2,1,0:T(8,128)(2,1)S(1)}, bf16[4,32,768]{2,1,0:T(8,128)(2,1)S(1)}, u32[]{:S(2)}, u32[]{:S(2)}) collective-permute-start(bf16[4,32,768]{2,1,0:T(8,128)(2,1)S(1)} %get-tuple-element.60), channel_id=1, source_target_pairs={{0,4},{1,5},{2,6},{3,7},{4,0},{5,1},{6,2},{7,3},{8,12},{9,13},{10,... | collective-permute-start | bytes 589832 | tf_op jit(solution)/shard_map/ppermute | solution.py:387
  68.3 9.1 %collective-permute-start.18 = (bf16[4,32,768]{2,1,0:T(8,128)(2,1)S(1)}, bf16[4,32,768]{2,1,0:T(8,128)(2,1)S(1)}, u32[]{:S(2)}, u32[]{:S(2)}) collective-permute-start(bf16[4,32,768]{2,1,0:T(8,128)(2,1)S(1)} %get-tuple-element.66), channel_id=1, source_target_pairs={{0,1},{1,0},{2,3},{3,2},{4,5},{5,4},{6,7},{7,6},{8,9},{9,8},{10,11... | collective-permute-start | bytes 589832 | tf_op jit(solution)/shard_map/ppermute | solution.py:387
  68.4 9.4 %collective-permute-start.19 = (bf16[4,32,768]{2,1,0:T(8,128)(2,1)S(1)}, bf16[4,32,768]{2,1,0:T(8,128)(2,1)S(1)}, u32[]{:S(2)}, u32[]{:S(2)}) collective-permute-start(bf16[4,32,768]{2,1,0:T(8,128)(2,1)S(1)} %get-tuple-element.67), channel_id=1, source_target_pairs={{0,2},{1,3},{2,0},{3,1},{4,6},{5,7},{6,4},{7,5},{8,10},{9,11},{10,... | collective-permute-start | bytes 589832 | tf_op jit(solution)/shard_map/ppermute | solution.py:387
  75.0 7.2 %collective-permute-start.20 = (bf16[4,32,768]{2,1,0:T(8,128)(2,1)S(1)}, bf16[4,32,768]{2,1,0:T(8,128)(2,1)S(1)}, u32[]{:S(2)}, u32[]{:S(2)}) collective-permute-start(bf16[4,32,768]{2,1,0:T(8,128)(2,1)S(1)} %get-tuple-element.68), channel_id=1, source_target_pairs={{0,3},{1,2},{2,1},{3,0},{4,7},{5,6},{6,5},{7,4},{8,11},{9,10},{10,... | collective-permute-start | bytes 589832 | tf_op jit(solution)/shard_map/ppermute | solution.py:387
  75.8 8.5 %collective-permute-start.15 = (bf16[4,32,768]{2,1,0:T(8,128)(2,1)S(1)}, bf16[4,32,768]{2,1,0:T(8,128)(2,1)S(1)}, u32[]{:S(2)}, u32[]{:S(2)}) collective-permute-start(bf16[4,32,768]{2,1,0:T(8,128)(2,1)S(1)} %get-tuple-element.62), channel_id=1, source_target_pairs={{0,1},{1,0},{2,3},{3,2},{4,5},{5,4},{6,7},{7,6},{8,9},{9,8},{10,11... | collective-permute-start | bytes 589832 | tf_op jit(solution)/shard_map/ppermute | solution.py:387
  76.4 9.5 %collective-permute-start.16 = (bf16[4,32,768]{2,1,0:T(8,128)(2,1)S(1)}, bf16[4,32,768]{2,1,0:T(8,128)(2,1)S(1)}, u32[]{:S(2)}, u32[]{:S(2)}) collective-permute-start(bf16[4,32,768]{2,1,0:T(8,128)(2,1)S(1)} %get-tuple-element.63), channel_id=1, source_target_pairs={{0,2},{1,3},{2,0},{3,1},{4,6},{5,7},{6,4},{7,5},{8,10},{9,11},{10,... | collective-permute-start | bytes 589832 | tf_op jit(solution)/shard_map/ppermute | solution.py:387
  77.4 12.9 %collective-permute-start.17 = (bf16[4,32,768]{2,1,0:T(8,128)(2,1)S(1)}, bf16[4,32,768]{2,1,0:T(8,128)(2,1)S(1)}, u32[]{:S(2)}, u32[]{:S(2)}) collective-permute-start(bf16[4,32,768]{2,1,0:T(8,128)(2,1)S(1)} %get-tuple-element.64), channel_id=1, source_target_pairs={{0,3},{1,2},{2,1},{3,0},{4,7},{5,6},{6,5},{7,4},{8,11},{9,10},{10,... | collective-permute-start | bytes 589832 | tf_op jit(solution)/shard_map/ppermute | solution.py:387
  82.3 15.4 %collective-permute-start.21 = (bf16[4,32,768]{2,1,0:T(8,128)(2,1)S(1)}, bf16[4,32,768]{2,1,0:T(8,128)(2,1)S(1)}, u32[]{:S(2)}, u32[]{:S(2)}) collective-permute-start(bf16[4,32,768]{2,1,0:T(8,128)(2,1)S(1)} %get-tuple-element.70), channel_id=1, source_target_pairs={{0,8},{1,9},{2,10},{3,11},{4,12},{5,13},{6,14},{7,15},{8,0},{9,1},... | collective-permute-start | bytes 589832 | tf_op jit(solution)/shard_map/ppermute | solution.py:387
  82.3 15.3 %collective-permute-start.22 = (bf16[4,32,768]{2,1,0:T(8,128)(2,1)S(1)}, bf16[4,32,768]{2,1,0:T(8,128)(2,1)S(1)}, u32[]{:S(2)}, u32[]{:S(2)}) collective-permute-start(bf16[4,32,768]{2,1,0:T(8,128)(2,1)S(1)} %get-tuple-element.71), channel_id=1, source_target_pairs={{0,12},{1,13},{2,14},{3,15},{4,8},{5,9},{6,10},{7,11},{8,4},{9,5},... | collective-permute-start | bytes 589832 | tf_op jit(solution)/shard_map/ppermute | solution.py:387
  84.3 14.6 %collective-permute-start.23 = (bf16[4,32,768]{2,1,0:T(8,128)(2,1)S(1)}, bf16[4,32,768]{2,1,0:T(8,128)(2,1)S(1)}, u32[]{:S(2)}, u32[]{:S(2)}) collective-permute-start(bf16[4,32,768]{2,1,0:T(8,128)(2,1)S(1)} %get-tuple-element.72), channel_id=1, source_target_pairs={{0,4},{1,5},{2,6},{3,7},{4,0},{5,1},{6,2},{7,3},{8,12},{9,13},{10,... | collective-permute-start | bytes 589832 | tf_op jit(solution)/shard_map/ppermute | solution.py:387

commit v4 on v3

--- a/solution.py
+++ b/solution.py
@@ -228,30 +228,48 @@
     )(*pieces)
 
 
+def halves_kernel(*refs):
+    ins, outs = refs[:4], refs[4:]
+    for i in range(4):
+        for p in range(4):
+            tiles = [ins[i][f, p].astype(F32) for f in range(2)]
+            for half in range(2):
+                rows = [tile[half * HALF : (half + 1) * HALF] for tile in tiles]
+                outs[4 * half + p][i] = jnp.concatenate(rows, axis=0).astype(BF16)
+
+
+def halves(pieces):
+    shape = (4,) + pieces[0].shape[2:]
+    blocks = pl.pallas_call(
+        halves_kernel,
+        in_specs=[VMEM] * 4,
+        out_specs=[VMEM] * 8,
+        out_shape=[jax.ShapeDtypeStruct(shape, BF16)] * 8,
+        compiler_params=pltpu.CompilerParams(vmem_limit_bytes=4 << 20),
+        cost_estimate=pl.CostEstimate(flops=0, bytes_accessed=1 << 20, transcendentals=0),
+        name="halves",
+    )(*pieces)
+    return blocks[:4], blocks[4:]
+
+
 def chosen(rows, columns, source):
     r = lax.broadcasted_iota(jnp.int32, (rows, columns), 0)
     c = lax.broadcasted_iota(jnp.int32, (rows, columns), 1)
     return (c == source(r)).astype(F32).astype(BF16)
 
 
-def gather(parts, tile, scratch, positions, length, a):
-    count = positions.stop - positions.start
-    pick = chosen(
-        count * TILE, TILE * TILE, lambda r: (r % TILE) * TILE + positions.start + r // TILE
-    )
+def project_kernel(*refs):
+    parts, wqkv, qkv, scratch, a = refs[:4], *refs[4:]
+    length = 2 * TILE
+    pick = chosen(TILE * TILE, TILE * TILE, lambda r: r % TILE * TILE + r // TILE)
     for block in range(2):
         for n in range(TILE):
             p, i, f = 2 * block + n // 8, n // 2 % 4, n % 2
-            scratch[n * TILE : (n + 1) * TILE, :] = tile(parts, p, i, f)
+            scratch[n * TILE : (n + 1) * TILE, :] = parts[i][p, f]
         taken = jnp.dot(pick, scratch[...], preferred_element_type=F32).astype(BF16)
-        for q in range(count):
+        for q in range(TILE):
             start = q * length + block * TILE
             a[start : start + TILE, :] = taken[q * TILE : (q + 1) * TILE]
-
-
-def project_kernel(*refs):
-    parts, wqkv, qkv, scratch, a = refs[:4], *refs[4:]
-    gather(parts, lambda z, p, i, f: z[i][p, f], scratch, slice(0, TILE), 2 * TILE, a)
     for j in range(3):
         project_rows(a, wqkv, qkv, (0,), j)
 
@@ -273,7 +291,7 @@
     )(*parts, wqkv)
 
 
-def temporal_kernel(half, outer_first, early, *refs):
+def temporal_kernel(half, outer_first, me, early, *refs):
     parts, wqkv, wo, outs = refs[:4], refs[4], refs[5], refs[6:10]
     scratch, a, qkv, mixed, change, bias = refs[10:]
     length = 2 * TILE
@@ -281,14 +299,16 @@
     row, column = (lax.broadcasted_iota(jnp.int32, bias.shape, axis) for axis in range(2))
     other = ((row ^ column) & (run - length)) != 0
     bias[...] = jnp.where(other, -jnp.inf, 0.0)
-    gather(
-        parts,
-        lambda y, p, i, f: y[p][i, f],
-        scratch,
-        slice(half * HALF, (half + 1) * HALF),
-        length,
-        a,
+    for p in range(4):
+        for i in range(4):
+            start = (4 * p + i) * TILE
+            scratch[start : start + TILE, :] = parts[p][i]
+    pick = chosen(
+        HALF * length,
+        HALF * length,
+        lambda r: r % length // 2 * TILE + r % 2 * HALF + r // length,
     )
+    a[...] = jnp.dot(pick, scratch[...], preferred_element_type=F32).astype(BF16)
     groups = range(HALF // 4)
     for g in groups:
         first = (half * HALF + 4 * g) * length
@@ -315,13 +335,13 @@
                     outs[i][p, at] = tile
 
 
-def temporal(half, early, parts, wqkv, wo, outer_first):
+def temporal(me, half, early, parts, wqkv, wo, outer_first):
     d = wo.shape[0]
     rows = HALF * 2 * TILE
     block = jax.ShapeDtypeStruct((4, 2 * TILE, d), BF16)
     return pl.pallas_call(
         functools.partial(temporal_kernel, half, outer_first),
-        in_specs=[VMEM] * 7,
+        in_specs=[SMEM] + [VMEM] * 7,
         out_specs=[VMEM] * 4,
         out_shape=[block] * 4,
         scratch_shapes=[
@@ -339,7 +359,7 @@
             transcendentals=2 * rows * GROUP * HEADS,
         ),
         name="temporal",
-    )(early, *parts, wqkv, wo)
+    )(me, early, *parts, wqkv, wo)
 
 
 def last_kernel(me, mid01, mid23, *refs):
@@ -381,6 +401,10 @@
     )(me, mid01, mid23, *early, *late)
 
 
+def after(block, earlier):
+    return lax.optimization_barrier((block, earlier))[0]
+
+
 def exchange(pieces, masks):
     size = lax.axis_size("wide")
     return [pieces[0]] + [
@@ -394,11 +418,14 @@
     mid01, *pieces = spatial(me, frames_in, 0, 2, qkv_spatial, out_spatial, True, True)
     z_parts = exchange(regroup(exchange(pieces, OUTER)), INNER)
     mid23, *pieces = spatial(me, frames_in, 2, 2, qkv_spatial, out_spatial, False, False)
-    y_parts = exchange(regroup(exchange(pieces, INNER)), OUTER)
+    first_half, second_half = halves(exchange(pieces, INNER))
+    first_half = exchange(first_half, OUTER)
     projected = project_early(z_parts, qkv_temporal)
-    pieces = temporal(0, projected, y_parts, qkv_temporal, out_temporal, True)
+    pieces = temporal(me, 0, projected, first_half, qkv_temporal, out_temporal, True)
     early = exchange(regroup(exchange(pieces, OUTER)), INNER)
-    pieces = temporal(1, projected, y_parts, qkv_temporal, out_temporal, False)
+    second_half = after(second_half, projected)
+    second_half = exchange(second_half, OUTER)
+    pieces = temporal(me, 1, projected, second_half, qkv_temporal, out_temporal, False)
     late = exchange(regroup(exchange(pieces, INNER)), OUTER)
     return last(me, mid01, mid23, early, late)
 

time: 101 us -> 97.9 us (0.969)
  waiting for transfers between devices: 45.3 us -> 38.3 us
  starting transfers between devices: 26.2 us -> 29.6 us
    ppermute x24 -> x27, waiting for transfers between devices: 45.3 us -> 38.3 us  [exchange(): lax.ppermute(piece, 'wide', [(w, w ^ mask) for w in range(size)])]
    ppermute x24 -> x27, starting transfers between devices: 26.2 us -> 29.6 us  [exchange(): lax.ppermute(piece, 'wide', [(w, w ^ mask) for w in range(size)])]
  transfers between devices with their start and end apart: 24 -> 27, of which waited for: 14 -> 12; matrix products, arithmetic and copies ran while one was open for 0% -> 0% of each run, Pallas kernels for 14% -> 20%
where the time goes in v4:
time: 97.9 us; the launch traced here: 97.1 us
  waiting for transfers between devices  38.3 us (39%)
  starting transfers between devices  29.6 us (30%)
  Pallas kernels  29.1 us (30%)
    ppermute x27, waiting for transfers between devices, exchange(): lax.ppermute(piece, 'wide', [(w, w ^ mask) for w in range(size)])  38.3 us
    ppermute x27, starting transfers between devices, exchange(): lax.ppermute(piece, 'wide', [(w, w ^ mask) for w in range(size)])  29.6 us
    pallas_call x2, Pallas kernels, spatial(): pl.pallas_call(functools.partial(spatial_kernel, outer_first, begin, fetc...  13.4 us
    pallas_call x2, Pallas kernels, temporal(): pl.pallas_call(functools.partial(temporal_kernel, half, outer_first), in_...  11.3 us
    pallas_call x1, Pallas kernels, project_early(): pl.pallas_call(project_kernel, in_specs=[VMEM] * 5, out_specs=VMEM, out_s...  2.47 us
  transfers between devices with their start and end apart: 27, of which 12 were waited for; matrix products, arithmetic and copies ran while one was open for 0% of the time, Pallas kernels for 20%

profile of v4, /device:TPU:0, one launch (start us, length us, event | category | flops | bytes accessed | tf_op | source)
XLA Modules:
  0.0 97.1 jit_solution(4023952950632675833)
XLA Ops:
  0.0 8.0 %spatial_outer.1 = (bf16[2,256,768]{2,1,0:T(8,128)(2,1)S(1)}, bf16[2,4,16,768]{3,2,1,0:T(8,128)(2,1)S(1)}, bf16[2,4,16,768]{3,2,1,0:T(8,128)(2,1)S(1)}, bf16[2,4...) custom-call(s32[1]{0:T(128)} %bitcast.me, bf16[4,256,768]{2,1,0:T(8,128)(2,1)} %x_in.3, bf16[768,2304]{1,0:T(8,128)(2,1)} %wqkv_in.3, ...), custom_call_target="tpu_custom_call" | custom-call | flops 4026531840 | bytes 4718592 | tf_op jit(solution)/shard_map/spatial_outer/pallas_call | solution.py:185
  8.0 4.1 %collective-permute-start = (bf16[2,4,16,768]{3,2,1,0:T(8,128)(2,1)S(1)}, bf16[2,4,16,768]{3,2,1,0:T(8,128)(2,1)S(1)}, u32[]{:S(2)}, u32[]{:S(2)}) collective-permute-start(bf16[2,4,16,768]{3,2,1,0:T(8,128)(2,1)S(1)} %get-tuple-element.50), channel_id=1, source_target_pairs={{0,8},{1,9},{2,10},{3,11},{4,12},{5,13},{6,14},{7,15},{8,0},{9,1},... | collective-permute-start | bytes 589832 | tf_op jit(solution)/shard_map/ppermute | solution.py:411
  12.1 1.3 %collective-permute-start.1 = (bf16[2,4,16,768]{3,2,1,0:T(8,128)(2,1)S(1)}, bf16[2,4,16,768]{3,2,1,0:T(8,128)(2,1)S(1)}, u32[]{:S(2)}, u32[]{:S(2)}) collective-permute-start(bf16[2,4,16,768]{3,2,1,0:T(8,128)(2,1)S(1)} %get-tuple-element.51), channel_id=1, source_target_pairs={{0,12},{1,13},{2,14},{3,15},{4,8},{5,9},{6,10},{7,11},{8,4},{9,5},... | collective-permute-start | bytes 589832 | tf_op jit(solution)/shard_map/ppermute | solution.py:411
  13.7 5.4 %spatial_inner.1 = (bf16[2,256,768]{2,1,0:T(8,128)(2,1)S(1)}, bf16[2,4,16,768]{3,2,1,0:T(8,128)(2,1)S(1)}, bf16[2,4,16,768]{3,2,1,0:T(8,128)(2,1)S(1)}, bf16[2,4...) custom-call(s32[1]{0:T(128)} %bitcast.me, bf16[4,256,768]{2,1,0:T(8,128)(2,1)S(1)} %copy-done.2, ...), custom_call_target="tpu_custom_call" | custom-call | flops 4026531840 | bytes 4718592 | tf_op jit(solution)/shard_map/spatial_inner/pallas_call | solution.py:185
  19.2 1.6 %collective-permute-start.7 = (bf16[2,4,16,768]{3,2,1,0:T(8,128)(2,1)S(1)}, bf16[2,4,16,768]{3,2,1,0:T(8,128)(2,1)S(1)}, u32[]{:S(2)}, u32[]{:S(2)}) collective-permute-start(bf16[2,4,16,768]{3,2,1,0:T(8,128)(2,1)S(1)} %get-tuple-element.59), channel_id=1, source_target_pairs={{0,2},{1,3},{2,0},{3,1},{4,6},{5,7},{6,4},{7,5},{8,10},{9,11},{10,... | collective-permute-start | bytes 589832 | tf_op jit(solution)/shard_map/ppermute | solution.py:411
  20.8 5.5 %collective-permute-done.refs_1_ = bf16[2,4,16,768]{3,2,1,0:T(8,128)(2,1)S(1)} collective-permute-done((bf16[2,4,16,768]{3,2,1,0:T(8,128)(2,1)S(1)}, bf16[2,4,16,768]{3,2,1,0:T(8,128)(2,1)S(1)}, u32[]{:S(2)}, u32[]{:S(2)}) %collective-permute-start) | collective-permute-done | bytes 196640 | tf_op jit(solution)/shard_map/ppermute | solution.py:411
  26.8 1.5 %collective-permute-start.3 = (bf16[4,2,16,768]{3,2,1,0:T(8,128)(2,1)S(1)}, bf16[4,2,16,768]{3,2,1,0:T(8,128)(2,1)S(1)}, u32[]{:S(2)}, u32[]{:S(2)}) collective-permute-start(bf16[4,2,16,768]{3,2,1,0:T(8,128)(2,1)S(1)} %get-tuple-element.54), channel_id=1, source_target_pairs={{0,1},{1,0},{2,3},{3,2},{4,5},{5,4},{6,7},{7,6},{8,9},{9,8},{10,11... | collective-permute-start | bytes 589832 | tf_op jit(solution)/shard_map/ppermute | solution.py:411
  28.6 1.3 %collective-permute-start.5 = (bf16[4,2,16,768]{3,2,1,0:T(8,128)(2,1)S(1)}, bf16[4,2,16,768]{3,2,1,0:T(8,128)(2,1)S(1)}, u32[]{:S(2)}, u32[]{:S(2)}) collective-permute-start(bf16[4,2,16,768]{3,2,1,0:T(8,128)(2,1)S(1)} %get-tuple-element.56), channel_id=1, source_target_pairs={{0,3},{1,2},{2,1},{3,0},{4,7},{5,6},{6,5},{7,4},{8,11},{9,10},{10,... | collective-permute-start | bytes 589832 | tf_op jit(solution)/shard_map/ppermute | solution.py:411
  29.8 3.3 %collective-permute-done.8.refs_3_ = bf16[2,4,16,768]{3,2,1,0:T(8,128)(2,1)S(1)} collective-permute-done((bf16[2,4,16,768]{3,2,1,0:T(8,128)(2,1)S(1)}, bf16[2,4,16,768]{3,2,1,0:T(8,128)(2,1)S(1)}, u32[]{:S(2)}, u32[]{:S(2)}) %collective-permute-start.8) | collective-permute-done | bytes 196640 | tf_op jit(solution)/shard_map/ppermute | solution.py:411
  33.2 1.2 %collective-permute-start.9 = (bf16[4,16,768]{2,1,0:T(8,128)(2,1)S(1)}, bf16[4,16,768]{2,1,0:T(8,128)(2,1)S(1)}, u32[]{:S(2)}, u32[]{:S(2)}) collective-permute-start(bf16[4,16,768]{2,1,0:T(8,128)(2,1)S(1)} %get-tuple-element.62), channel_id=1, source_target_pairs={{0,8},{1,9},{2,10},{3,11},{4,12},{5,13},{6,14},{7,15},{8,0},{9,1},... | collective-permute-start | bytes 294920 | tf_op jit(solution)/shard_map/ppermute | solution.py:411
  34.4 1.9 %collective-permute-start.10 = (bf16[4,16,768]{2,1,0:T(8,128)(2,1)S(1)}, bf16[4,16,768]{2,1,0:T(8,128)(2,1)S(1)}, u32[]{:S(2)}, u32[]{:S(2)}) collective-permute-start(bf16[4,16,768]{2,1,0:T(8,128)(2,1)S(1)} %get-tuple-element.63), channel_id=1, source_target_pairs={{0,12},{1,13},{2,14},{3,15},{4,8},{5,9},{6,10},{7,11},{8,4},{9,5},... | collective-permute-start | bytes 294920 | tf_op jit(solution)/shard_map/ppermute | solution.py:411
  36.9 1.2 %collective-permute-done.4.refs_2_ = bf16[4,2,16,768]{3,2,1,0:T(8,128)(2,1)S(1)} collective-permute-done((bf16[4,2,16,768]{3,2,1,0:T(8,128)(2,1)S(1)}, bf16[4,2,16,768]{3,2,1,0:T(8,128)(2,1)S(1)}, u32[]{:S(2)}, u32[]{:S(2)}) %collective-permute-start.4) | collective-permute-done | bytes 196640 | tf_op jit(solution)/shard_map/ppermute | solution.py:411
  38.0 3.5 %collective-permute-done.5.refs_3_ = bf16[4,2,16,768]{3,2,1,0:T(8,128)(2,1)S(1)} collective-permute-done((bf16[4,2,16,768]{3,2,1,0:T(8,128)(2,1)S(1)}, bf16[4,2,16,768]{3,2,1,0:T(8,128)(2,1)S(1)}, u32[]{:S(2)}, u32[]{:S(2)}) %collective-permute-start.5) | collective-permute-done | bytes 196640 | tf_op jit(solution)/shard_map/ppermute | solution.py:411
  41.6 2.5 %project_early.1.early = bf16[512,2304]{1,0:T(8,128)(2,1)S(1)} custom-call(bf16[4,2,16,768]{3,2,1,0:T(8,128)(2,1)S(1)} %get-tuple-element.53.refs_0_, bf16[4,2,16,768]{3,2,1,0:T(8,128)(2,1)S(1)} %collective-permute-done.3.refs_1_, bf16[4,2,16,768]{3,2,1,0:T(8,128)(2,1)S(1)} %collective-permute-done.4.refs_2_, ...), custom_call_target="tpu_custom_call" | custom-call | flops 1811939328 | bytes 3538944 | tf_op jit(solution)/shard_map/project_early/pallas_call | solution.py:280
  44.1 2.0 %collective-permute-start.18 = (bf16[4,16,768]{2,1,0:T(8,128)(2,1)S(1)}, bf16[4,16,768]{2,1,0:T(8,128)(2,1)S(1)}, u32[]{:S(2)}, u32[]{:S(2)}) collective-permute-start(bf16[4,16,768]{2,1,0:T(8,128)(2,1)S(1)} %get-tuple-element.78), channel_id=1, source_target_pairs={{0,8},{1,9},{2,10},{3,11},{4,12},{5,13},{6,14},{7,15},{8,0},{9,1},... | collective-permute-start | bytes 294920 | tf_op jit(solution)/shard_map/ppermute | solution.py:411
  46.1 1.2 %collective-permute-start.19 = (bf16[4,16,768]{2,1,0:T(8,128)(2,1)S(1)}, bf16[4,16,768]{2,1,0:T(8,128)(2,1)S(1)}, u32[]{:S(2)}, u32[]{:S(2)}) collective-permute-start(bf16[4,16,768]{2,1,0:T(8,128)(2,1)S(1)} %get-tuple-element.79), channel_id=1, source_target_pairs={{0,12},{1,13},{2,14},{3,15},{4,8},{5,9},{6,10},{7,11},{8,4},{9,5},... | collective-permute-start | bytes 294920 | tf_op jit(solution)/shard_map/ppermute | solution.py:411
  47.7 5.6 %temporal.2 = (bf16[4,32,768]{2,1,0:T(8,128)(2,1)S(1)}, bf16[4,32,768]{2,1,0:T(8,128)(2,1)S(1)}, bf16[4,32,768]{2,1,0:T(8,128)(2,1)S(1)}, bf16[4,32,768]{2,1,0:T(8,128)(2,1)S(1)}) custom-call(s32[1]{0:T(128)} %bitcast.me, bf16[512,2304]{1,0:T(8,128)(2,1)S(1)} %project_early.1.early, bf16[4,16,768]{2,1,0:T(8,128)(2,1)S(1)} %get-tuple-element.61.refs_0_, ...), custom_call_target="tpu_custom_call" | custom-call | flops 3120562176 | bytes 4718592 | tf_op jit(solution)/shard_map/temporal/pallas_call | solution.py:342
  53.4 2.8 %collective-permute-start.12 = (bf16[4,32,768]{2,1,0:T(8,128)(2,1)S(1)}, bf16[4,32,768]{2,1,0:T(8,128)(2,1)S(1)}, u32[]{:S(2)}, u32[]{:S(2)}) collective-permute-start(bf16[4,32,768]{2,1,0:T(8,128)(2,1)S(1)} %get-tuple-element.66), channel_id=1, source_target_pairs={{0,8},{1,9},{2,10},{3,11},{4,12},{5,13},{6,14},{7,15},{8,0},{9,1},... | collective-permute-start | bytes 589832 | tf_op jit(solution)/shard_map/ppermute | solution.py:411
  56.2 1.2 %collective-permute-start.13 = (bf16[4,32,768]{2,1,0:T(8,128)(2,1)S(1)}, bf16[4,32,768]{2,1,0:T(8,128)(2,1)S(1)}, u32[]{:S(2)}, u32[]{:S(2)}) collective-permute-start(bf16[4,32,768]{2,1,0:T(8,128)(2,1)S(1)} %get-tuple-element.67), channel_id=1, source_target_pairs={{0,12},{1,13},{2,14},{3,15},{4,8},{5,9},{6,10},{7,11},{8,4},{9,5},... | collective-permute-start | bytes 589832 | tf_op jit(solution)/shard_map/ppermute | solution.py:411
  57.4 5.6 %temporal.3 = (bf16[4,32,768]{2,1,0:T(8,128)(2,1)S(1)}, bf16[4,32,768]{2,1,0:T(8,128)(2,1)S(1)}, bf16[4,32,768]{2,1,0:T(8,128)(2,1)S(1)}, bf16[4,32,768]{2,1,0:T(8,128)(2,1)S(1)}) custom-call(s32[1]{0:T(128)} %bitcast.me, bf16[512,2304]{1,0:T(8,128)(2,1)S(1)} %project_early.1.early, bf16[4,16,768]{2,1,0:T(8,128)(2,1)S(1)} %get-tuple-element.77.refs_0_, ...), custom_call_target="tpu_custom_call" | custom-call | flops 3120562176 | bytes 4718592 | tf_op jit(solution)/shard_map/temporal/pallas_call | solution.py:342
  63.1 1.6 %collective-permute-start.22 = (bf16[4,32,768]{2,1,0:T(8,128)(2,1)S(1)}, bf16[4,32,768]{2,1,0:T(8,128)(2,1)S(1)}, u32[]{:S(2)}, u32[]{:S(2)}) collective-permute-start(bf16[4,32,768]{2,1,0:T(8,128)(2,1)S(1)} %get-tuple-element.83), channel_id=1, source_target_pairs={{0,2},{1,3},{2,0},{3,1},{4,6},{5,7},{6,4},{7,5},{8,10},{9,11},{10,... | collective-permute-start | bytes 589832 | tf_op jit(solution)/shard_map/ppermute | solution.py:411
  64.7 5.7 %collective-permute-done.12.refs_1_ = bf16[4,32,768]{2,1,0:T(8,128)(2,1)S(1)} collective-permute-done((bf16[4,32,768]{2,1,0:T(8,128)(2,1)S(1)}, bf16[4,32,768]{2,1,0:T(8,128)(2,1)S(1)}, u32[]{:S(2)}, u32[]{:S(2)}) %collective-permute-start.12) | collective-permute-done | bytes 196640 | tf_op jit(solution)/shard_map/ppermute | solution.py:411
  70.8 1.3 %collective-permute-start.15 = (bf16[4,32,768]{2,1,0:T(8,128)(2,1)S(1)}, bf16[4,32,768]{2,1,0:T(8,128)(2,1)S(1)}, u32[]{:S(2)}, u32[]{:S(2)}) collective-permute-start(bf16[4,32,768]{2,1,0:T(8,128)(2,1)S(1)} %get-tuple-element.70), channel_id=1, source_target_pairs={{0,1},{1,0},{2,3},{3,2},{4,5},{5,4},{6,7},{7,6},{8,9},{9,8},{10,11... | collective-permute-start | bytes 589832 | tf_op jit(solution)/shard_map/ppermute | solution.py:411
  72.6 0.9 collective-permute-start.17
  73.6 3.9 %collective-permute-done.23.refs_3_ = bf16[4,32,768]{2,1,0:T(8,128)(2,1)S(1)} collective-permute-done((bf16[4,32,768]{2,1,0:T(8,128)(2,1)S(1)}, bf16[4,32,768]{2,1,0:T(8,128)(2,1)S(1)}, u32[]{:S(2)}, u32[]{:S(2)}) %collective-permute-start.23) | collective-permute-done | bytes 196640 | tf_op jit(solution)/shard_map/ppermute | solution.py:411
  77.6 2.9 %collective-permute-start.25 = (bf16[4,32,768]{2,1,0:T(8,128)(2,1)S(1)}, bf16[4,32,768]{2,1,0:T(8,128)(2,1)S(1)}, u32[]{:S(2)}, u32[]{:S(2)}) collective-permute-start(bf16[4,32,768]{2,1,0:T(8,128)(2,1)S(1)} %get-tuple-element.87), channel_id=1, source_target_pairs={{0,12},{1,13},{2,14},{3,15},{4,8},{5,9},{6,10},{7,11},{8,4},{9,5},... | collective-permute-start | bytes 589832 | tf_op jit(solution)/shard_map/ppermute | solution.py:411
  80.5 0.6 collective-permute-start.26
  81.1 0.8 collective-permute-done.16.refs_2_
  81.9 4.1 %collective-permute-done.17.refs_3_ = bf16[4,32,768]{2,1,0:T(8,128)(2,1)S(1)} collective-permute-done((bf16[4,32,768]{2,1,0:T(8,128)(2,1)S(1)}, bf16[4,32,768]{2,1,0:T(8,128)(2,1)S(1)}, u32[]{:S(2)}, u32[]{:S(2)}) %collective-permute-start.17) | collective-permute-done | bytes 196640 | tf_op jit(solution)/shard_map/ppermute | solution.py:411
  85.9 8.2 %collective-permute-done.24.refs_5_ = bf16[4,32,768]{2,1,0:T(8,128)(2,1)S(1)} collective-permute-done((bf16[4,32,768]{2,1,0:T(8,128)(2,1)S(1)}, bf16[4,32,768]{2,1,0:T(8,128)(2,1)S(1)}, u32[]{:S(2)}, u32[]{:S(2)}) %collective-permute-start.24) | collective-permute-done | bytes 196640 | tf_op jit(solution)/shard_map/ppermute | solution.py:411
  94.2 1.1 %collective-permute-done.26.refs_7_ = bf16[4,32,768]{2,1,0:T(8,128)(2,1)S(1)} collective-permute-done((bf16[4,32,768]{2,1,0:T(8,128)(2,1)S(1)}, bf16[4,32,768]{2,1,0:T(8,128)(2,1)S(1)}, u32[]{:S(2)}, u32[]{:S(2)}) %collective-permute-start.26) | collective-permute-done | bytes 196640 | tf_op jit(solution)/shard_map/ppermute | solution.py:411
  95.3 1.8 %last.1 = bf16[4,256,768]{2,1,0:T(8,128)(2,1)} custom-call(s32[1]{0:T(128)} %bitcast.me, bf16[2,256,768]{2,1,0:T(8,128)(2,1)S(1)} %get-tuple-element.47.mid01, bf16[2,256,768]{2,1,0:T(8,128)(2,1)S(1)} %get-tuple-element.48.mid23, bf16[4,32,768]{2,1,0:T(8,128)(2,1)S(1)} %get-tuple-element.69.refs_0_, bf16[4,32,768]{2,1,0:T(8,128)(2,1)S(1)} %collective-permute-done.15.refs_1_, ...), custom_call_target="tpu_custom_call" | custom-call | flops 786432 | bytes 1572864 | tf_op jit(solution)/shard_map/last/pallas_call | solution.py:390
  (42 shorter events, 3.3 us)
Async XLA Ops:
  0.0 13.7 %copy-start = (bf16[768,2304]{1,0:T(8,128)(2,1)S(1)}, bf16[768,2304]{1,0:T(8,128)(2,1)}, u32[]{:S(2)}) copy-start(bf16[768,2304]{1,0:T(8,128)(2,1)} %wqkv_in.3) | copy-start | bytes 10616836
  0.0 13.7 %copy-start.2 = (bf16[4,256,768]{2,1,0:T(8,128)(2,1)S(1)}, bf16[4,256,768]{2,1,0:T(8,128)(2,1)}, u32[]{:S(2)}) copy-start(bf16[4,256,768]{2,1,0:T(8,128)(2,1)} %x_in.3) | copy-start | bytes 4718596
  0.0 13.7 %copy-start.3 = (bf16[768,768]{1,0:T(8,128)(2,1)S(1)}, bf16[768,768]{1,0:T(8,128)(2,1)}, u32[]{:S(2)}) copy-start(bf16[768,768]{1,0:T(8,128)(2,1)} %wo_in.3) | copy-start | bytes 3538948
  8.0 18.3 %collective-permute-start = (bf16[2,4,16,768]{3,2,1,0:T(8,128)(2,1)S(1)}, bf16[2,4,16,768]{3,2,1,0:T(8,128)(2,1)S(1)}, u32[]{:S(2)}, u32[]{:S(2)}) collective-permute-start(bf16[2,4,16,768]{3,2,1,0:T(8,128)(2,1)S(1)} %get-tuple-element.50), channel_id=1, source_target_pairs={{0,8},{1,9},{2,10},{3,11},{4,12},{5,13},{6,14},{7,15},{8,0},{9,1},... | collective-permute-start | bytes 589832 | tf_op jit(solution)/shard_map/ppermute | solution.py:411
  12.1 14.2 %collective-permute-start.1 = (bf16[2,4,16,768]{3,2,1,0:T(8,128)(2,1)S(1)}, bf16[2,4,16,768]{3,2,1,0:T(8,128)(2,1)S(1)}, u32[]{:S(2)}, u32[]{:S(2)}) collective-permute-start(bf16[2,4,16,768]{3,2,1,0:T(8,128)(2,1)S(1)} %get-tuple-element.51), channel_id=1, source_target_pairs={{0,12},{1,13},{2,14},{3,15},{4,8},{5,9},{6,10},{7,11},{8,4},{9,5},... | collective-permute-start | bytes 589832 | tf_op jit(solution)/shard_map/ppermute | solution.py:411
  13.4 13.4 %collective-permute-start.2 = (bf16[2,4,16,768]{3,2,1,0:T(8,128)(2,1)S(1)}, bf16[2,4,16,768]{3,2,1,0:T(8,128)(2,1)S(1)}, u32[]{:S(2)}, u32[]{:S(2)}) collective-permute-start(bf16[2,4,16,768]{3,2,1,0:T(8,128)(2,1)S(1)} %get-tuple-element.52), channel_id=1, source_target_pairs={{0,4},{1,5},{2,6},{3,7},{4,0},{5,1},{6,2},{7,3},{8,12},{9,13},{10,... | collective-permute-start | bytes 589832 | tf_op jit(solution)/shard_map/ppermute | solution.py:411
  13.7 27.9 %copy-start.1 = (bf16[768,2304]{1,0:T(8,128)(2,1)S(1)}, bf16[768,2304]{1,0:T(8,128)(2,1)}, u32[]{:S(2)}) copy-start(bf16[768,2304]{1,0:T(8,128)(2,1)} %refs_4_.5) | copy-start | bytes 10616836
  19.1 9.5 %collective-permute-start.6 = (bf16[2,4,16,768]{3,2,1,0:T(8,128)(2,1)S(1)}, bf16[2,4,16,768]{3,2,1,0:T(8,128)(2,1)S(1)}, u32[]{:S(2)}, u32[]{:S(2)}) collective-permute-start(bf16[2,4,16,768]{3,2,1,0:T(8,128)(2,1)S(1)} %get-tuple-element.58), channel_id=1, source_target_pairs={{0,1},{1,0},{2,3},{3,2},{4,5},{5,4},{6,7},{7,6},{8,9},{9,8},{10,11... | collective-permute-start | bytes 589832 | tf_op jit(solution)/shard_map/ppermute | solution.py:411
  19.2 10.7 %collective-permute-start.7 = (bf16[2,4,16,768]{3,2,1,0:T(8,128)(2,1)S(1)}, bf16[2,4,16,768]{3,2,1,0:T(8,128)(2,1)S(1)}, u32[]{:S(2)}, u32[]{:S(2)}) collective-permute-start(bf16[2,4,16,768]{3,2,1,0:T(8,128)(2,1)S(1)} %get-tuple-element.59), channel_id=1, source_target_pairs={{0,2},{1,3},{2,0},{3,1},{4,6},{5,7},{6,4},{7,5},{8,10},{9,11},{10,... | collective-permute-start | bytes 589832 | tf_op jit(solution)/shard_map/ppermute | solution.py:411
  26.3 6.9 %collective-permute-start.8 = (bf16[2,4,16,768]{3,2,1,0:T(8,128)(2,1)S(1)}, bf16[2,4,16,768]{3,2,1,0:T(8,128)(2,1)S(1)}, u32[]{:S(2)}, u32[]{:S(2)}) collective-permute-start(bf16[2,4,16,768]{3,2,1,0:T(8,128)(2,1)S(1)} %get-tuple-element.60), channel_id=1, source_target_pairs={{0,3},{1,2},{2,1},{3,0},{4,7},{5,6},{6,5},{7,4},{8,11},{9,10},{10,... | collective-permute-start | bytes 589832 | tf_op jit(solution)/shard_map/ppermute | solution.py:411
  26.8 9.5 %collective-permute-start.3 = (bf16[4,2,16,768]{3,2,1,0:T(8,128)(2,1)S(1)}, bf16[4,2,16,768]{3,2,1,0:T(8,128)(2,1)S(1)}, u32[]{:S(2)}, u32[]{:S(2)}) collective-permute-start(bf16[4,2,16,768]{3,2,1,0:T(8,128)(2,1)S(1)} %get-tuple-element.54), channel_id=1, source_target_pairs={{0,1},{1,0},{2,3},{3,2},{4,5},{5,4},{6,7},{7,6},{8,9},{9,8},{10,11... | collective-permute-start | bytes 589832 | tf_op jit(solution)/shard_map/ppermute | solution.py:411
  28.4 9.6 %collective-permute-start.4 = (bf16[4,2,16,768]{3,2,1,0:T(8,128)(2,1)S(1)}, bf16[4,2,16,768]{3,2,1,0:T(8,128)(2,1)S(1)}, u32[]{:S(2)}, u32[]{:S(2)}) collective-permute-start(bf16[4,2,16,768]{3,2,1,0:T(8,128)(2,1)S(1)} %get-tuple-element.55), channel_id=1, source_target_pairs={{0,2},{1,3},{2,0},{3,1},{4,6},{5,7},{6,4},{7,5},{8,10},{9,11},{10,... | collective-permute-start | bytes 589832 | tf_op jit(solution)/shard_map/ppermute | solution.py:411
  28.6 13.0 %collective-permute-start.5 = (bf16[4,2,16,768]{3,2,1,0:T(8,128)(2,1)S(1)}, bf16[4,2,16,768]{3,2,1,0:T(8,128)(2,1)S(1)}, u32[]{:S(2)}, u32[]{:S(2)}) collective-permute-start(bf16[4,2,16,768]{3,2,1,0:T(8,128)(2,1)S(1)} %get-tuple-element.56), channel_id=1, source_target_pairs={{0,3},{1,2},{2,1},{3,0},{4,7},{5,6},{6,5},{7,4},{8,11},{9,10},{10,... | collective-permute-start | bytes 589832 | tf_op jit(solution)/shard_map/ppermute | solution.py:411
  33.2 14.0 %collective-permute-start.9 = (bf16[4,16,768]{2,1,0:T(8,128)(2,1)S(1)}, bf16[4,16,768]{2,1,0:T(8,128)(2,1)S(1)}, u32[]{:S(2)}, u32[]{:S(2)}) collective-permute-start(bf16[4,16,768]{2,1,0:T(8,128)(2,1)S(1)} %get-tuple-element.62), channel_id=1, source_target_pairs={{0,8},{1,9},{2,10},{3,11},{4,12},{5,13},{6,14},{7,15},{8,0},{9,1},... | collective-permute-start | bytes 294920 | tf_op jit(solution)/shard_map/ppermute | solution.py:411
  34.4 13.3 %collective-permute-start.10 = (bf16[4,16,768]{2,1,0:T(8,128)(2,1)S(1)}, bf16[4,16,768]{2,1,0:T(8,128)(2,1)S(1)}, u32[]{:S(2)}, u32[]{:S(2)}) collective-permute-start(bf16[4,16,768]{2,1,0:T(8,128)(2,1)S(1)} %get-tuple-element.63), channel_id=1, source_target_pairs={{0,12},{1,13},{2,14},{3,15},{4,8},{5,9},{6,10},{7,11},{8,4},{9,5},... | collective-permute-start | bytes 294920 | tf_op jit(solution)/shard_map/ppermute | solution.py:411
  36.4 11.3 %collective-permute-start.11 = (bf16[4,16,768]{2,1,0:T(8,128)(2,1)S(1)}, bf16[4,16,768]{2,1,0:T(8,128)(2,1)S(1)}, u32[]{:S(2)}, u32[]{:S(2)}) collective-permute-start(bf16[4,16,768]{2,1,0:T(8,128)(2,1)S(1)} %get-tuple-element.64), channel_id=1, source_target_pairs={{0,4},{1,5},{2,6},{3,7},{4,0},{5,1},{6,2},{7,3},{8,12},{9,13},{10,... | collective-permute-start | bytes 294920 | tf_op jit(solution)/shard_map/ppermute | solution.py:411
  41.6 6.2 %copy-start.4 = (bf16[768,768]{1,0:T(8,128)(2,1)S(1)}, bf16[768,768]{1,0:T(8,128)(2,1)}, u32[]{:S(2)}) copy-start(bf16[768,768]{1,0:T(8,128)(2,1)} %refs_5_.3) | copy-start | bytes 3538948
  44.1 13.3 %collective-permute-start.18 = (bf16[4,16,768]{2,1,0:T(8,128)(2,1)S(1)}, bf16[4,16,768]{2,1,0:T(8,128)(2,1)S(1)}, u32[]{:S(2)}, u32[]{:S(2)}) collective-permute-start(bf16[4,16,768]{2,1,0:T(8,128)(2,1)S(1)} %get-tuple-element.78), channel_id=1, source_target_pairs={{0,8},{1,9},{2,10},{3,11},{4,12},{5,13},{6,14},{7,15},{8,0},{9,1},... | collective-permute-start | bytes 294920 | tf_op jit(solution)/shard_map/ppermute | solution.py:411
  46.1 11.3 %collective-permute-start.19 = (bf16[4,16,768]{2,1,0:T(8,128)(2,1)S(1)}, bf16[4,16,768]{2,1,0:T(8,128)(2,1)S(1)}, u32[]{:S(2)}, u32[]{:S(2)}) collective-permute-start(bf16[4,16,768]{2,1,0:T(8,128)(2,1)S(1)} %get-tuple-element.79), channel_id=1, source_target_pairs={{0,12},{1,13},{2,14},{3,15},{4,8},{5,9},{6,10},{7,11},{8,4},{9,5},... | collective-permute-start | bytes 294920 | tf_op jit(solution)/shard_map/ppermute | solution.py:411
  47.2 10.1 %collective-permute-start.20 = (bf16[4,16,768]{2,1,0:T(8,128)(2,1)S(1)}, bf16[4,16,768]{2,1,0:T(8,128)(2,1)S(1)}, u32[]{:S(2)}, u32[]{:S(2)}) collective-permute-start(bf16[4,16,768]{2,1,0:T(8,128)(2,1)S(1)} %get-tuple-element.80), channel_id=1, source_target_pairs={{0,4},{1,5},{2,6},{3,7},{4,0},{5,1},{6,2},{7,3},{8,12},{9,13},{10,... | collective-permute-start | bytes 294920 | tf_op jit(solution)/shard_map/ppermute | solution.py:411
  53.4 17.0 %collective-permute-start.12 = (bf16[4,32,768]{2,1,0:T(8,128)(2,1)S(1)}, bf16[4,32,768]{2,1,0:T(8,128)(2,1)S(1)}, u32[]{:S(2)}, u32[]{:S(2)}) collective-permute-start(bf16[4,32,768]{2,1,0:T(8,128)(2,1)S(1)} %get-tuple-element.66), channel_id=1, source_target_pairs={{0,8},{1,9},{2,10},{3,11},{4,12},{5,13},{6,14},{7,15},{8,0},{9,1},... | collective-permute-start | bytes 589832 | tf_op jit(solution)/shard_map/ppermute | solution.py:411
  56.2 14.2 %collective-permute-start.13 = (bf16[4,32,768]{2,1,0:T(8,128)(2,1)S(1)}, bf16[4,32,768]{2,1,0:T(8,128)(2,1)S(1)}, u32[]{:S(2)}, u32[]{:S(2)}) collective-permute-start(bf16[4,32,768]{2,1,0:T(8,128)(2,1)S(1)} %get-tuple-element.67), channel_id=1, source_target_pairs={{0,12},{1,13},{2,14},{3,15},{4,8},{5,9},{6,10},{7,11},{8,4},{9,5},... | collective-permute-start | bytes 589832 | tf_op jit(solution)/shard_map/ppermute | solution.py:411
  57.3 13.4 %collective-permute-start.14 = (bf16[4,32,768]{2,1,0:T(8,128)(2,1)S(1)}, bf16[4,32,768]{2,1,0:T(8,128)(2,1)S(1)}, u32[]{:S(2)}, u32[]{:S(2)}) collective-permute-start(bf16[4,32,768]{2,1,0:T(8,128)(2,1)S(1)} %get-tuple-element.68), channel_id=1, source_target_pairs={{0,4},{1,5},{2,6},{3,7},{4,0},{5,1},{6,2},{7,3},{8,12},{9,13},{10,... | collective-permute-start | bytes 589832 | tf_op jit(solution)/shard_map/ppermute | solution.py:411
  63.0 9.7 %collective-permute-start.21 = (bf16[4,32,768]{2,1,0:T(8,128)(2,1)S(1)}, bf16[4,32,768]{2,1,0:T(8,128)(2,1)S(1)}, u32[]{:S(2)}, u32[]{:S(2)}) collective-permute-start(bf16[4,32,768]{2,1,0:T(8,128)(2,1)S(1)} %get-tuple-element.82), channel_id=1, source_target_pairs={{0,1},{1,0},{2,3},{3,2},{4,5},{5,4},{6,7},{7,6},{8,9},{9,8},{10,11... | collective-permute-start | bytes 589832 | tf_op jit(solution)/shard_map/ppermute | solution.py:411
  63.1 10.5 %collective-permute-start.22 = (bf16[4,32,768]{2,1,0:T(8,128)(2,1)S(1)}, bf16[4,32,768]{2,1,0:T(8,128)(2,1)S(1)}, u32[]{:S(2)}, u32[]{:S(2)}) collective-permute-start(bf16[4,32,768]{2,1,0:T(8,128)(2,1)S(1)} %get-tuple-element.83), channel_id=1, source_target_pairs={{0,2},{1,3},{2,0},{3,1},{4,6},{5,7},{6,4},{7,5},{8,10},{9,11},{10,... | collective-permute-start | bytes 589832 | tf_op jit(solution)/shard_map/ppermute | solution.py:411
  70.4 7.1 %collective-permute-start.23 = (bf16[4,32,768]{2,1,0:T(8,128)(2,1)S(1)}, bf16[4,32,768]{2,1,0:T(8,128)(2,1)S(1)}, u32[]{:S(2)}, u32[]{:S(2)}) collective-permute-start(bf16[4,32,768]{2,1,0:T(8,128)(2,1)S(1)} %get-tuple-element.84), channel_id=1, source_target_pairs={{0,3},{1,2},{2,1},{3,0},{4,7},{5,6},{6,5},{7,4},{8,11},{9,10},{10,... | collective-permute-start | bytes 589832 | tf_op jit(solution)/shard_map/ppermute | solution.py:411
  70.8 9.7 %collective-permute-start.15 = (bf16[4,32,768]{2,1,0:T(8,128)(2,1)S(1)}, bf16[4,32,768]{2,1,0:T(8,128)(2,1)S(1)}, u32[]{:S(2)}, u32[]{:S(2)}) collective-permute-start(bf16[4,32,768]{2,1,0:T(8,128)(2,1)S(1)} %get-tuple-element.70), channel_id=1, source_target_pairs={{0,1},{1,0},{2,3},{3,2},{4,5},{5,4},{6,7},{7,6},{8,9},{9,8},{10,11... | collective-permute-start | bytes 589832 | tf_op jit(solution)/shard_map/ppermute | solution.py:411
  72.1 9.7 %collective-permute-start.16 = (bf16[4,32,768]{2,1,0:T(8,128)(2,1)S(1)}, bf16[4,32,768]{2,1,0:T(8,128)(2,1)S(1)}, u32[]{:S(2)}, u32[]{:S(2)}) collective-permute-start(bf16[4,32,768]{2,1,0:T(8,128)(2,1)S(1)} %get-tuple-element.71), channel_id=1, source_target_pairs={{0,2},{1,3},{2,0},{3,1},{4,6},{5,7},{6,4},{7,5},{8,10},{9,11},{10,... | collective-permute-start | bytes 589832 | tf_op jit(solution)/shard_map/ppermute | solution.py:411
  72.6 13.3 %collective-permute-start.17 = (bf16[4,32,768]{2,1,0:T(8,128)(2,1)S(1)}, bf16[4,32,768]{2,1,0:T(8,128)(2,1)S(1)}, u32[]{:S(2)}, u32[]{:S(2)}) collective-permute-start(bf16[4,32,768]{2,1,0:T(8,128)(2,1)S(1)} %get-tuple-element.72), channel_id=1, source_target_pairs={{0,3},{1,2},{2,1},{3,0},{4,7},{5,6},{6,5},{7,4},{8,11},{9,10},{10,... | collective-permute-start | bytes 589832 | tf_op jit(solution)/shard_map/ppermute | solution.py:411
  77.6 16.6 %collective-permute-start.24 = (bf16[4,32,768]{2,1,0:T(8,128)(2,1)S(1)}, bf16[4,32,768]{2,1,0:T(8,128)(2,1)S(1)}, u32[]{:S(2)}, u32[]{:S(2)}) collective-permute-start(bf16[4,32,768]{2,1,0:T(8,128)(2,1)S(1)} %get-tuple-element.86), channel_id=1, source_target_pairs={{0,8},{1,9},{2,10},{3,11},{4,12},{5,13},{6,14},{7,15},{8,0},{9,1},... | collective-permute-start | bytes 589832 | tf_op jit(solution)/shard_map/ppermute | solution.py:411
  77.6 16.5 %collective-permute-start.25 = (bf16[4,32,768]{2,1,0:T(8,128)(2,1)S(1)}, bf16[4,32,768]{2,1,0:T(8,128)(2,1)S(1)}, u32[]{:S(2)}, u32[]{:S(2)}) collective-permute-start(bf16[4,32,768]{2,1,0:T(8,128)(2,1)S(1)} %get-tuple-element.87), channel_id=1, source_target_pairs={{0,12},{1,13},{2,14},{3,15},{4,8},{5,9},{6,10},{7,11},{8,4},{9,5},... | collective-permute-start | bytes 589832 | tf_op jit(solution)/shard_map/ppermute | solution.py:411
  80.5 14.8 %collective-permute-start.26 = (bf16[4,32,768]{2,1,0:T(8,128)(2,1)S(1)}, bf16[4,32,768]{2,1,0:T(8,128)(2,1)S(1)}, u32[]{:S(2)}, u32[]{:S(2)}) collective-permute-start(bf16[4,32,768]{2,1,0:T(8,128)(2,1)S(1)} %get-tuple-element.88), channel_id=1, source_target_pairs={{0,4},{1,5},{2,6},{3,7},{4,0},{5,1},{6,2},{7,3},{8,12},{9,13},{10,... | collective-permute-start | bytes 589832 | tf_op jit(solution)/shard_map/ppermute | solution.py:411

commit v5 on v4

--- a/solution.py
+++ b/solution.py
@@ -21,7 +21,7 @@
 HBM = pl.BlockSpec(memory_space=pltpu.HBM)
 
 OUTER = (0, 8, 12, 4)
-INNER = (0, 1, 2, 3)
+INNER = (0, 2, 3, 1)
 
 
 def normalize(floats):

time: 97.9 us -> 94.3 us (0.963)
  waiting for transfers between devices: 38.3 us -> 23.9 us
  starting transfers between devices: 29.6 us -> 40.8 us
    ppermute x27, waiting for transfers between devices: 38.3 us -> 23.9 us  [exchange(): lax.ppermute(piece, 'wide', [(w, w ^ mask) for w in range(size)])]
    ppermute x27, starting transfers between devices: 29.6 us -> 40.8 us  [exchange(): lax.ppermute(piece, 'wide', [(w, w ^ mask) for w in range(size)])]
  transfers between devices with their start and end apart: 27 -> 27, of which waited for: 12 -> 6; matrix products, arithmetic and copies ran while one was open for 0% -> 0% of each run, Pallas kernels for 20% -> 21%
where the time goes in v5:
time: 94.3 us; the launch traced here: 94 us
  starting transfers between devices  40.8 us (43%)
  Pallas kernels  29.1 us (31%)
  waiting for transfers between devices  23.9 us (25%)
    ppermute x27, starting transfers between devices, exchange(): lax.ppermute(piece, 'wide', [(w, w ^ mask) for w in range(size)])  40.8 us
    ppermute x27, waiting for transfers between devices, exchange(): lax.ppermute(piece, 'wide', [(w, w ^ mask) for w in range(size)])  23.9 us
    pallas_call x2, Pallas kernels, spatial(): pl.pallas_call(functools.partial(spatial_kernel, outer_first, begin, fetc...  13.4 us
    pallas_call x2, Pallas kernels, temporal(): pl.pallas_call(functools.partial(temporal_kernel, half, outer_first), in_...  11.3 us
    pallas_call x1, Pallas kernels, project_early(): pl.pallas_call(project_kernel, in_specs=[VMEM] * 5, out_specs=VMEM, out_s...  2.48 us
  transfers between devices with their start and end apart: 27, of which 6 were waited for; matrix products, arithmetic and copies ran while one was open for 0% of the time, Pallas kernels for 21%

profile of v5, /device:TPU:0, one launch (start us, length us, event | category | flops | bytes accessed | tf_op | source)
XLA Modules:
  0.0 94.0 jit_solution(11415906639359547574)
XLA Ops:
  0.0 8.0 %spatial_outer.1 = (bf16[2,256,768]{2,1,0:T(8,128)(2,1)S(1)}, bf16[2,4,16,768]{3,2,1,0:T(8,128)(2,1)S(1)}, bf16[2,4,16,768]{3,2,1,0:T(8,128)(2,1)S(1)}, bf16[2,4...) custom-call(s32[1]{0:T(128)} %bitcast.me, bf16[4,256,768]{2,1,0:T(8,128)(2,1)} %x_in.3, bf16[768,2304]{1,0:T(8,128)(2,1)} %wqkv_in.3, ...), custom_call_target="tpu_custom_call" | custom-call | flops 4026531840 | bytes 4718592 | tf_op jit(solution)/shard_map/spatial_outer/pallas_call | solution.py:185
  8.0 4.1 %collective-permute-start = (bf16[2,4,16,768]{3,2,1,0:T(8,128)(2,1)S(1)}, bf16[2,4,16,768]{3,2,1,0:T(8,128)(2,1)S(1)}, u32[]{:S(2)}, u32[]{:S(2)}) collective-permute-start(bf16[2,4,16,768]{3,2,1,0:T(8,128)(2,1)S(1)} %get-tuple-element.50), channel_id=1, source_target_pairs={{0,8},{1,9},{2,10},{3,11},{4,12},{5,13},{6,14},{7,15},{8,0},{9,1},... | collective-permute-start | bytes 589832 | tf_op jit(solution)/shard_map/ppermute | solution.py:411
  12.1 1.3 %collective-permute-start.1 = (bf16[2,4,16,768]{3,2,1,0:T(8,128)(2,1)S(1)}, bf16[2,4,16,768]{3,2,1,0:T(8,128)(2,1)S(1)}, u32[]{:S(2)}, u32[]{:S(2)}) collective-permute-start(bf16[2,4,16,768]{3,2,1,0:T(8,128)(2,1)S(1)} %get-tuple-element.51), channel_id=1, source_target_pairs={{0,12},{1,13},{2,14},{3,15},{4,8},{5,9},{6,10},{7,11},{8,4},{9,5},... | collective-permute-start | bytes 589832 | tf_op jit(solution)/shard_map/ppermute | solution.py:411
  13.4 0.2 collective-permute-start.2
  13.7 5.4 %spatial_inner.1 = (bf16[2,256,768]{2,1,0:T(8,128)(2,1)S(1)}, bf16[2,4,16,768]{3,2,1,0:T(8,128)(2,1)S(1)}, bf16[2,4,16,768]{3,2,1,0:T(8,128)(2,1)S(1)}, bf16[2,4...) custom-call(s32[1]{0:T(128)} %bitcast.me, bf16[4,256,768]{2,1,0:T(8,128)(2,1)S(1)} %copy-done.2, ...), custom_call_target="tpu_custom_call" | custom-call | flops 4026531840 | bytes 4718592 | tf_op jit(solution)/shard_map/spatial_inner/pallas_call | solution.py:185
  19.1 1.6 %collective-permute-start.6 = (bf16[2,4,16,768]{3,2,1,0:T(8,128)(2,1)S(1)}, bf16[2,4,16,768]{3,2,1,0:T(8,128)(2,1)S(1)}, u32[]{:S(2)}, u32[]{:S(2)}) collective-permute-start(bf16[2,4,16,768]{3,2,1,0:T(8,128)(2,1)S(1)} %get-tuple-element.58), channel_id=1, source_target_pairs={{0,2},{1,3},{2,0},{3,1},{4,6},{5,7},{6,4},{7,5},{8,10},{9,11},{10,... | collective-permute-start | bytes 589832 | tf_op jit(solution)/shard_map/ppermute | solution.py:411
  20.7 5.6 %collective-permute-done.refs_1_ = bf16[2,4,16,768]{3,2,1,0:T(8,128)(2,1)S(1)} collective-permute-done((bf16[2,4,16,768]{3,2,1,0:T(8,128)(2,1)S(1)}, bf16[2,4,16,768]{3,2,1,0:T(8,128)(2,1)S(1)}, u32[]{:S(2)}, u32[]{:S(2)}) %collective-permute-start) | collective-permute-done | bytes 196640 | tf_op jit(solution)/shard_map/ppermute | solution.py:411
  26.3 0.5 collective-permute-done.2.refs_3_
  26.8 1.7 %collective-permute-start.3 = (bf16[4,2,16,768]{3,2,1,0:T(8,128)(2,1)S(1)}, bf16[4,2,16,768]{3,2,1,0:T(8,128)(2,1)S(1)}, u32[]{:S(2)}, u32[]{:S(2)}) collective-permute-start(bf16[4,2,16,768]{3,2,1,0:T(8,128)(2,1)S(1)} %get-tuple-element.54), channel_id=1, source_target_pairs={{0,2},{1,3},{2,0},{3,1},{4,6},{5,7},{6,4},{7,5},{8,10},{9,11},{10,... | collective-permute-start | bytes 589832 | tf_op jit(solution)/shard_map/ppermute | solution.py:411
  28.5 0.5 collective-permute-start.5
  29.1 5.6 %collective-permute-start.9 = (bf16[4,16,768]{2,1,0:T(8,128)(2,1)S(1)}, bf16[4,16,768]{2,1,0:T(8,128)(2,1)S(1)}, u32[]{:S(2)}, u32[]{:S(2)}) collective-permute-start(bf16[4,16,768]{2,1,0:T(8,128)(2,1)S(1)} %get-tuple-element.62), channel_id=1, source_target_pairs={{0,8},{1,9},{2,10},{3,11},{4,12},{5,13},{6,14},{7,15},{8,0},{9,1},... | collective-permute-start | bytes 294920 | tf_op jit(solution)/shard_map/ppermute | solution.py:411
  34.7 0.4 collective-permute-start.10
  35.1 3.1 %collective-permute-start.11 = (bf16[4,16,768]{2,1,0:T(8,128)(2,1)S(1)}, bf16[4,16,768]{2,1,0:T(8,128)(2,1)S(1)}, u32[]{:S(2)}, u32[]{:S(2)}) collective-permute-start(bf16[4,16,768]{2,1,0:T(8,128)(2,1)S(1)} %get-tuple-element.64), channel_id=1, source_target_pairs={{0,4},{1,5},{2,6},{3,7},{4,0},{5,1},{6,2},{7,3},{8,12},{9,13},{10,... | collective-permute-start | bytes 294920 | tf_op jit(solution)/shard_map/ppermute | solution.py:411
  38.3 2.5 %project_early.1.early = bf16[512,2304]{1,0:T(8,128)(2,1)S(1)} custom-call(bf16[4,2,16,768]{3,2,1,0:T(8,128)(2,1)S(1)} %get-tuple-element.53.refs_0_, bf16[4,2,16,768]{3,2,1,0:T(8,128)(2,1)S(1)} %collective-permute-done.3.refs_1_, bf16[4,2,16,768]{3,2,1,0:T(8,128)(2,1)S(1)} %collective-permute-done.4.refs_2_, ...), custom_call_target="tpu_custom_call" | custom-call | flops 1811939328 | bytes 3538944 | tf_op jit(solution)/shard_map/project_early/pallas_call | solution.py:280
  40.8 4.3 %collective-permute-start.18 = (bf16[4,16,768]{2,1,0:T(8,128)(2,1)S(1)}, bf16[4,16,768]{2,1,0:T(8,128)(2,1)S(1)}, u32[]{:S(2)}, u32[]{:S(2)}) collective-permute-start(bf16[4,16,768]{2,1,0:T(8,128)(2,1)S(1)} %get-tuple-element.78), channel_id=1, source_target_pairs={{0,8},{1,9},{2,10},{3,11},{4,12},{5,13},{6,14},{7,15},{8,0},{9,1},... | collective-permute-start | bytes 294920 | tf_op jit(solution)/shard_map/ppermute | solution.py:411
  45.1 0.4 collective-permute-start.19
  45.7 5.6 %temporal.2 = (bf16[4,32,768]{2,1,0:T(8,128)(2,1)S(1)}, bf16[4,32,768]{2,1,0:T(8,128)(2,1)S(1)}, bf16[4,32,768]{2,1,0:T(8,128)(2,1)S(1)}, bf16[4,32,768]{2,1,0:T(8,128)(2,1)S(1)}) custom-call(s32[1]{0:T(128)} %bitcast.me, bf16[512,2304]{1,0:T(8,128)(2,1)S(1)} %project_early.1.early, bf16[4,16,768]{2,1,0:T(8,128)(2,1)S(1)} %get-tuple-element.61.refs_0_, ...), custom_call_target="tpu_custom_call" | custom-call | flops 3120562176 | bytes 4718592 | tf_op jit(solution)/shard_map/temporal/pallas_call | solution.py:342
  51.4 3.8 %collective-permute-start.12 = (bf16[4,32,768]{2,1,0:T(8,128)(2,1)S(1)}, bf16[4,32,768]{2,1,0:T(8,128)(2,1)S(1)}, u32[]{:S(2)}, u32[]{:S(2)}) collective-permute-start(bf16[4,32,768]{2,1,0:T(8,128)(2,1)S(1)} %get-tuple-element.66), channel_id=1, source_target_pairs={{0,8},{1,9},{2,10},{3,11},{4,12},{5,13},{6,14},{7,15},{8,0},{9,1},... | collective-permute-start | bytes 589832 | tf_op jit(solution)/shard_map/ppermute | solution.py:411
  55.2 0.4 collective-permute-start.13
  55.6 0.2 collective-permute-start.14
  55.8 5.6 %temporal.3 = (bf16[4,32,768]{2,1,0:T(8,128)(2,1)S(1)}, bf16[4,32,768]{2,1,0:T(8,128)(2,1)S(1)}, bf16[4,32,768]{2,1,0:T(8,128)(2,1)S(1)}, bf16[4,32,768]{2,1,0:T(8,128)(2,1)S(1)}) custom-call(s32[1]{0:T(128)} %bitcast.me, bf16[512,2304]{1,0:T(8,128)(2,1)S(1)} %project_early.1.early, bf16[4,16,768]{2,1,0:T(8,128)(2,1)S(1)} %get-tuple-element.77.refs_0_, ...), custom_call_target="tpu_custom_call" | custom-call | flops 3120562176 | bytes 4718592 | tf_op jit(solution)/shard_map/temporal/pallas_call | solution.py:342
  61.5 1.6 %collective-permute-start.21 = (bf16[4,32,768]{2,1,0:T(8,128)(2,1)S(1)}, bf16[4,32,768]{2,1,0:T(8,128)(2,1)S(1)}, u32[]{:S(2)}, u32[]{:S(2)}) collective-permute-start(bf16[4,32,768]{2,1,0:T(8,128)(2,1)S(1)} %get-tuple-element.82), channel_id=1, source_target_pairs={{0,2},{1,3},{2,0},{3,1},{4,6},{5,7},{6,4},{7,5},{8,10},{9,11},{10,... | collective-permute-start | bytes 589832 | tf_op jit(solution)/shard_map/ppermute | solution.py:411
  63.1 5.9 %collective-permute-done.12.refs_1_ = bf16[4,32,768]{2,1,0:T(8,128)(2,1)S(1)} collective-permute-done((bf16[4,32,768]{2,1,0:T(8,128)(2,1)S(1)}, bf16[4,32,768]{2,1,0:T(8,128)(2,1)S(1)}, u32[]{:S(2)}, u32[]{:S(2)}) %collective-permute-start.12) | collective-permute-done | bytes 196640 | tf_op jit(solution)/shard_map/ppermute | solution.py:411
  69.0 1.3 %collective-permute-done.14.refs_3_ = bf16[4,32,768]{2,1,0:T(8,128)(2,1)S(1)} collective-permute-done((bf16[4,32,768]{2,1,0:T(8,128)(2,1)S(1)}, bf16[4,32,768]{2,1,0:T(8,128)(2,1)S(1)}, u32[]{:S(2)}, u32[]{:S(2)}) %collective-permute-start.14) | collective-permute-done | bytes 196640 | tf_op jit(solution)/shard_map/ppermute | solution.py:411
  70.3 1.6 %collective-permute-start.15 = (bf16[4,32,768]{2,1,0:T(8,128)(2,1)S(1)}, bf16[4,32,768]{2,1,0:T(8,128)(2,1)S(1)}, u32[]{:S(2)}, u32[]{:S(2)}) collective-permute-start(bf16[4,32,768]{2,1,0:T(8,128)(2,1)S(1)} %get-tuple-element.70), channel_id=1, source_target_pairs={{0,2},{1,3},{2,0},{3,1},{4,6},{5,7},{6,4},{7,5},{8,10},{9,11},{10,... | collective-permute-start | bytes 589832 | tf_op jit(solution)/shard_map/ppermute | solution.py:411
  71.9 0.6 collective-permute-start.17
  72.6 4.4 %collective-permute-start.24 = (bf16[4,32,768]{2,1,0:T(8,128)(2,1)S(1)}, bf16[4,32,768]{2,1,0:T(8,128)(2,1)S(1)}, u32[]{:S(2)}, u32[]{:S(2)}) collective-permute-start(bf16[4,32,768]{2,1,0:T(8,128)(2,1)S(1)} %get-tuple-element.86), channel_id=1, source_target_pairs={{0,8},{1,9},{2,10},{3,11},{4,12},{5,13},{6,14},{7,15},{8,0},{9,1},... | collective-permute-start | bytes 589832 | tf_op jit(solution)/shard_map/ppermute | solution.py:411
  77.0 1.4 %collective-permute-start.25 = (bf16[4,32,768]{2,1,0:T(8,128)(2,1)S(1)}, bf16[4,32,768]{2,1,0:T(8,128)(2,1)S(1)}, u32[]{:S(2)}, u32[]{:S(2)}) collective-permute-start(bf16[4,32,768]{2,1,0:T(8,128)(2,1)S(1)} %get-tuple-element.87), channel_id=1, source_target_pairs={{0,12},{1,13},{2,14},{3,15},{4,8},{5,9},{6,10},{7,11},{8,4},{9,5},... | collective-permute-start | bytes 589832 | tf_op jit(solution)/shard_map/ppermute | solution.py:411
  78.5 3.1 %collective-permute-start.26 = (bf16[4,32,768]{2,1,0:T(8,128)(2,1)S(1)}, bf16[4,32,768]{2,1,0:T(8,128)(2,1)S(1)}, u32[]{:S(2)}, u32[]{:S(2)}) collective-permute-start(bf16[4,32,768]{2,1,0:T(8,128)(2,1)S(1)} %get-tuple-element.88), channel_id=1, source_target_pairs={{0,4},{1,5},{2,6},{3,7},{4,0},{5,1},{6,2},{7,3},{8,12},{9,13},{10,... | collective-permute-start | bytes 589832 | tf_op jit(solution)/shard_map/ppermute | solution.py:411
  81.6 9.6 %collective-permute-done.24.refs_5_ = bf16[4,32,768]{2,1,0:T(8,128)(2,1)S(1)} collective-permute-done((bf16[4,32,768]{2,1,0:T(8,128)(2,1)S(1)}, bf16[4,32,768]{2,1,0:T(8,128)(2,1)S(1)}, u32[]{:S(2)}, u32[]{:S(2)}) %collective-permute-start.24) | collective-permute-done | bytes 196640 | tf_op jit(solution)/shard_map/ppermute | solution.py:411
  91.2 1.0 %collective-permute-done.26.refs_7_ = bf16[4,32,768]{2,1,0:T(8,128)(2,1)S(1)} collective-permute-done((bf16[4,32,768]{2,1,0:T(8,128)(2,1)S(1)}, bf16[4,32,768]{2,1,0:T(8,128)(2,1)S(1)}, u32[]{:S(2)}, u32[]{:S(2)}) %collective-permute-start.26) | collective-permute-done | bytes 196640 | tf_op jit(solution)/shard_map/ppermute | solution.py:411
  92.2 1.8 %last.1 = bf16[4,256,768]{2,1,0:T(8,128)(2,1)} custom-call(s32[1]{0:T(128)} %bitcast.me, bf16[2,256,768]{2,1,0:T(8,128)(2,1)S(1)} %get-tuple-element.47.mid01, bf16[2,256,768]{2,1,0:T(8,128)(2,1)S(1)} %get-tuple-element.48.mid23, bf16[4,32,768]{2,1,0:T(8,128)(2,1)S(1)} %get-tuple-element.69.refs_0_, bf16[4,32,768]{2,1,0:T(8,128)(2,1)S(1)} %collective-permute-done.15.refs_1_, ...), custom_call_target="tpu_custom_call" | custom-call | flops 786432 | bytes 1572864 | tf_op jit(solution)/shard_map/last/pallas_call | solution.py:390
  (42 shorter events, 0.5 us)
Async XLA Ops:
  0.0 13.7 %copy-start = (bf16[768,2304]{1,0:T(8,128)(2,1)S(1)}, bf16[768,2304]{1,0:T(8,128)(2,1)}, u32[]{:S(2)}) copy-start(bf16[768,2304]{1,0:T(8,128)(2,1)} %wqkv_in.3) | copy-start | bytes 10616836
  0.0 13.7 %copy-start.2 = (bf16[4,256,768]{2,1,0:T(8,128)(2,1)S(1)}, bf16[4,256,768]{2,1,0:T(8,128)(2,1)}, u32[]{:S(2)}) copy-start(bf16[4,256,768]{2,1,0:T(8,128)(2,1)} %x_in.3) | copy-start | bytes 4718596
  0.0 13.7 %copy-start.3 = (bf16[768,768]{1,0:T(8,128)(2,1)S(1)}, bf16[768,768]{1,0:T(8,128)(2,1)}, u32[]{:S(2)}) copy-start(bf16[768,768]{1,0:T(8,128)(2,1)} %wo_in.3) | copy-start | bytes 3538948
  8.0 18.3 %collective-permute-start = (bf16[2,4,16,768]{3,2,1,0:T(8,128)(2,1)S(1)}, bf16[2,4,16,768]{3,2,1,0:T(8,128)(2,1)S(1)}, u32[]{:S(2)}, u32[]{:S(2)}) collective-permute-start(bf16[2,4,16,768]{3,2,1,0:T(8,128)(2,1)S(1)} %get-tuple-element.50), channel_id=1, source_target_pairs={{0,8},{1,9},{2,10},{3,11},{4,12},{5,13},{6,14},{7,15},{8,0},{9,1},... | collective-permute-start | bytes 589832 | tf_op jit(solution)/shard_map/ppermute | solution.py:411
  12.1 14.2 %collective-permute-start.1 = (bf16[2,4,16,768]{3,2,1,0:T(8,128)(2,1)S(1)}, bf16[2,4,16,768]{3,2,1,0:T(8,128)(2,1)S(1)}, u32[]{:S(2)}, u32[]{:S(2)}) collective-permute-start(bf16[2,4,16,768]{3,2,1,0:T(8,128)(2,1)S(1)} %get-tuple-element.51), channel_id=1, source_target_pairs={{0,12},{1,13},{2,14},{3,15},{4,8},{5,9},{6,10},{7,11},{8,4},{9,5},... | collective-permute-start | bytes 589832 | tf_op jit(solution)/shard_map/ppermute | solution.py:411
  13.4 13.4 %collective-permute-start.2 = (bf16[2,4,16,768]{3,2,1,0:T(8,128)(2,1)S(1)}, bf16[2,4,16,768]{3,2,1,0:T(8,128)(2,1)S(1)}, u32[]{:S(2)}, u32[]{:S(2)}) collective-permute-start(bf16[2,4,16,768]{3,2,1,0:T(8,128)(2,1)S(1)} %get-tuple-element.52), channel_id=1, source_target_pairs={{0,4},{1,5},{2,6},{3,7},{4,0},{5,1},{6,2},{7,3},{8,12},{9,13},{10,... | collective-permute-start | bytes 589832 | tf_op jit(solution)/shard_map/ppermute | solution.py:411
  13.7 24.6 %copy-start.1 = (bf16[768,2304]{1,0:T(8,128)(2,1)S(1)}, bf16[768,2304]{1,0:T(8,128)(2,1)}, u32[]{:S(2)}) copy-start(bf16[768,2304]{1,0:T(8,128)(2,1)} %refs_4_.5) | copy-start | bytes 10616836
  19.1 9.4 %collective-permute-start.6 = (bf16[2,4,16,768]{3,2,1,0:T(8,128)(2,1)S(1)}, bf16[2,4,16,768]{3,2,1,0:T(8,128)(2,1)S(1)}, u32[]{:S(2)}, u32[]{:S(2)}) collective-permute-start(bf16[2,4,16,768]{3,2,1,0:T(8,128)(2,1)S(1)} %get-tuple-element.58), channel_id=1, source_target_pairs={{0,2},{1,3},{2,0},{3,1},{4,6},{5,7},{6,4},{7,5},{8,10},{9,11},{10,... | collective-permute-start | bytes 589832 | tf_op jit(solution)/shard_map/ppermute | solution.py:411
  20.7 8.4 %collective-permute-start.7 = (bf16[2,4,16,768]{3,2,1,0:T(8,128)(2,1)S(1)}, bf16[2,4,16,768]{3,2,1,0:T(8,128)(2,1)S(1)}, u32[]{:S(2)}, u32[]{:S(2)}) collective-permute-start(bf16[2,4,16,768]{3,2,1,0:T(8,128)(2,1)S(1)} %get-tuple-element.59), channel_id=1, source_target_pairs={{0,3},{1,2},{2,1},{3,0},{4,7},{5,6},{6,5},{7,4},{8,11},{9,10},{10,... | collective-permute-start | bytes 589832 | tf_op jit(solution)/shard_map/ppermute | solution.py:411
  26.3 2.8 %collective-permute-start.8 = (bf16[2,4,16,768]{3,2,1,0:T(8,128)(2,1)S(1)}, bf16[2,4,16,768]{3,2,1,0:T(8,128)(2,1)S(1)}, u32[]{:S(2)}, u32[]{:S(2)}) collective-permute-start(bf16[2,4,16,768]{3,2,1,0:T(8,128)(2,1)S(1)} %get-tuple-element.60), channel_id=1, source_target_pairs={{0,1},{1,0},{2,3},{3,2},{4,5},{5,4},{6,7},{7,6},{8,9},{9,8},{10,11... | collective-permute-start | bytes 589832 | tf_op jit(solution)/shard_map/ppermute | solution.py:411
  26.8 8.3 %collective-permute-start.3 = (bf16[4,2,16,768]{3,2,1,0:T(8,128)(2,1)S(1)}, bf16[4,2,16,768]{3,2,1,0:T(8,128)(2,1)S(1)}, u32[]{:S(2)}, u32[]{:S(2)}) collective-permute-start(bf16[4,2,16,768]{3,2,1,0:T(8,128)(2,1)S(1)} %get-tuple-element.54), channel_id=1, source_target_pairs={{0,2},{1,3},{2,0},{3,1},{4,6},{5,7},{6,4},{7,5},{8,10},{9,11},{10,... | collective-permute-start | bytes 589832 | tf_op jit(solution)/shard_map/ppermute | solution.py:411
  28.5 9.8 %collective-permute-start.4 = (bf16[4,2,16,768]{3,2,1,0:T(8,128)(2,1)S(1)}, bf16[4,2,16,768]{3,2,1,0:T(8,128)(2,1)S(1)}, u32[]{:S(2)}, u32[]{:S(2)}) collective-permute-start(bf16[4,2,16,768]{3,2,1,0:T(8,128)(2,1)S(1)} %get-tuple-element.55), channel_id=1, source_target_pairs={{0,3},{1,2},{2,1},{3,0},{4,7},{5,6},{6,5},{7,4},{8,11},{9,10},{10,... | collective-permute-start | bytes 589832 | tf_op jit(solution)/shard_map/ppermute | solution.py:411
  28.5 9.8 %collective-permute-start.5 = (bf16[4,2,16,768]{3,2,1,0:T(8,128)(2,1)S(1)}, bf16[4,2,16,768]{3,2,1,0:T(8,128)(2,1)S(1)}, u32[]{:S(2)}, u32[]{:S(2)}) collective-permute-start(bf16[4,2,16,768]{3,2,1,0:T(8,128)(2,1)S(1)} %get-tuple-element.56), channel_id=1, source_target_pairs={{0,1},{1,0},{2,3},{3,2},{4,5},{5,4},{6,7},{7,6},{8,9},{9,8},{10,11... | collective-permute-start | bytes 589832 | tf_op jit(solution)/shard_map/ppermute | solution.py:411
  29.1 16.4 %collective-permute-start.9 = (bf16[4,16,768]{2,1,0:T(8,128)(2,1)S(1)}, bf16[4,16,768]{2,1,0:T(8,128)(2,1)S(1)}, u32[]{:S(2)}, u32[]{:S(2)}) collective-permute-start(bf16[4,16,768]{2,1,0:T(8,128)(2,1)S(1)} %get-tuple-element.62), channel_id=1, source_target_pairs={{0,8},{1,9},{2,10},{3,11},{4,12},{5,13},{6,14},{7,15},{8,0},{9,1},... | collective-permute-start | bytes 294920 | tf_op jit(solution)/shard_map/ppermute | solution.py:411
  34.7 11.0 %collective-permute-start.10 = (bf16[4,16,768]{2,1,0:T(8,128)(2,1)S(1)}, bf16[4,16,768]{2,1,0:T(8,128)(2,1)S(1)}, u32[]{:S(2)}, u32[]{:S(2)}) collective-permute-start(bf16[4,16,768]{2,1,0:T(8,128)(2,1)S(1)} %get-tuple-element.63), channel_id=1, source_target_pairs={{0,12},{1,13},{2,14},{3,15},{4,8},{5,9},{6,10},{7,11},{8,4},{9,5},... | collective-permute-start | bytes 294920 | tf_op jit(solution)/shard_map/ppermute | solution.py:411
  35.1 10.6 %collective-permute-start.11 = (bf16[4,16,768]{2,1,0:T(8,128)(2,1)S(1)}, bf16[4,16,768]{2,1,0:T(8,128)(2,1)S(1)}, u32[]{:S(2)}, u32[]{:S(2)}) collective-permute-start(bf16[4,16,768]{2,1,0:T(8,128)(2,1)S(1)} %get-tuple-element.64), channel_id=1, source_target_pairs={{0,4},{1,5},{2,6},{3,7},{4,0},{5,1},{6,2},{7,3},{8,12},{9,13},{10,... | collective-permute-start | bytes 294920 | tf_op jit(solution)/shard_map/ppermute | solution.py:411
  38.3 7.5 %copy-start.4 = (bf16[768,768]{1,0:T(8,128)(2,1)S(1)}, bf16[768,768]{1,0:T(8,128)(2,1)}, u32[]{:S(2)}) copy-start(bf16[768,768]{1,0:T(8,128)(2,1)} %refs_5_.3) | copy-start | bytes 3538948
  40.8 14.9 %collective-permute-start.18 = (bf16[4,16,768]{2,1,0:T(8,128)(2,1)S(1)}, bf16[4,16,768]{2,1,0:T(8,128)(2,1)S(1)}, u32[]{:S(2)}, u32[]{:S(2)}) collective-permute-start(bf16[4,16,768]{2,1,0:T(8,128)(2,1)S(1)} %get-tuple-element.78), channel_id=1, source_target_pairs={{0,8},{1,9},{2,10},{3,11},{4,12},{5,13},{6,14},{7,15},{8,0},{9,1},... | collective-permute-start | bytes 294920 | tf_op jit(solution)/shard_map/ppermute | solution.py:411
  45.1 10.8 %collective-permute-start.19 = (bf16[4,16,768]{2,1,0:T(8,128)(2,1)S(1)}, bf16[4,16,768]{2,1,0:T(8,128)(2,1)S(1)}, u32[]{:S(2)}, u32[]{:S(2)}) collective-permute-start(bf16[4,16,768]{2,1,0:T(8,128)(2,1)S(1)} %get-tuple-element.79), channel_id=1, source_target_pairs={{0,12},{1,13},{2,14},{3,15},{4,8},{5,9},{6,10},{7,11},{8,4},{9,5},... | collective-permute-start | bytes 294920 | tf_op jit(solution)/shard_map/ppermute | solution.py:411
  45.5 10.3 %collective-permute-start.20 = (bf16[4,16,768]{2,1,0:T(8,128)(2,1)S(1)}, bf16[4,16,768]{2,1,0:T(8,128)(2,1)S(1)}, u32[]{:S(2)}, u32[]{:S(2)}) collective-permute-start(bf16[4,16,768]{2,1,0:T(8,128)(2,1)S(1)} %get-tuple-element.80), channel_id=1, source_target_pairs={{0,4},{1,5},{2,6},{3,7},{4,0},{5,1},{6,2},{7,3},{8,12},{9,13},{10,... | collective-permute-start | bytes 294920 | tf_op jit(solution)/shard_map/ppermute | solution.py:411
  51.4 17.6 %collective-permute-start.12 = (bf16[4,32,768]{2,1,0:T(8,128)(2,1)S(1)}, bf16[4,32,768]{2,1,0:T(8,128)(2,1)S(1)}, u32[]{:S(2)}, u32[]{:S(2)}) collective-permute-start(bf16[4,32,768]{2,1,0:T(8,128)(2,1)S(1)} %get-tuple-element.66), channel_id=1, source_target_pairs={{0,8},{1,9},{2,10},{3,11},{4,12},{5,13},{6,14},{7,15},{8,0},{9,1},... | collective-permute-start | bytes 589832 | tf_op jit(solution)/shard_map/ppermute | solution.py:411
  55.2 13.8 %collective-permute-start.13 = (bf16[4,32,768]{2,1,0:T(8,128)(2,1)S(1)}, bf16[4,32,768]{2,1,0:T(8,128)(2,1)S(1)}, u32[]{:S(2)}, u32[]{:S(2)}) collective-permute-start(bf16[4,32,768]{2,1,0:T(8,128)(2,1)S(1)} %get-tuple-element.67), channel_id=1, source_target_pairs={{0,12},{1,13},{2,14},{3,15},{4,8},{5,9},{6,10},{7,11},{8,4},{9,5},... | collective-permute-start | bytes 589832 | tf_op jit(solution)/shard_map/ppermute | solution.py:411
  55.6 14.6 %collective-permute-start.14 = (bf16[4,32,768]{2,1,0:T(8,128)(2,1)S(1)}, bf16[4,32,768]{2,1,0:T(8,128)(2,1)S(1)}, u32[]{:S(2)}, u32[]{:S(2)}) collective-permute-start(bf16[4,32,768]{2,1,0:T(8,128)(2,1)S(1)} %get-tuple-element.68), channel_id=1, source_target_pairs={{0,4},{1,5},{2,6},{3,7},{4,0},{5,1},{6,2},{7,3},{8,12},{9,13},{10,... | collective-permute-start | bytes 589832 | tf_op jit(solution)/shard_map/ppermute | solution.py:411
  61.5 10.4 %collective-permute-start.21 = (bf16[4,32,768]{2,1,0:T(8,128)(2,1)S(1)}, bf16[4,32,768]{2,1,0:T(8,128)(2,1)S(1)}, u32[]{:S(2)}, u32[]{:S(2)}) collective-permute-start(bf16[4,32,768]{2,1,0:T(8,128)(2,1)S(1)} %get-tuple-element.82), channel_id=1, source_target_pairs={{0,2},{1,3},{2,0},{3,1},{4,6},{5,7},{6,4},{7,5},{8,10},{9,11},{10,... | collective-permute-start | bytes 589832 | tf_op jit(solution)/shard_map/ppermute | solution.py:411
  63.1 9.5 %collective-permute-start.22 = (bf16[4,32,768]{2,1,0:T(8,128)(2,1)S(1)}, bf16[4,32,768]{2,1,0:T(8,128)(2,1)S(1)}, u32[]{:S(2)}, u32[]{:S(2)}) collective-permute-start(bf16[4,32,768]{2,1,0:T(8,128)(2,1)S(1)} %get-tuple-element.83), channel_id=1, source_target_pairs={{0,3},{1,2},{2,1},{3,0},{4,7},{5,6},{6,5},{7,4},{8,11},{9,10},{10,... | collective-permute-start | bytes 589832 | tf_op jit(solution)/shard_map/ppermute | solution.py:411
  69.0 3.5 %collective-permute-start.23 = (bf16[4,32,768]{2,1,0:T(8,128)(2,1)S(1)}, bf16[4,32,768]{2,1,0:T(8,128)(2,1)S(1)}, u32[]{:S(2)}, u32[]{:S(2)}) collective-permute-start(bf16[4,32,768]{2,1,0:T(8,128)(2,1)S(1)} %get-tuple-element.84), channel_id=1, source_target_pairs={{0,1},{1,0},{2,3},{3,2},{4,5},{5,4},{6,7},{7,6},{8,9},{9,8},{10,11... | collective-permute-start | bytes 589832 | tf_op jit(solution)/shard_map/ppermute | solution.py:411
  70.3 8.2 %collective-permute-start.15 = (bf16[4,32,768]{2,1,0:T(8,128)(2,1)S(1)}, bf16[4,32,768]{2,1,0:T(8,128)(2,1)S(1)}, u32[]{:S(2)}, u32[]{:S(2)}) collective-permute-start(bf16[4,32,768]{2,1,0:T(8,128)(2,1)S(1)} %get-tuple-element.70), channel_id=1, source_target_pairs={{0,2},{1,3},{2,0},{3,1},{4,6},{5,7},{6,4},{7,5},{8,10},{9,11},{10,... | collective-permute-start | bytes 589832 | tf_op jit(solution)/shard_map/ppermute | solution.py:411
  71.9 9.7 %collective-permute-start.16 = (bf16[4,32,768]{2,1,0:T(8,128)(2,1)S(1)}, bf16[4,32,768]{2,1,0:T(8,128)(2,1)S(1)}, u32[]{:S(2)}, u32[]{:S(2)}) collective-permute-start(bf16[4,32,768]{2,1,0:T(8,128)(2,1)S(1)} %get-tuple-element.71), channel_id=1, source_target_pairs={{0,3},{1,2},{2,1},{3,0},{4,7},{5,6},{6,5},{7,4},{8,11},{9,10},{10,... | collective-permute-start | bytes 589832 | tf_op jit(solution)/shard_map/ppermute | solution.py:411
  71.9 9.7 %collective-permute-start.17 = (bf16[4,32,768]{2,1,0:T(8,128)(2,1)S(1)}, bf16[4,32,768]{2,1,0:T(8,128)(2,1)S(1)}, u32[]{:S(2)}, u32[]{:S(2)}) collective-permute-start(bf16[4,32,768]{2,1,0:T(8,128)(2,1)S(1)} %get-tuple-element.72), channel_id=1, source_target_pairs={{0,1},{1,0},{2,3},{3,2},{4,5},{5,4},{6,7},{7,6},{8,9},{9,8},{10,11... | collective-permute-start | bytes 589832 | tf_op jit(solution)/shard_map/ppermute | solution.py:411
  72.6 18.6 %collective-permute-start.24 = (bf16[4,32,768]{2,1,0:T(8,128)(2,1)S(1)}, bf16[4,32,768]{2,1,0:T(8,128)(2,1)S(1)}, u32[]{:S(2)}, u32[]{:S(2)}) collective-permute-start(bf16[4,32,768]{2,1,0:T(8,128)(2,1)S(1)} %get-tuple-element.86), channel_id=1, source_target_pairs={{0,8},{1,9},{2,10},{3,11},{4,12},{5,13},{6,14},{7,15},{8,0},{9,1},... | collective-permute-start | bytes 589832 | tf_op jit(solution)/shard_map/ppermute | solution.py:411
  77.0 14.2 %collective-permute-start.25 = (bf16[4,32,768]{2,1,0:T(8,128)(2,1)S(1)}, bf16[4,32,768]{2,1,0:T(8,128)(2,1)S(1)}, u32[]{:S(2)}, u32[]{:S(2)}) collective-permute-start(bf16[4,32,768]{2,1,0:T(8,128)(2,1)S(1)} %get-tuple-element.87), channel_id=1, source_target_pairs={{0,12},{1,13},{2,14},{3,15},{4,8},{5,9},{6,10},{7,11},{8,4},{9,5},... | collective-permute-start | bytes 589832 | tf_op jit(solution)/shard_map/ppermute | solution.py:411
  78.5 13.7 %collective-permute-start.26 = (bf16[4,32,768]{2,1,0:T(8,128)(2,1)S(1)}, bf16[4,32,768]{2,1,0:T(8,128)(2,1)S(1)}, u32[]{:S(2)}, u32[]{:S(2)}) collective-permute-start(bf16[4,32,768]{2,1,0:T(8,128)(2,1)S(1)} %get-tuple-element.88), channel_id=1, source_target_pairs={{0,4},{1,5},{2,6},{3,7},{4,0},{5,1},{6,2},{7,3},{8,12},{9,13},{10,... | collective-permute-start | bytes 589832 | tf_op jit(solution)/shard_map/ppermute | solution.py:411

commit v6 on v5

--- a/solution.py
+++ b/solution.py
@@ -20,7 +20,7 @@
 SMEM = pl.BlockSpec(memory_space=pltpu.SMEM)
 HBM = pl.BlockSpec(memory_space=pltpu.HBM)
 
-OUTER = (0, 8, 12, 4)
+OUTER = (0, 12, 8, 4)
 INNER = (0, 2, 3, 1)
 
 

time: 94.3 us -> 93.7 us (level)
  starting transfers between devices: 40.8 us -> 28.2 us
  waiting for transfers between devices: 23.9 us -> 36.2 us
    ppermute x27, starting transfers between devices: 40.8 us -> 28.2 us  [exchange(): lax.ppermute(piece, 'wide', [(w, w ^ mask) for w in range(size)])]
    ppermute x27, waiting for transfers between devices: 23.9 us -> 36.2 us  [exchange(): lax.ppermute(piece, 'wide', [(w, w ^ mask) for w in range(size)])]
  transfers between devices with their start and end apart: 27 -> 27, of which waited for: 6 -> 8; matrix products, arithmetic and copies ran while one was open for 0% -> 0% of each run, Pallas kernels for 21% -> 21%
where the time goes in v6:
time: 93.7 us; the launch traced here: 93.6 us
  waiting for transfers between devices  36.2 us (39%)
  Pallas kernels  29.1 us (31%)
  starting transfers between devices  28.2 us (30%)
    ppermute x27, waiting for transfers between devices, exchange(): lax.ppermute(piece, 'wide', [(w, w ^ mask) for w in range(size)])  36.2 us
    ppermute x27, starting transfers between devices, exchange(): lax.ppermute(piece, 'wide', [(w, w ^ mask) for w in range(size)])  28.2 us
    pallas_call x2, Pallas kernels, spatial(): pl.pallas_call(functools.partial(spatial_kernel, outer_first, begin, fetc...  13.4 us
    pallas_call x2, Pallas kernels, temporal(): pl.pallas_call(functools.partial(temporal_kernel, half, outer_first), in_...  11.3 us
    pallas_call x1, Pallas kernels, project_early(): pl.pallas_call(project_kernel, in_specs=[VMEM] * 5, out_specs=VMEM, out_s...  2.47 us
  transfers between devices with their start and end apart: 27, of which 8 were waited for; matrix products, arithmetic and copies ran while one was open for 0% of the time, Pallas kernels for 21%

profile of v6, /device:TPU:0, one launch (start us, length us, event | category | flops | bytes accessed | tf_op | source)
XLA Modules:
  0.0 93.6 jit_solution(912003789315079771)
XLA Ops:
  0.0 8.0 %spatial_outer.1 = (bf16[2,256,768]{2,1,0:T(8,128)(2,1)S(1)}, bf16[2,4,16,768]{3,2,1,0:T(8,128)(2,1)S(1)}, bf16[2,4,16,768]{3,2,1,0:T(8,128)(2,1)S(1)}, bf16[2,4...) custom-call(s32[1]{0:T(128)} %bitcast.me, bf16[4,256,768]{2,1,0:T(8,128)(2,1)} %x_in.3, bf16[768,2304]{1,0:T(8,128)(2,1)} %wqkv_in.3, ...), custom_call_target="tpu_custom_call" | custom-call | flops 4026531840 | bytes 4718592 | tf_op jit(solution)/shard_map/spatial_outer/pallas_call | solution.py:185
  8.0 5.1 %collective-permute-start = (bf16[2,4,16,768]{3,2,1,0:T(8,128)(2,1)S(1)}, bf16[2,4,16,768]{3,2,1,0:T(8,128)(2,1)S(1)}, u32[]{:S(2)}, u32[]{:S(2)}) collective-permute-start(bf16[2,4,16,768]{3,2,1,0:T(8,128)(2,1)S(1)} %get-tuple-element.50), channel_id=1, source_target_pairs={{0,12},{1,13},{2,14},{3,15},{4,8},{5,9},{6,10},{7,11},{8,4},{9,5},... | collective-permute-start | bytes 589832 | tf_op jit(solution)/shard_map/ppermute | solution.py:411
  13.1 0.6 collective-permute-start.2
  13.8 5.4 %spatial_inner.1 = (bf16[2,256,768]{2,1,0:T(8,128)(2,1)S(1)}, bf16[2,4,16,768]{3,2,1,0:T(8,128)(2,1)S(1)}, bf16[2,4,16,768]{3,2,1,0:T(8,128)(2,1)S(1)}, bf16[2,4...) custom-call(s32[1]{0:T(128)} %bitcast.me, bf16[4,256,768]{2,1,0:T(8,128)(2,1)S(1)} %copy-done.2, ...), custom_call_target="tpu_custom_call" | custom-call | flops 4026531840 | bytes 4718592 | tf_op jit(solution)/shard_map/spatial_inner/pallas_call | solution.py:185
  19.2 1.7 %collective-permute-start.6 = (bf16[2,4,16,768]{3,2,1,0:T(8,128)(2,1)S(1)}, bf16[2,4,16,768]{3,2,1,0:T(8,128)(2,1)S(1)}, u32[]{:S(2)}, u32[]{:S(2)}) collective-permute-start(bf16[2,4,16,768]{3,2,1,0:T(8,128)(2,1)S(1)} %get-tuple-element.58), channel_id=1, source_target_pairs={{0,2},{1,3},{2,0},{3,1},{4,6},{5,7},{6,4},{7,5},{8,10},{9,11},{10,... | collective-permute-start | bytes 589832 | tf_op jit(solution)/shard_map/ppermute | solution.py:411
  20.9 0.5 collective-permute-start.8
  21.4 8.4 %collective-permute-done.1.refs_2_ = bf16[2,4,16,768]{3,2,1,0:T(8,128)(2,1)S(1)} collective-permute-done((bf16[2,4,16,768]{3,2,1,0:T(8,128)(2,1)S(1)}, bf16[2,4,16,768]{3,2,1,0:T(8,128)(2,1)S(1)}, u32[]{:S(2)}, u32[]{:S(2)}) %collective-permute-start.1) | collective-permute-done | bytes 196640 | tf_op jit(solution)/shard_map/ppermute | solution.py:411
  29.8 1.6 %collective-permute-start.3 = (bf16[4,2,16,768]{3,2,1,0:T(8,128)(2,1)S(1)}, bf16[4,2,16,768]{3,2,1,0:T(8,128)(2,1)S(1)}, u32[]{:S(2)}, u32[]{:S(2)}) collective-permute-start(bf16[4,2,16,768]{3,2,1,0:T(8,128)(2,1)S(1)} %get-tuple-element.54), channel_id=1, source_target_pairs={{0,2},{1,3},{2,0},{3,1},{4,6},{5,7},{6,4},{7,5},{8,10},{9,11},{10,... | collective-permute-start | bytes 589832 | tf_op jit(solution)/shard_map/ppermute | solution.py:411
  31.4 0.6 collective-permute-start.5
  32.1 2.5 %collective-permute-start.9 = (bf16[4,16,768]{2,1,0:T(8,128)(2,1)S(1)}, bf16[4,16,768]{2,1,0:T(8,128)(2,1)S(1)}, u32[]{:S(2)}, u32[]{:S(2)}) collective-permute-start(bf16[4,16,768]{2,1,0:T(8,128)(2,1)S(1)} %get-tuple-element.62), channel_id=1, source_target_pairs={{0,12},{1,13},{2,14},{3,15},{4,8},{5,9},{6,10},{7,11},{8,4},{9,5},... | collective-permute-start | bytes 294920 | tf_op jit(solution)/shard_map/ppermute | solution.py:411
  34.7 2.7 %collective-permute-done.3.refs_1_ = bf16[4,2,16,768]{3,2,1,0:T(8,128)(2,1)S(1)} collective-permute-done((bf16[4,2,16,768]{3,2,1,0:T(8,128)(2,1)S(1)}, bf16[4,2,16,768]{3,2,1,0:T(8,128)(2,1)S(1)}, u32[]{:S(2)}, u32[]{:S(2)}) %collective-permute-start.3) | collective-permute-done | bytes 196640 | tf_op jit(solution)/shard_map/ppermute | solution.py:411
  37.3 1.8 %collective-permute-done.4.refs_2_ = bf16[4,2,16,768]{3,2,1,0:T(8,128)(2,1)S(1)} collective-permute-done((bf16[4,2,16,768]{3,2,1,0:T(8,128)(2,1)S(1)}, bf16[4,2,16,768]{3,2,1,0:T(8,128)(2,1)S(1)}, u32[]{:S(2)}, u32[]{:S(2)}) %collective-permute-start.4) | collective-permute-done | bytes 196640 | tf_op jit(solution)/shard_map/ppermute | solution.py:411
  39.1 2.5 %project_early.1.early = bf16[512,2304]{1,0:T(8,128)(2,1)S(1)} custom-call(bf16[4,2,16,768]{3,2,1,0:T(8,128)(2,1)S(1)} %get-tuple-element.53.refs_0_, bf16[4,2,16,768]{3,2,1,0:T(8,128)(2,1)S(1)} %collective-permute-done.3.refs_1_, bf16[4,2,16,768]{3,2,1,0:T(8,128)(2,1)S(1)} %collective-permute-done.4.refs_2_, ...), custom_call_target="tpu_custom_call" | custom-call | flops 1811939328 | bytes 3538944 | tf_op jit(solution)/shard_map/project_early/pallas_call | solution.py:280
  41.6 2.4 %collective-permute-start.18 = (bf16[4,16,768]{2,1,0:T(8,128)(2,1)S(1)}, bf16[4,16,768]{2,1,0:T(8,128)(2,1)S(1)}, u32[]{:S(2)}, u32[]{:S(2)}) collective-permute-start(bf16[4,16,768]{2,1,0:T(8,128)(2,1)S(1)} %get-tuple-element.78), channel_id=1, source_target_pairs={{0,12},{1,13},{2,14},{3,15},{4,8},{5,9},{6,10},{7,11},{8,4},{9,5},... | collective-permute-start | bytes 294920 | tf_op jit(solution)/shard_map/ppermute | solution.py:411
  44.0 2.1 %collective-permute-start.20 = (bf16[4,16,768]{2,1,0:T(8,128)(2,1)S(1)}, bf16[4,16,768]{2,1,0:T(8,128)(2,1)S(1)}, u32[]{:S(2)}, u32[]{:S(2)}) collective-permute-start(bf16[4,16,768]{2,1,0:T(8,128)(2,1)S(1)} %get-tuple-element.80), channel_id=1, source_target_pairs={{0,4},{1,5},{2,6},{3,7},{4,0},{5,1},{6,2},{7,3},{8,12},{9,13},{10,... | collective-permute-start | bytes 294920 | tf_op jit(solution)/shard_map/ppermute | solution.py:411
  46.1 5.6 %temporal.2 = (bf16[4,32,768]{2,1,0:T(8,128)(2,1)S(1)}, bf16[4,32,768]{2,1,0:T(8,128)(2,1)S(1)}, bf16[4,32,768]{2,1,0:T(8,128)(2,1)S(1)}, bf16[4,32,768]{2,1,0:T(8,128)(2,1)S(1)}) custom-call(s32[1]{0:T(128)} %bitcast.me, bf16[512,2304]{1,0:T(8,128)(2,1)S(1)} %project_early.1.early, bf16[4,16,768]{2,1,0:T(8,128)(2,1)S(1)} %get-tuple-element.61.refs_0_, ...), custom_call_target="tpu_custom_call" | custom-call | flops 3120562176 | bytes 4718592 | tf_op jit(solution)/shard_map/temporal/pallas_call | solution.py:342
  51.7 2.4 %collective-permute-start.12 = (bf16[4,32,768]{2,1,0:T(8,128)(2,1)S(1)}, bf16[4,32,768]{2,1,0:T(8,128)(2,1)S(1)}, u32[]{:S(2)}, u32[]{:S(2)}) collective-permute-start(bf16[4,32,768]{2,1,0:T(8,128)(2,1)S(1)} %get-tuple-element.66), channel_id=1, source_target_pairs={{0,12},{1,13},{2,14},{3,15},{4,8},{5,9},{6,10},{7,11},{8,4},{9,5},... | collective-permute-start | bytes 589832 | tf_op jit(solution)/shard_map/ppermute | solution.py:411
  54.1 2.1 %collective-permute-start.14 = (bf16[4,32,768]{2,1,0:T(8,128)(2,1)S(1)}, bf16[4,32,768]{2,1,0:T(8,128)(2,1)S(1)}, u32[]{:S(2)}, u32[]{:S(2)}) collective-permute-start(bf16[4,32,768]{2,1,0:T(8,128)(2,1)S(1)} %get-tuple-element.68), channel_id=1, source_target_pairs={{0,4},{1,5},{2,6},{3,7},{4,0},{5,1},{6,2},{7,3},{8,12},{9,13},{10,... | collective-permute-start | bytes 589832 | tf_op jit(solution)/shard_map/ppermute | solution.py:411
  56.2 5.6 %temporal.3 = (bf16[4,32,768]{2,1,0:T(8,128)(2,1)S(1)}, bf16[4,32,768]{2,1,0:T(8,128)(2,1)S(1)}, bf16[4,32,768]{2,1,0:T(8,128)(2,1)S(1)}, bf16[4,32,768]{2,1,0:T(8,128)(2,1)S(1)}) custom-call(s32[1]{0:T(128)} %bitcast.me, bf16[512,2304]{1,0:T(8,128)(2,1)S(1)} %project_early.1.early, bf16[4,16,768]{2,1,0:T(8,128)(2,1)S(1)} %get-tuple-element.77.refs_0_, ...), custom_call_target="tpu_custom_call" | custom-call | flops 3120562176 | bytes 4718592 | tf_op jit(solution)/shard_map/temporal/pallas_call | solution.py:342
  61.8 0.7 collective-permute-start.21
  62.5 0.2 collective-permute-start.22
  62.6 1.4 %collective-permute-start.23 = (bf16[4,32,768]{2,1,0:T(8,128)(2,1)S(1)}, bf16[4,32,768]{2,1,0:T(8,128)(2,1)S(1)}, u32[]{:S(2)}, u32[]{:S(2)}) collective-permute-start(bf16[4,32,768]{2,1,0:T(8,128)(2,1)S(1)} %get-tuple-element.84), channel_id=1, source_target_pairs={{0,1},{1,0},{2,3},{3,2},{4,5},{5,4},{6,7},{7,6},{8,9},{9,8},{10,11... | collective-permute-start | bytes 589832 | tf_op jit(solution)/shard_map/ppermute | solution.py:411
  64.0 7.2 %collective-permute-done.13.refs_2_ = bf16[4,32,768]{2,1,0:T(8,128)(2,1)S(1)} collective-permute-done((bf16[4,32,768]{2,1,0:T(8,128)(2,1)S(1)}, bf16[4,32,768]{2,1,0:T(8,128)(2,1)S(1)}, u32[]{:S(2)}, u32[]{:S(2)}) %collective-permute-start.13) | collective-permute-done | bytes 196640 | tf_op jit(solution)/shard_map/ppermute | solution.py:411
  71.3 1.6 %collective-permute-start.15 = (bf16[4,32,768]{2,1,0:T(8,128)(2,1)S(1)}, bf16[4,32,768]{2,1,0:T(8,128)(2,1)S(1)}, u32[]{:S(2)}, u32[]{:S(2)}) collective-permute-start(bf16[4,32,768]{2,1,0:T(8,128)(2,1)S(1)} %get-tuple-element.70), channel_id=1, source_target_pairs={{0,2},{1,3},{2,0},{3,1},{4,6},{5,7},{6,4},{7,5},{8,10},{9,11},{10,... | collective-permute-start | bytes 589832 | tf_op jit(solution)/shard_map/ppermute | solution.py:411
  72.8 0.6 collective-permute-start.17
  73.5 0.1 regroup.5
  73.5 2.1 %collective-permute-start.24 = (bf16[4,32,768]{2,1,0:T(8,128)(2,1)S(1)}, bf16[4,32,768]{2,1,0:T(8,128)(2,1)S(1)}, u32[]{:S(2)}, u32[]{:S(2)}) collective-permute-start(bf16[4,32,768]{2,1,0:T(8,128)(2,1)S(1)} %get-tuple-element.86), channel_id=1, source_target_pairs={{0,12},{1,13},{2,14},{3,15},{4,8},{5,9},{6,10},{7,11},{8,4},{9,5},... | collective-permute-start | bytes 589832 | tf_op jit(solution)/shard_map/ppermute | solution.py:411
  75.7 3.5 %collective-permute-done.15.refs_1_ = bf16[4,32,768]{2,1,0:T(8,128)(2,1)S(1)} collective-permute-done((bf16[4,32,768]{2,1,0:T(8,128)(2,1)S(1)}, bf16[4,32,768]{2,1,0:T(8,128)(2,1)S(1)}, u32[]{:S(2)}, u32[]{:S(2)}) %collective-permute-start.15) | collective-permute-done | bytes 196640 | tf_op jit(solution)/shard_map/ppermute | solution.py:411
  79.1 2.1 %collective-permute-done.16.refs_2_ = bf16[4,32,768]{2,1,0:T(8,128)(2,1)S(1)} collective-permute-done((bf16[4,32,768]{2,1,0:T(8,128)(2,1)S(1)}, bf16[4,32,768]{2,1,0:T(8,128)(2,1)S(1)}, u32[]{:S(2)}, u32[]{:S(2)}) %collective-permute-start.16) | collective-permute-done | bytes 196640 | tf_op jit(solution)/shard_map/ppermute | solution.py:411
  81.3 2.0 %collective-permute-done.24.refs_5_ = bf16[4,32,768]{2,1,0:T(8,128)(2,1)S(1)} collective-permute-done((bf16[4,32,768]{2,1,0:T(8,128)(2,1)S(1)}, bf16[4,32,768]{2,1,0:T(8,128)(2,1)S(1)}, u32[]{:S(2)}, u32[]{:S(2)}) %collective-permute-start.24) | collective-permute-done | bytes 196640 | tf_op jit(solution)/shard_map/ppermute | solution.py:411
  83.3 8.4 %collective-permute-done.25.refs_6_ = bf16[4,32,768]{2,1,0:T(8,128)(2,1)S(1)} collective-permute-done((bf16[4,32,768]{2,1,0:T(8,128)(2,1)S(1)}, bf16[4,32,768]{2,1,0:T(8,128)(2,1)S(1)}, u32[]{:S(2)}, u32[]{:S(2)}) %collective-permute-start.25) | collective-permute-done | bytes 196640 | tf_op jit(solution)/shard_map/ppermute | solution.py:411
  91.8 1.8 %last.1 = bf16[4,256,768]{2,1,0:T(8,128)(2,1)} custom-call(s32[1]{0:T(128)} %bitcast.me, bf16[2,256,768]{2,1,0:T(8,128)(2,1)S(1)} %get-tuple-element.47.mid01, bf16[2,256,768]{2,1,0:T(8,128)(2,1)S(1)} %get-tuple-element.48.mid23, bf16[4,32,768]{2,1,0:T(8,128)(2,1)S(1)} %get-tuple-element.69.refs_0_, bf16[4,32,768]{2,1,0:T(8,128)(2,1)S(1)} %collective-permute-done.15.refs_1_, ...), custom_call_target="tpu_custom_call" | custom-call | flops 786432 | bytes 1572864 | tf_op jit(solution)/shard_map/last/pallas_call | solution.py:390
  (42 shorter events, 0.2 us)
Async XLA Ops:
  0.0 13.7 %copy-start = (bf16[768,2304]{1,0:T(8,128)(2,1)S(1)}, bf16[768,2304]{1,0:T(8,128)(2,1)}, u32[]{:S(2)}) copy-start(bf16[768,2304]{1,0:T(8,128)(2,1)} %wqkv_in.3) | copy-start | bytes 10616836
  0.0 13.7 %copy-start.2 = (bf16[4,256,768]{2,1,0:T(8,128)(2,1)S(1)}, bf16[4,256,768]{2,1,0:T(8,128)(2,1)}, u32[]{:S(2)}) copy-start(bf16[4,256,768]{2,1,0:T(8,128)(2,1)} %x_in.3) | copy-start | bytes 4718596
  0.0 13.7 %copy-start.3 = (bf16[768,768]{1,0:T(8,128)(2,1)S(1)}, bf16[768,768]{1,0:T(8,128)(2,1)}, u32[]{:S(2)}) copy-start(bf16[768,768]{1,0:T(8,128)(2,1)} %wo_in.3) | copy-start | bytes 3538948
  8.0 12.9 %collective-permute-start = (bf16[2,4,16,768]{3,2,1,0:T(8,128)(2,1)S(1)}, bf16[2,4,16,768]{3,2,1,0:T(8,128)(2,1)S(1)}, u32[]{:S(2)}, u32[]{:S(2)}) collective-permute-start(bf16[2,4,16,768]{3,2,1,0:T(8,128)(2,1)S(1)} %get-tuple-element.50), channel_id=1, source_target_pairs={{0,12},{1,13},{2,14},{3,15},{4,8},{5,9},{6,10},{7,11},{8,4},{9,5},... | collective-permute-start | bytes 589832 | tf_op jit(solution)/shard_map/ppermute | solution.py:411
  13.1 16.7 %collective-permute-start.1 = (bf16[2,4,16,768]{3,2,1,0:T(8,128)(2,1)S(1)}, bf16[2,4,16,768]{3,2,1,0:T(8,128)(2,1)S(1)}, u32[]{:S(2)}, u32[]{:S(2)}) collective-permute-start(bf16[2,4,16,768]{3,2,1,0:T(8,128)(2,1)S(1)} %get-tuple-element.51), channel_id=1, source_target_pairs={{0,8},{1,9},{2,10},{3,11},{4,12},{5,13},{6,14},{7,15},{8,0},{9,1},... | collective-permute-start | bytes 589832 | tf_op jit(solution)/shard_map/ppermute | solution.py:411
  13.1 16.7 %collective-permute-start.2 = (bf16[2,4,16,768]{3,2,1,0:T(8,128)(2,1)S(1)}, bf16[2,4,16,768]{3,2,1,0:T(8,128)(2,1)S(1)}, u32[]{:S(2)}, u32[]{:S(2)}) collective-permute-start(bf16[2,4,16,768]{3,2,1,0:T(8,128)(2,1)S(1)} %get-tuple-element.52), channel_id=1, source_target_pairs={{0,4},{1,5},{2,6},{3,7},{4,0},{5,1},{6,2},{7,3},{8,12},{9,13},{10,... | collective-permute-start | bytes 589832 | tf_op jit(solution)/shard_map/ppermute | solution.py:411
  13.7 25.4 %copy-start.1 = (bf16[768,2304]{1,0:T(8,128)(2,1)S(1)}, bf16[768,2304]{1,0:T(8,128)(2,1)}, u32[]{:S(2)}) copy-start(bf16[768,2304]{1,0:T(8,128)(2,1)} %refs_4_.5) | copy-start | bytes 10616836
  19.2 12.3 %collective-permute-start.6 = (bf16[2,4,16,768]{3,2,1,0:T(8,128)(2,1)S(1)}, bf16[2,4,16,768]{3,2,1,0:T(8,128)(2,1)S(1)}, u32[]{:S(2)}, u32[]{:S(2)}) collective-permute-start(bf16[2,4,16,768]{3,2,1,0:T(8,128)(2,1)S(1)} %get-tuple-element.58), channel_id=1, source_target_pairs={{0,2},{1,3},{2,0},{3,1},{4,6},{5,7},{6,4},{7,5},{8,10},{9,11},{10,... | collective-permute-start | bytes 589832 | tf_op jit(solution)/shard_map/ppermute | solution.py:411
  20.9 11.2 %collective-permute-start.7 = (bf16[2,4,16,768]{3,2,1,0:T(8,128)(2,1)S(1)}, bf16[2,4,16,768]{3,2,1,0:T(8,128)(2,1)S(1)}, u32[]{:S(2)}, u32[]{:S(2)}) collective-permute-start(bf16[2,4,16,768]{3,2,1,0:T(8,128)(2,1)S(1)} %get-tuple-element.59), channel_id=1, source_target_pairs={{0,3},{1,2},{2,1},{3,0},{4,7},{5,6},{6,5},{7,4},{8,11},{9,10},{10,... | collective-permute-start | bytes 589832 | tf_op jit(solution)/shard_map/ppermute | solution.py:411
  20.9 11.2 %collective-permute-start.8 = (bf16[2,4,16,768]{3,2,1,0:T(8,128)(2,1)S(1)}, bf16[2,4,16,768]{3,2,1,0:T(8,128)(2,1)S(1)}, u32[]{:S(2)}, u32[]{:S(2)}) collective-permute-start(bf16[2,4,16,768]{3,2,1,0:T(8,128)(2,1)S(1)} %get-tuple-element.60), channel_id=1, source_target_pairs={{0,1},{1,0},{2,3},{3,2},{4,5},{5,4},{6,7},{7,6},{8,9},{9,8},{10,11... | collective-permute-start | bytes 589832 | tf_op jit(solution)/shard_map/ppermute | solution.py:411
  29.8 7.5 %collective-permute-start.3 = (bf16[4,2,16,768]{3,2,1,0:T(8,128)(2,1)S(1)}, bf16[4,2,16,768]{3,2,1,0:T(8,128)(2,1)S(1)}, u32[]{:S(2)}, u32[]{:S(2)}) collective-permute-start(bf16[4,2,16,768]{3,2,1,0:T(8,128)(2,1)S(1)} %get-tuple-element.54), channel_id=1, source_target_pairs={{0,2},{1,3},{2,0},{3,1},{4,6},{5,7},{6,4},{7,5},{8,10},{9,11},{10,... | collective-permute-start | bytes 589832 | tf_op jit(solution)/shard_map/ppermute | solution.py:411
  31.4 7.7 %collective-permute-start.4 = (bf16[4,2,16,768]{3,2,1,0:T(8,128)(2,1)S(1)}, bf16[4,2,16,768]{3,2,1,0:T(8,128)(2,1)S(1)}, u32[]{:S(2)}, u32[]{:S(2)}) collective-permute-start(bf16[4,2,16,768]{3,2,1,0:T(8,128)(2,1)S(1)} %get-tuple-element.55), channel_id=1, source_target_pairs={{0,3},{1,2},{2,1},{3,0},{4,7},{5,6},{6,5},{7,4},{8,11},{9,10},{10,... | collective-permute-start | bytes 589832 | tf_op jit(solution)/shard_map/ppermute | solution.py:411
  31.4 7.7 %collective-permute-start.5 = (bf16[4,2,16,768]{3,2,1,0:T(8,128)(2,1)S(1)}, bf16[4,2,16,768]{3,2,1,0:T(8,128)(2,1)S(1)}, u32[]{:S(2)}, u32[]{:S(2)}) collective-permute-start(bf16[4,2,16,768]{3,2,1,0:T(8,128)(2,1)S(1)} %get-tuple-element.56), channel_id=1, source_target_pairs={{0,1},{1,0},{2,3},{3,2},{4,5},{5,4},{6,7},{7,6},{8,9},{9,8},{10,11... | collective-permute-start | bytes 589832 | tf_op jit(solution)/shard_map/ppermute | solution.py:411
  32.1 11.8 %collective-permute-start.9 = (bf16[4,16,768]{2,1,0:T(8,128)(2,1)S(1)}, bf16[4,16,768]{2,1,0:T(8,128)(2,1)S(1)}, u32[]{:S(2)}, u32[]{:S(2)}) collective-permute-start(bf16[4,16,768]{2,1,0:T(8,128)(2,1)S(1)} %get-tuple-element.62), channel_id=1, source_target_pairs={{0,12},{1,13},{2,14},{3,15},{4,8},{5,9},{6,10},{7,11},{8,4},{9,5},... | collective-permute-start | bytes 294920 | tf_op jit(solution)/shard_map/ppermute | solution.py:411
  34.7 11.4 %collective-permute-start.10 = (bf16[4,16,768]{2,1,0:T(8,128)(2,1)S(1)}, bf16[4,16,768]{2,1,0:T(8,128)(2,1)S(1)}, u32[]{:S(2)}, u32[]{:S(2)}) collective-permute-start(bf16[4,16,768]{2,1,0:T(8,128)(2,1)S(1)} %get-tuple-element.63), channel_id=1, source_target_pairs={{0,8},{1,9},{2,10},{3,11},{4,12},{5,13},{6,14},{7,15},{8,0},{9,1},... | collective-permute-start | bytes 294920 | tf_op jit(solution)/shard_map/ppermute | solution.py:411
  37.3 8.7 %collective-permute-start.11 = (bf16[4,16,768]{2,1,0:T(8,128)(2,1)S(1)}, bf16[4,16,768]{2,1,0:T(8,128)(2,1)S(1)}, u32[]{:S(2)}, u32[]{:S(2)}) collective-permute-start(bf16[4,16,768]{2,1,0:T(8,128)(2,1)S(1)} %get-tuple-element.64), channel_id=1, source_target_pairs={{0,4},{1,5},{2,6},{3,7},{4,0},{5,1},{6,2},{7,3},{8,12},{9,13},{10,... | collective-permute-start | bytes 294920 | tf_op jit(solution)/shard_map/ppermute | solution.py:411
  39.1 6.9 %copy-start.4 = (bf16[768,768]{1,0:T(8,128)(2,1)S(1)}, bf16[768,768]{1,0:T(8,128)(2,1)}, u32[]{:S(2)}) copy-start(bf16[768,768]{1,0:T(8,128)(2,1)} %refs_5_.3) | copy-start | bytes 3538948
  41.6 12.5 %collective-permute-start.18 = (bf16[4,16,768]{2,1,0:T(8,128)(2,1)S(1)}, bf16[4,16,768]{2,1,0:T(8,128)(2,1)S(1)}, u32[]{:S(2)}, u32[]{:S(2)}) collective-permute-start(bf16[4,16,768]{2,1,0:T(8,128)(2,1)S(1)} %get-tuple-element.78), channel_id=1, source_target_pairs={{0,12},{1,13},{2,14},{3,15},{4,8},{5,9},{6,10},{7,11},{8,4},{9,5},... | collective-permute-start | bytes 294920 | tf_op jit(solution)/shard_map/ppermute | solution.py:411
  44.0 12.2 %collective-permute-start.19 = (bf16[4,16,768]{2,1,0:T(8,128)(2,1)S(1)}, bf16[4,16,768]{2,1,0:T(8,128)(2,1)S(1)}, u32[]{:S(2)}, u32[]{:S(2)}) collective-permute-start(bf16[4,16,768]{2,1,0:T(8,128)(2,1)S(1)} %get-tuple-element.79), channel_id=1, source_target_pairs={{0,8},{1,9},{2,10},{3,11},{4,12},{5,13},{6,14},{7,15},{8,0},{9,1},... | collective-permute-start | bytes 294920 | tf_op jit(solution)/shard_map/ppermute | solution.py:411
  44.0 12.2 %collective-permute-start.20 = (bf16[4,16,768]{2,1,0:T(8,128)(2,1)S(1)}, bf16[4,16,768]{2,1,0:T(8,128)(2,1)S(1)}, u32[]{:S(2)}, u32[]{:S(2)}) collective-permute-start(bf16[4,16,768]{2,1,0:T(8,128)(2,1)S(1)} %get-tuple-element.80), channel_id=1, source_target_pairs={{0,4},{1,5},{2,6},{3,7},{4,0},{5,1},{6,2},{7,3},{8,12},{9,13},{10,... | collective-permute-start | bytes 294920 | tf_op jit(solution)/shard_map/ppermute | solution.py:411
  51.7 10.9 %collective-permute-start.12 = (bf16[4,32,768]{2,1,0:T(8,128)(2,1)S(1)}, bf16[4,32,768]{2,1,0:T(8,128)(2,1)S(1)}, u32[]{:S(2)}, u32[]{:S(2)}) collective-permute-start(bf16[4,32,768]{2,1,0:T(8,128)(2,1)S(1)} %get-tuple-element.66), channel_id=1, source_target_pairs={{0,12},{1,13},{2,14},{3,15},{4,8},{5,9},{6,10},{7,11},{8,4},{9,5},... | collective-permute-start | bytes 589832 | tf_op jit(solution)/shard_map/ppermute | solution.py:411
  54.1 17.1 %collective-permute-start.13 = (bf16[4,32,768]{2,1,0:T(8,128)(2,1)S(1)}, bf16[4,32,768]{2,1,0:T(8,128)(2,1)S(1)}, u32[]{:S(2)}, u32[]{:S(2)}) collective-permute-start(bf16[4,32,768]{2,1,0:T(8,128)(2,1)S(1)} %get-tuple-element.67), channel_id=1, source_target_pairs={{0,8},{1,9},{2,10},{3,11},{4,12},{5,13},{6,14},{7,15},{8,0},{9,1},... | collective-permute-start | bytes 589832 | tf_op jit(solution)/shard_map/ppermute | solution.py:411
  54.1 17.1 %collective-permute-start.14 = (bf16[4,32,768]{2,1,0:T(8,128)(2,1)S(1)}, bf16[4,32,768]{2,1,0:T(8,128)(2,1)S(1)}, u32[]{:S(2)}, u32[]{:S(2)}) collective-permute-start(bf16[4,32,768]{2,1,0:T(8,128)(2,1)S(1)} %get-tuple-element.68), channel_id=1, source_target_pairs={{0,4},{1,5},{2,6},{3,7},{4,0},{5,1},{6,2},{7,3},{8,12},{9,13},{10,... | collective-permute-start | bytes 589832 | tf_op jit(solution)/shard_map/ppermute | solution.py:411
  61.8 11.0 %collective-permute-start.21 = (bf16[4,32,768]{2,1,0:T(8,128)(2,1)S(1)}, bf16[4,32,768]{2,1,0:T(8,128)(2,1)S(1)}, u32[]{:S(2)}, u32[]{:S(2)}) collective-permute-start(bf16[4,32,768]{2,1,0:T(8,128)(2,1)S(1)} %get-tuple-element.82), channel_id=1, source_target_pairs={{0,2},{1,3},{2,0},{3,1},{4,6},{5,7},{6,4},{7,5},{8,10},{9,11},{10,... | collective-permute-start | bytes 589832 | tf_op jit(solution)/shard_map/ppermute | solution.py:411
  62.5 11.0 %collective-permute-start.22 = (bf16[4,32,768]{2,1,0:T(8,128)(2,1)S(1)}, bf16[4,32,768]{2,1,0:T(8,128)(2,1)S(1)}, u32[]{:S(2)}, u32[]{:S(2)}) collective-permute-start(bf16[4,32,768]{2,1,0:T(8,128)(2,1)S(1)} %get-tuple-element.83), channel_id=1, source_target_pairs={{0,3},{1,2},{2,1},{3,0},{4,7},{5,6},{6,5},{7,4},{8,11},{9,10},{10,... | collective-permute-start | bytes 589832 | tf_op jit(solution)/shard_map/ppermute | solution.py:411
  62.6 10.8 %collective-permute-start.23 = (bf16[4,32,768]{2,1,0:T(8,128)(2,1)S(1)}, bf16[4,32,768]{2,1,0:T(8,128)(2,1)S(1)}, u32[]{:S(2)}, u32[]{:S(2)}) collective-permute-start(bf16[4,32,768]{2,1,0:T(8,128)(2,1)S(1)} %get-tuple-element.84), channel_id=1, source_target_pairs={{0,1},{1,0},{2,3},{3,2},{4,5},{5,4},{6,7},{7,6},{8,9},{9,8},{10,11... | collective-permute-start | bytes 589832 | tf_op jit(solution)/shard_map/ppermute | solution.py:411
  71.3 7.9 %collective-permute-start.15 = (bf16[4,32,768]{2,1,0:T(8,128)(2,1)S(1)}, bf16[4,32,768]{2,1,0:T(8,128)(2,1)S(1)}, u32[]{:S(2)}, u32[]{:S(2)}) collective-permute-start(bf16[4,32,768]{2,1,0:T(8,128)(2,1)S(1)} %get-tuple-element.70), channel_id=1, source_target_pairs={{0,2},{1,3},{2,0},{3,1},{4,6},{5,7},{6,4},{7,5},{8,10},{9,11},{10,... | collective-permute-start | bytes 589832 | tf_op jit(solution)/shard_map/ppermute | solution.py:411
  72.8 8.4 %collective-permute-start.16 = (bf16[4,32,768]{2,1,0:T(8,128)(2,1)S(1)}, bf16[4,32,768]{2,1,0:T(8,128)(2,1)S(1)}, u32[]{:S(2)}, u32[]{:S(2)}) collective-permute-start(bf16[4,32,768]{2,1,0:T(8,128)(2,1)S(1)} %get-tuple-element.71), channel_id=1, source_target_pairs={{0,3},{1,2},{2,1},{3,0},{4,7},{5,6},{6,5},{7,4},{8,11},{9,10},{10,... | collective-permute-start | bytes 589832 | tf_op jit(solution)/shard_map/ppermute | solution.py:411
  72.8 8.4 %collective-permute-start.17 = (bf16[4,32,768]{2,1,0:T(8,128)(2,1)S(1)}, bf16[4,32,768]{2,1,0:T(8,128)(2,1)S(1)}, u32[]{:S(2)}, u32[]{:S(2)}) collective-permute-start(bf16[4,32,768]{2,1,0:T(8,128)(2,1)S(1)} %get-tuple-element.72), channel_id=1, source_target_pairs={{0,1},{1,0},{2,3},{3,2},{4,5},{5,4},{6,7},{7,6},{8,9},{9,8},{10,11... | collective-permute-start | bytes 589832 | tf_op jit(solution)/shard_map/ppermute | solution.py:411
  73.5 9.8 %collective-permute-start.24 = (bf16[4,32,768]{2,1,0:T(8,128)(2,1)S(1)}, bf16[4,32,768]{2,1,0:T(8,128)(2,1)S(1)}, u32[]{:S(2)}, u32[]{:S(2)}) collective-permute-start(bf16[4,32,768]{2,1,0:T(8,128)(2,1)S(1)} %get-tuple-element.86), channel_id=1, source_target_pairs={{0,12},{1,13},{2,14},{3,15},{4,8},{5,9},{6,10},{7,11},{8,4},{9,5},... | collective-permute-start | bytes 589832 | tf_op jit(solution)/shard_map/ppermute | solution.py:411
  75.7 16.1 %collective-permute-start.25 = (bf16[4,32,768]{2,1,0:T(8,128)(2,1)S(1)}, bf16[4,32,768]{2,1,0:T(8,128)(2,1)S(1)}, u32[]{:S(2)}, u32[]{:S(2)}) collective-permute-start(bf16[4,32,768]{2,1,0:T(8,128)(2,1)S(1)} %get-tuple-element.87), channel_id=1, source_target_pairs={{0,8},{1,9},{2,10},{3,11},{4,12},{5,13},{6,14},{7,15},{8,0},{9,1},... | collective-permute-start | bytes 589832 | tf_op jit(solution)/shard_map/ppermute | solution.py:411
  79.1 12.6 %collective-permute-start.26 = (bf16[4,32,768]{2,1,0:T(8,128)(2,1)S(1)}, bf16[4,32,768]{2,1,0:T(8,128)(2,1)S(1)}, u32[]{:S(2)}, u32[]{:S(2)}) collective-permute-start(bf16[4,32,768]{2,1,0:T(8,128)(2,1)S(1)} %get-tuple-element.88), channel_id=1, source_target_pairs={{0,4},{1,5},{2,6},{3,7},{4,0},{5,1},{6,2},{7,3},{8,12},{9,13},{10,... | collective-permute-start | bytes 589832 | tf_op jit(solution)/shard_map/ppermute | solution.py:411

commit v7 on v6

--- a/solution.py
+++ b/solution.py
@@ -138,23 +138,24 @@
     number = me[0]
     if fetch:
         x, wqkv, wo, sems = held
-        pairs = [(x_in.at[pl.ds(begin, frames)], x)]
+        pairs = [(x_in.at[begin + f], x.at[f]) for f in range(frames)]
         pairs += [(wqkv_in.at[:, pl.ds(j * d, d)], wqkv.at[:, pl.ds(j * d, d)]) for j in range(3)]
         pairs += [(wo_in, wo)]
         copies = [pltpu.make_async_copy(*pair, sems.at[n]) for n, pair in enumerate(pairs)]
         for copy in copies:
             copy.start()
-        copies[0].wait()
     else:
         x, wqkv, wo = x_in.at[pl.ds(begin, frames)], wqkv_in, wo_in
     for f in range(frames):
+        if fetch:
+            copies[f].wait()
         a[f * patches : (f + 1) * patches, :] = normalize(x[f].astype(F32))
     for j in range(3):
         if fetch:
-            copies[1 + j].wait()
+            copies[frames + j].wait()
         project_rows(a, wqkv, qkv, (0,), j)
     if fetch:
-        copies[4].wait()
+        copies[frames + 3].wait()
     attend(qkv, mixed, [slice(f * patches, (f + 1) * patches) for f in range(frames)])
     for f in range(frames):
         r = slice(f * patches, (f + 1) * patches)
@@ -180,7 +181,7 @@
         pltpu.VMEM((frames, patches, d), BF16),
         pltpu.VMEM(wqkv.shape, BF16),
         pltpu.VMEM(wo.shape, BF16),
-        pltpu.SemaphoreType.DMA((5,)),
+        pltpu.SemaphoreType.DMA((frames + 4,)),
     ]
     return pl.pallas_call(
         functools.partial(spatial_kernel, outer_first, begin, fetch),

time: 93.7 us -> 93.7 us (level)
  no operation moved by 1% of the time
where the time goes in v7:
time: 93.7 us; the launch traced here: 93.6 us
  waiting for transfers between devices  36.2 us (39%)
  Pallas kernels  29.1 us (31%)
  starting transfers between devices  28.2 us (30%)
    ppermute x27, waiting for transfers between devices, exchange(): lax.ppermute(piece, 'wide', [(w, w ^ mask) for w in range(size)])  36.2 us
    ppermute x27, starting transfers between devices, exchange(): lax.ppermute(piece, 'wide', [(w, w ^ mask) for w in range(size)])  28.2 us
    pallas_call x2, Pallas kernels, spatial(): pl.pallas_call(functools.partial(spatial_kernel, outer_first, begin, fetc...  13.4 us
    pallas_call x2, Pallas kernels, temporal(): pl.pallas_call(functools.partial(temporal_kernel, half, outer_first), in_...  11.3 us
    pallas_call x1, Pallas kernels, project_early(): pl.pallas_call(project_kernel, in_specs=[VMEM] * 5, out_specs=VMEM, out_s...  2.47 us
  transfers between devices with their start and end apart: 27, of which 8 were waited for; matrix products, arithmetic and copies ran while one was open for 0% of the time, Pallas kernels for 21%

profile of v7, /device:TPU:0, one launch (start us, length us, event | category | flops | bytes accessed | tf_op | source)
XLA Modules:
  0.0 93.6 jit_solution(10864876164307528008)
XLA Ops:
  0.0 7.9 %spatial_outer.1 = (bf16[2,256,768]{2,1,0:T(8,128)(2,1)S(1)}, bf16[2,4,16,768]{3,2,1,0:T(8,128)(2,1)S(1)}, bf16[2,4,16,768]{3,2,1,0:T(8,128)(2,1)S(1)}, bf16[2,4...) custom-call(s32[1]{0:T(128)} %bitcast.me, bf16[4,256,768]{2,1,0:T(8,128)(2,1)} %x_in.3, bf16[768,2304]{1,0:T(8,128)(2,1)} %wqkv_in.3, ...), custom_call_target="tpu_custom_call" | custom-call | flops 4026531840 | bytes 4718592 | tf_op jit(solution)/shard_map/spatial_outer/pallas_call | solution.py:186
  8.0 5.1 %collective-permute-start = (bf16[2,4,16,768]{3,2,1,0:T(8,128)(2,1)S(1)}, bf16[2,4,16,768]{3,2,1,0:T(8,128)(2,1)S(1)}, u32[]{:S(2)}, u32[]{:S(2)}) collective-permute-start(bf16[2,4,16,768]{3,2,1,0:T(8,128)(2,1)S(1)} %get-tuple-element.50), channel_id=1, source_target_pairs={{0,12},{1,13},{2,14},{3,15},{4,8},{5,9},{6,10},{7,11},{8,4},{9,5},... | collective-permute-start | bytes 589832 | tf_op jit(solution)/shard_map/ppermute | solution.py:412
  13.1 0.6 collective-permute-start.2
  13.7 5.4 %spatial_inner.1 = (bf16[2,256,768]{2,1,0:T(8,128)(2,1)S(1)}, bf16[2,4,16,768]{3,2,1,0:T(8,128)(2,1)S(1)}, bf16[2,4,16,768]{3,2,1,0:T(8,128)(2,1)S(1)}, bf16[2,4...) custom-call(s32[1]{0:T(128)} %bitcast.me, bf16[4,256,768]{2,1,0:T(8,128)(2,1)S(1)} %copy-done.2, ...), custom_call_target="tpu_custom_call" | custom-call | flops 4026531840 | bytes 4718592 | tf_op jit(solution)/shard_map/spatial_inner/pallas_call | solution.py:186
  19.1 1.7 %collective-permute-start.6 = (bf16[2,4,16,768]{3,2,1,0:T(8,128)(2,1)S(1)}, bf16[2,4,16,768]{3,2,1,0:T(8,128)(2,1)S(1)}, u32[]{:S(2)}, u32[]{:S(2)}) collective-permute-start(bf16[2,4,16,768]{3,2,1,0:T(8,128)(2,1)S(1)} %get-tuple-element.58), channel_id=1, source_target_pairs={{0,2},{1,3},{2,0},{3,1},{4,6},{5,7},{6,4},{7,5},{8,10},{9,11},{10,... | collective-permute-start | bytes 589832 | tf_op jit(solution)/shard_map/ppermute | solution.py:412
  20.9 0.5 collective-permute-start.8
  21.4 8.4 %collective-permute-done.1.refs_2_ = bf16[2,4,16,768]{3,2,1,0:T(8,128)(2,1)S(1)} collective-permute-done((bf16[2,4,16,768]{3,2,1,0:T(8,128)(2,1)S(1)}, bf16[2,4,16,768]{3,2,1,0:T(8,128)(2,1)S(1)}, u32[]{:S(2)}, u32[]{:S(2)}) %collective-permute-start.1) | collective-permute-done | bytes 196640 | tf_op jit(solution)/shard_map/ppermute | solution.py:412
  29.8 1.6 %collective-permute-start.3 = (bf16[4,2,16,768]{3,2,1,0:T(8,128)(2,1)S(1)}, bf16[4,2,16,768]{3,2,1,0:T(8,128)(2,1)S(1)}, u32[]{:S(2)}, u32[]{:S(2)}) collective-permute-start(bf16[4,2,16,768]{3,2,1,0:T(8,128)(2,1)S(1)} %get-tuple-element.54), channel_id=1, source_target_pairs={{0,2},{1,3},{2,0},{3,1},{4,6},{5,7},{6,4},{7,5},{8,10},{9,11},{10,... | collective-permute-start | bytes 589832 | tf_op jit(solution)/shard_map/ppermute | solution.py:412
  31.4 0.6 collective-permute-start.5
  32.1 2.5 %collective-permute-start.9 = (bf16[4,16,768]{2,1,0:T(8,128)(2,1)S(1)}, bf16[4,16,768]{2,1,0:T(8,128)(2,1)S(1)}, u32[]{:S(2)}, u32[]{:S(2)}) collective-permute-start(bf16[4,16,768]{2,1,0:T(8,128)(2,1)S(1)} %get-tuple-element.62), channel_id=1, source_target_pairs={{0,12},{1,13},{2,14},{3,15},{4,8},{5,9},{6,10},{7,11},{8,4},{9,5},... | collective-permute-start | bytes 294920 | tf_op jit(solution)/shard_map/ppermute | solution.py:412
  34.6 2.7 %collective-permute-done.3.refs_1_ = bf16[4,2,16,768]{3,2,1,0:T(8,128)(2,1)S(1)} collective-permute-done((bf16[4,2,16,768]{3,2,1,0:T(8,128)(2,1)S(1)}, bf16[4,2,16,768]{3,2,1,0:T(8,128)(2,1)S(1)}, u32[]{:S(2)}, u32[]{:S(2)}) %collective-permute-start.3) | collective-permute-done | bytes 196640 | tf_op jit(solution)/shard_map/ppermute | solution.py:412
  37.3 1.8 %collective-permute-done.4.refs_2_ = bf16[4,2,16,768]{3,2,1,0:T(8,128)(2,1)S(1)} collective-permute-done((bf16[4,2,16,768]{3,2,1,0:T(8,128)(2,1)S(1)}, bf16[4,2,16,768]{3,2,1,0:T(8,128)(2,1)S(1)}, u32[]{:S(2)}, u32[]{:S(2)}) %collective-permute-start.4) | collective-permute-done | bytes 196640 | tf_op jit(solution)/shard_map/ppermute | solution.py:412
  39.1 2.5 %project_early.1.early = bf16[512,2304]{1,0:T(8,128)(2,1)S(1)} custom-call(bf16[4,2,16,768]{3,2,1,0:T(8,128)(2,1)S(1)} %get-tuple-element.53.refs_0_, bf16[4,2,16,768]{3,2,1,0:T(8,128)(2,1)S(1)} %collective-permute-done.3.refs_1_, bf16[4,2,16,768]{3,2,1,0:T(8,128)(2,1)S(1)} %collective-permute-done.4.refs_2_, ...), custom_call_target="tpu_custom_call" | custom-call | flops 1811939328 | bytes 3538944 | tf_op jit(solution)/shard_map/project_early/pallas_call | solution.py:281
  41.6 2.4 %collective-permute-start.18 = (bf16[4,16,768]{2,1,0:T(8,128)(2,1)S(1)}, bf16[4,16,768]{2,1,0:T(8,128)(2,1)S(1)}, u32[]{:S(2)}, u32[]{:S(2)}) collective-permute-start(bf16[4,16,768]{2,1,0:T(8,128)(2,1)S(1)} %get-tuple-element.78), channel_id=1, source_target_pairs={{0,12},{1,13},{2,14},{3,15},{4,8},{5,9},{6,10},{7,11},{8,4},{9,5},... | collective-permute-start | bytes 294920 | tf_op jit(solution)/shard_map/ppermute | solution.py:412
  44.0 2.1 %collective-permute-start.20 = (bf16[4,16,768]{2,1,0:T(8,128)(2,1)S(1)}, bf16[4,16,768]{2,1,0:T(8,128)(2,1)S(1)}, u32[]{:S(2)}, u32[]{:S(2)}) collective-permute-start(bf16[4,16,768]{2,1,0:T(8,128)(2,1)S(1)} %get-tuple-element.80), channel_id=1, source_target_pairs={{0,4},{1,5},{2,6},{3,7},{4,0},{5,1},{6,2},{7,3},{8,12},{9,13},{10,... | collective-permute-start | bytes 294920 | tf_op jit(solution)/shard_map/ppermute | solution.py:412
  46.1 5.6 %temporal.2 = (bf16[4,32,768]{2,1,0:T(8,128)(2,1)S(1)}, bf16[4,32,768]{2,1,0:T(8,128)(2,1)S(1)}, bf16[4,32,768]{2,1,0:T(8,128)(2,1)S(1)}, bf16[4,32,768]{2,1,0:T(8,128)(2,1)S(1)}) custom-call(s32[1]{0:T(128)} %bitcast.me, bf16[512,2304]{1,0:T(8,128)(2,1)S(1)} %project_early.1.early, bf16[4,16,768]{2,1,0:T(8,128)(2,1)S(1)} %get-tuple-element.61.refs_0_, ...), custom_call_target="tpu_custom_call" | custom-call | flops 3120562176 | bytes 4718592 | tf_op jit(solution)/shard_map/temporal/pallas_call | solution.py:343
  51.7 2.4 %collective-permute-start.12 = (bf16[4,32,768]{2,1,0:T(8,128)(2,1)S(1)}, bf16[4,32,768]{2,1,0:T(8,128)(2,1)S(1)}, u32[]{:S(2)}, u32[]{:S(2)}) collective-permute-start(bf16[4,32,768]{2,1,0:T(8,128)(2,1)S(1)} %get-tuple-element.66), channel_id=1, source_target_pairs={{0,12},{1,13},{2,14},{3,15},{4,8},{5,9},{6,10},{7,11},{8,4},{9,5},... | collective-permute-start | bytes 589832 | tf_op jit(solution)/shard_map/ppermute | solution.py:412
  54.1 2.1 %collective-permute-start.14 = (bf16[4,32,768]{2,1,0:T(8,128)(2,1)S(1)}, bf16[4,32,768]{2,1,0:T(8,128)(2,1)S(1)}, u32[]{:S(2)}, u32[]{:S(2)}) collective-permute-start(bf16[4,32,768]{2,1,0:T(8,128)(2,1)S(1)} %get-tuple-element.68), channel_id=1, source_target_pairs={{0,4},{1,5},{2,6},{3,7},{4,0},{5,1},{6,2},{7,3},{8,12},{9,13},{10,... | collective-permute-start | bytes 589832 | tf_op jit(solution)/shard_map/ppermute | solution.py:412
  56.2 5.6 %temporal.3 = (bf16[4,32,768]{2,1,0:T(8,128)(2,1)S(1)}, bf16[4,32,768]{2,1,0:T(8,128)(2,1)S(1)}, bf16[4,32,768]{2,1,0:T(8,128)(2,1)S(1)}, bf16[4,32,768]{2,1,0:T(8,128)(2,1)S(1)}) custom-call(s32[1]{0:T(128)} %bitcast.me, bf16[512,2304]{1,0:T(8,128)(2,1)S(1)} %project_early.1.early, bf16[4,16,768]{2,1,0:T(8,128)(2,1)S(1)} %get-tuple-element.77.refs_0_, ...), custom_call_target="tpu_custom_call" | custom-call | flops 3120562176 | bytes 4718592 | tf_op jit(solution)/shard_map/temporal/pallas_call | solution.py:343
  61.8 0.7 collective-permute-start.21
  62.4 0.2 collective-permute-start.22
  62.6 1.4 %collective-permute-start.23 = (bf16[4,32,768]{2,1,0:T(8,128)(2,1)S(1)}, bf16[4,32,768]{2,1,0:T(8,128)(2,1)S(1)}, u32[]{:S(2)}, u32[]{:S(2)}) collective-permute-start(bf16[4,32,768]{2,1,0:T(8,128)(2,1)S(1)} %get-tuple-element.84), channel_id=1, source_target_pairs={{0,1},{1,0},{2,3},{3,2},{4,5},{5,4},{6,7},{7,6},{8,9},{9,8},{10,11... | collective-permute-start | bytes 589832 | tf_op jit(solution)/shard_map/ppermute | solution.py:412
  64.0 7.2 %collective-permute-done.13.refs_2_ = bf16[4,32,768]{2,1,0:T(8,128)(2,1)S(1)} collective-permute-done((bf16[4,32,768]{2,1,0:T(8,128)(2,1)S(1)}, bf16[4,32,768]{2,1,0:T(8,128)(2,1)S(1)}, u32[]{:S(2)}, u32[]{:S(2)}) %collective-permute-start.13) | collective-permute-done | bytes 196640 | tf_op jit(solution)/shard_map/ppermute | solution.py:412
  71.2 1.6 %collective-permute-start.15 = (bf16[4,32,768]{2,1,0:T(8,128)(2,1)S(1)}, bf16[4,32,768]{2,1,0:T(8,128)(2,1)S(1)}, u32[]{:S(2)}, u32[]{:S(2)}) collective-permute-start(bf16[4,32,768]{2,1,0:T(8,128)(2,1)S(1)} %get-tuple-element.70), channel_id=1, source_target_pairs={{0,2},{1,3},{2,0},{3,1},{4,6},{5,7},{6,4},{7,5},{8,10},{9,11},{10,... | collective-permute-start | bytes 589832 | tf_op jit(solution)/shard_map/ppermute | solution.py:412
  72.8 0.6 collective-permute-start.17
  73.5 0.1 regroup.5
  73.5 2.1 %collective-permute-start.24 = (bf16[4,32,768]{2,1,0:T(8,128)(2,1)S(1)}, bf16[4,32,768]{2,1,0:T(8,128)(2,1)S(1)}, u32[]{:S(2)}, u32[]{:S(2)}) collective-permute-start(bf16[4,32,768]{2,1,0:T(8,128)(2,1)S(1)} %get-tuple-element.86), channel_id=1, source_target_pairs={{0,12},{1,13},{2,14},{3,15},{4,8},{5,9},{6,10},{7,11},{8,4},{9,5},... | collective-permute-start | bytes 589832 | tf_op jit(solution)/shard_map/ppermute | solution.py:412
  75.7 3.4 %collective-permute-done.15.refs_1_ = bf16[4,32,768]{2,1,0:T(8,128)(2,1)S(1)} collective-permute-done((bf16[4,32,768]{2,1,0:T(8,128)(2,1)S(1)}, bf16[4,32,768]{2,1,0:T(8,128)(2,1)S(1)}, u32[]{:S(2)}, u32[]{:S(2)}) %collective-permute-start.15) | collective-permute-done | bytes 196640 | tf_op jit(solution)/shard_map/ppermute | solution.py:412
  79.1 2.2 %collective-permute-done.16.refs_2_ = bf16[4,32,768]{2,1,0:T(8,128)(2,1)S(1)} collective-permute-done((bf16[4,32,768]{2,1,0:T(8,128)(2,1)S(1)}, bf16[4,32,768]{2,1,0:T(8,128)(2,1)S(1)}, u32[]{:S(2)}, u32[]{:S(2)}) %collective-permute-start.16) | collective-permute-done | bytes 196640 | tf_op jit(solution)/shard_map/ppermute | solution.py:412
  81.3 2.0 %collective-permute-done.24.refs_5_ = bf16[4,32,768]{2,1,0:T(8,128)(2,1)S(1)} collective-permute-done((bf16[4,32,768]{2,1,0:T(8,128)(2,1)S(1)}, bf16[4,32,768]{2,1,0:T(8,128)(2,1)S(1)}, u32[]{:S(2)}, u32[]{:S(2)}) %collective-permute-start.24) | collective-permute-done | bytes 196640 | tf_op jit(solution)/shard_map/ppermute | solution.py:412
  83.3 8.5 %collective-permute-done.25.refs_6_ = bf16[4,32,768]{2,1,0:T(8,128)(2,1)S(1)} collective-permute-done((bf16[4,32,768]{2,1,0:T(8,128)(2,1)S(1)}, bf16[4,32,768]{2,1,0:T(8,128)(2,1)S(1)}, u32[]{:S(2)}, u32[]{:S(2)}) %collective-permute-start.25) | collective-permute-done | bytes 196640 | tf_op jit(solution)/shard_map/ppermute | solution.py:412
  91.7 1.8 %last.1 = bf16[4,256,768]{2,1,0:T(8,128)(2,1)} custom-call(s32[1]{0:T(128)} %bitcast.me, bf16[2,256,768]{2,1,0:T(8,128)(2,1)S(1)} %get-tuple-element.47.mid01, bf16[2,256,768]{2,1,0:T(8,128)(2,1)S(1)} %get-tuple-element.48.mid23, bf16[4,32,768]{2,1,0:T(8,128)(2,1)S(1)} %get-tuple-element.69.refs_0_, bf16[4,32,768]{2,1,0:T(8,128)(2,1)S(1)} %collective-permute-done.15.refs_1_, ...), custom_call_target="tpu_custom_call" | custom-call | flops 786432 | bytes 1572864 | tf_op jit(solution)/shard_map/last/pallas_call | solution.py:391
  (42 shorter events, 0.2 us)
Async XLA Ops:
  0.0 13.7 %copy-start = (bf16[768,2304]{1,0:T(8,128)(2,1)S(1)}, bf16[768,2304]{1,0:T(8,128)(2,1)}, u32[]{:S(2)}) copy-start(bf16[768,2304]{1,0:T(8,128)(2,1)} %wqkv_in.3) | copy-start | bytes 10616836
  0.0 13.7 %copy-start.2 = (bf16[4,256,768]{2,1,0:T(8,128)(2,1)S(1)}, bf16[4,256,768]{2,1,0:T(8,128)(2,1)}, u32[]{:S(2)}) copy-start(bf16[4,256,768]{2,1,0:T(8,128)(2,1)} %x_in.3) | copy-start | bytes 4718596
  0.0 13.7 %copy-start.3 = (bf16[768,768]{1,0:T(8,128)(2,1)S(1)}, bf16[768,768]{1,0:T(8,128)(2,1)}, u32[]{:S(2)}) copy-start(bf16[768,768]{1,0:T(8,128)(2,1)} %wo_in.3) | copy-start | bytes 3538948
  8.0 12.9 %collective-permute-start = (bf16[2,4,16,768]{3,2,1,0:T(8,128)(2,1)S(1)}, bf16[2,4,16,768]{3,2,1,0:T(8,128)(2,1)S(1)}, u32[]{:S(2)}, u32[]{:S(2)}) collective-permute-start(bf16[2,4,16,768]{3,2,1,0:T(8,128)(2,1)S(1)} %get-tuple-element.50), channel_id=1, source_target_pairs={{0,12},{1,13},{2,14},{3,15},{4,8},{5,9},{6,10},{7,11},{8,4},{9,5},... | collective-permute-start | bytes 589832 | tf_op jit(solution)/shard_map/ppermute | solution.py:412
  13.1 16.7 %collective-permute-start.1 = (bf16[2,4,16,768]{3,2,1,0:T(8,128)(2,1)S(1)}, bf16[2,4,16,768]{3,2,1,0:T(8,128)(2,1)S(1)}, u32[]{:S(2)}, u32[]{:S(2)}) collective-permute-start(bf16[2,4,16,768]{3,2,1,0:T(8,128)(2,1)S(1)} %get-tuple-element.51), channel_id=1, source_target_pairs={{0,8},{1,9},{2,10},{3,11},{4,12},{5,13},{6,14},{7,15},{8,0},{9,1},... | collective-permute-start | bytes 589832 | tf_op jit(solution)/shard_map/ppermute | solution.py:412
  13.1 16.7 %collective-permute-start.2 = (bf16[2,4,16,768]{3,2,1,0:T(8,128)(2,1)S(1)}, bf16[2,4,16,768]{3,2,1,0:T(8,128)(2,1)S(1)}, u32[]{:S(2)}, u32[]{:S(2)}) collective-permute-start(bf16[2,4,16,768]{3,2,1,0:T(8,128)(2,1)S(1)} %get-tuple-element.52), channel_id=1, source_target_pairs={{0,4},{1,5},{2,6},{3,7},{4,0},{5,1},{6,2},{7,3},{8,12},{9,13},{10,... | collective-permute-start | bytes 589832 | tf_op jit(solution)/shard_map/ppermute | solution.py:412
  13.7 25.4 %copy-start.1 = (bf16[768,2304]{1,0:T(8,128)(2,1)S(1)}, bf16[768,2304]{1,0:T(8,128)(2,1)}, u32[]{:S(2)}) copy-start(bf16[768,2304]{1,0:T(8,128)(2,1)} %refs_4_.5) | copy-start | bytes 10616836
  19.1 12.3 %collective-permute-start.6 = (bf16[2,4,16,768]{3,2,1,0:T(8,128)(2,1)S(1)}, bf16[2,4,16,768]{3,2,1,0:T(8,128)(2,1)S(1)}, u32[]{:S(2)}, u32[]{:S(2)}) collective-permute-start(bf16[2,4,16,768]{3,2,1,0:T(8,128)(2,1)S(1)} %get-tuple-element.58), channel_id=1, source_target_pairs={{0,2},{1,3},{2,0},{3,1},{4,6},{5,7},{6,4},{7,5},{8,10},{9,11},{10,... | collective-permute-start | bytes 589832 | tf_op jit(solution)/shard_map/ppermute | solution.py:412
  20.9 11.2 %collective-permute-start.7 = (bf16[2,4,16,768]{3,2,1,0:T(8,128)(2,1)S(1)}, bf16[2,4,16,768]{3,2,1,0:T(8,128)(2,1)S(1)}, u32[]{:S(2)}, u32[]{:S(2)}) collective-permute-start(bf16[2,4,16,768]{3,2,1,0:T(8,128)(2,1)S(1)} %get-tuple-element.59), channel_id=1, source_target_pairs={{0,3},{1,2},{2,1},{3,0},{4,7},{5,6},{6,5},{7,4},{8,11},{9,10},{10,... | collective-permute-start | bytes 589832 | tf_op jit(solution)/shard_map/ppermute | solution.py:412
  20.9 11.2 %collective-permute-start.8 = (bf16[2,4,16,768]{3,2,1,0:T(8,128)(2,1)S(1)}, bf16[2,4,16,768]{3,2,1,0:T(8,128)(2,1)S(1)}, u32[]{:S(2)}, u32[]{:S(2)}) collective-permute-start(bf16[2,4,16,768]{3,2,1,0:T(8,128)(2,1)S(1)} %get-tuple-element.60), channel_id=1, source_target_pairs={{0,1},{1,0},{2,3},{3,2},{4,5},{5,4},{6,7},{7,6},{8,9},{9,8},{10,11... | collective-permute-start | bytes 589832 | tf_op jit(solution)/shard_map/ppermute | solution.py:412
  29.8 7.5 %collective-permute-start.3 = (bf16[4,2,16,768]{3,2,1,0:T(8,128)(2,1)S(1)}, bf16[4,2,16,768]{3,2,1,0:T(8,128)(2,1)S(1)}, u32[]{:S(2)}, u32[]{:S(2)}) collective-permute-start(bf16[4,2,16,768]{3,2,1,0:T(8,128)(2,1)S(1)} %get-tuple-element.54), channel_id=1, source_target_pairs={{0,2},{1,3},{2,0},{3,1},{4,6},{5,7},{6,4},{7,5},{8,10},{9,11},{10,... | collective-permute-start | bytes 589832 | tf_op jit(solution)/shard_map/ppermute | solution.py:412
  31.4 7.7 %collective-permute-start.4 = (bf16[4,2,16,768]{3,2,1,0:T(8,128)(2,1)S(1)}, bf16[4,2,16,768]{3,2,1,0:T(8,128)(2,1)S(1)}, u32[]{:S(2)}, u32[]{:S(2)}) collective-permute-start(bf16[4,2,16,768]{3,2,1,0:T(8,128)(2,1)S(1)} %get-tuple-element.55), channel_id=1, source_target_pairs={{0,3},{1,2},{2,1},{3,0},{4,7},{5,6},{6,5},{7,4},{8,11},{9,10},{10,... | collective-permute-start | bytes 589832 | tf_op jit(solution)/shard_map/ppermute | solution.py:412
  31.4 7.7 %collective-permute-start.5 = (bf16[4,2,16,768]{3,2,1,0:T(8,128)(2,1)S(1)}, bf16[4,2,16,768]{3,2,1,0:T(8,128)(2,1)S(1)}, u32[]{:S(2)}, u32[]{:S(2)}) collective-permute-start(bf16[4,2,16,768]{3,2,1,0:T(8,128)(2,1)S(1)} %get-tuple-element.56), channel_id=1, source_target_pairs={{0,1},{1,0},{2,3},{3,2},{4,5},{5,4},{6,7},{7,6},{8,9},{9,8},{10,11... | collective-permute-start | bytes 589832 | tf_op jit(solution)/shard_map/ppermute | solution.py:412
  32.1 11.8 %collective-permute-start.9 = (bf16[4,16,768]{2,1,0:T(8,128)(2,1)S(1)}, bf16[4,16,768]{2,1,0:T(8,128)(2,1)S(1)}, u32[]{:S(2)}, u32[]{:S(2)}) collective-permute-start(bf16[4,16,768]{2,1,0:T(8,128)(2,1)S(1)} %get-tuple-element.62), channel_id=1, source_target_pairs={{0,12},{1,13},{2,14},{3,15},{4,8},{5,9},{6,10},{7,11},{8,4},{9,5},... | collective-permute-start | bytes 294920 | tf_op jit(solution)/shard_map/ppermute | solution.py:412
  34.6 11.4 %collective-permute-start.10 = (bf16[4,16,768]{2,1,0:T(8,128)(2,1)S(1)}, bf16[4,16,768]{2,1,0:T(8,128)(2,1)S(1)}, u32[]{:S(2)}, u32[]{:S(2)}) collective-permute-start(bf16[4,16,768]{2,1,0:T(8,128)(2,1)S(1)} %get-tuple-element.63), channel_id=1, source_target_pairs={{0,8},{1,9},{2,10},{3,11},{4,12},{5,13},{6,14},{7,15},{8,0},{9,1},... | collective-permute-start | bytes 294920 | tf_op jit(solution)/shard_map/ppermute | solution.py:412
  37.3 8.7 %collective-permute-start.11 = (bf16[4,16,768]{2,1,0:T(8,128)(2,1)S(1)}, bf16[4,16,768]{2,1,0:T(8,128)(2,1)S(1)}, u32[]{:S(2)}, u32[]{:S(2)}) collective-permute-start(bf16[4,16,768]{2,1,0:T(8,128)(2,1)S(1)} %get-tuple-element.64), channel_id=1, source_target_pairs={{0,4},{1,5},{2,6},{3,7},{4,0},{5,1},{6,2},{7,3},{8,12},{9,13},{10,... | collective-permute-start | bytes 294920 | tf_op jit(solution)/shard_map/ppermute | solution.py:412
  39.1 6.9 %copy-start.4 = (bf16[768,768]{1,0:T(8,128)(2,1)S(1)}, bf16[768,768]{1,0:T(8,128)(2,1)}, u32[]{:S(2)}) copy-start(bf16[768,768]{1,0:T(8,128)(2,1)} %refs_5_.3) | copy-start | bytes 3538948
  41.6 12.5 %collective-permute-start.18 = (bf16[4,16,768]{2,1,0:T(8,128)(2,1)S(1)}, bf16[4,16,768]{2,1,0:T(8,128)(2,1)S(1)}, u32[]{:S(2)}, u32[]{:S(2)}) collective-permute-start(bf16[4,16,768]{2,1,0:T(8,128)(2,1)S(1)} %get-tuple-element.78), channel_id=1, source_target_pairs={{0,12},{1,13},{2,14},{3,15},{4,8},{5,9},{6,10},{7,11},{8,4},{9,5},... | collective-permute-start | bytes 294920 | tf_op jit(solution)/shard_map/ppermute | solution.py:412
  43.9 12.2 %collective-permute-start.19 = (bf16[4,16,768]{2,1,0:T(8,128)(2,1)S(1)}, bf16[4,16,768]{2,1,0:T(8,128)(2,1)S(1)}, u32[]{:S(2)}, u32[]{:S(2)}) collective-permute-start(bf16[4,16,768]{2,1,0:T(8,128)(2,1)S(1)} %get-tuple-element.79), channel_id=1, source_target_pairs={{0,8},{1,9},{2,10},{3,11},{4,12},{5,13},{6,14},{7,15},{8,0},{9,1},... | collective-permute-start | bytes 294920 | tf_op jit(solution)/shard_map/ppermute | solution.py:412
  44.0 12.2 %collective-permute-start.20 = (bf16[4,16,768]{2,1,0:T(8,128)(2,1)S(1)}, bf16[4,16,768]{2,1,0:T(8,128)(2,1)S(1)}, u32[]{:S(2)}, u32[]{:S(2)}) collective-permute-start(bf16[4,16,768]{2,1,0:T(8,128)(2,1)S(1)} %get-tuple-element.80), channel_id=1, source_target_pairs={{0,4},{1,5},{2,6},{3,7},{4,0},{5,1},{6,2},{7,3},{8,12},{9,13},{10,... | collective-permute-start | bytes 294920 | tf_op jit(solution)/shard_map/ppermute | solution.py:412
  51.7 10.9 %collective-permute-start.12 = (bf16[4,32,768]{2,1,0:T(8,128)(2,1)S(1)}, bf16[4,32,768]{2,1,0:T(8,128)(2,1)S(1)}, u32[]{:S(2)}, u32[]{:S(2)}) collective-permute-start(bf16[4,32,768]{2,1,0:T(8,128)(2,1)S(1)} %get-tuple-element.66), channel_id=1, source_target_pairs={{0,12},{1,13},{2,14},{3,15},{4,8},{5,9},{6,10},{7,11},{8,4},{9,5},... | collective-permute-start | bytes 589832 | tf_op jit(solution)/shard_map/ppermute | solution.py:412
  54.0 17.1 %collective-permute-start.13 = (bf16[4,32,768]{2,1,0:T(8,128)(2,1)S(1)}, bf16[4,32,768]{2,1,0:T(8,128)(2,1)S(1)}, u32[]{:S(2)}, u32[]{:S(2)}) collective-permute-start(bf16[4,32,768]{2,1,0:T(8,128)(2,1)S(1)} %get-tuple-element.67), channel_id=1, source_target_pairs={{0,8},{1,9},{2,10},{3,11},{4,12},{5,13},{6,14},{7,15},{8,0},{9,1},... | collective-permute-start | bytes 589832 | tf_op jit(solution)/shard_map/ppermute | solution.py:412
  54.1 17.1 %collective-permute-start.14 = (bf16[4,32,768]{2,1,0:T(8,128)(2,1)S(1)}, bf16[4,32,768]{2,1,0:T(8,128)(2,1)S(1)}, u32[]{:S(2)}, u32[]{:S(2)}) collective-permute-start(bf16[4,32,768]{2,1,0:T(8,128)(2,1)S(1)} %get-tuple-element.68), channel_id=1, source_target_pairs={{0,4},{1,5},{2,6},{3,7},{4,0},{5,1},{6,2},{7,3},{8,12},{9,13},{10,... | collective-permute-start | bytes 589832 | tf_op jit(solution)/shard_map/ppermute | solution.py:412
  61.8 11.0 %collective-permute-start.21 = (bf16[4,32,768]{2,1,0:T(8,128)(2,1)S(1)}, bf16[4,32,768]{2,1,0:T(8,128)(2,1)S(1)}, u32[]{:S(2)}, u32[]{:S(2)}) collective-permute-start(bf16[4,32,768]{2,1,0:T(8,128)(2,1)S(1)} %get-tuple-element.82), channel_id=1, source_target_pairs={{0,2},{1,3},{2,0},{3,1},{4,6},{5,7},{6,4},{7,5},{8,10},{9,11},{10,... | collective-permute-start | bytes 589832 | tf_op jit(solution)/shard_map/ppermute | solution.py:412
  62.4 11.0 %collective-permute-start.22 = (bf16[4,32,768]{2,1,0:T(8,128)(2,1)S(1)}, bf16[4,32,768]{2,1,0:T(8,128)(2,1)S(1)}, u32[]{:S(2)}, u32[]{:S(2)}) collective-permute-start(bf16[4,32,768]{2,1,0:T(8,128)(2,1)S(1)} %get-tuple-element.83), channel_id=1, source_target_pairs={{0,3},{1,2},{2,1},{3,0},{4,7},{5,6},{6,5},{7,4},{8,11},{9,10},{10,... | collective-permute-start | bytes 589832 | tf_op jit(solution)/shard_map/ppermute | solution.py:412
  62.6 10.8 %collective-permute-start.23 = (bf16[4,32,768]{2,1,0:T(8,128)(2,1)S(1)}, bf16[4,32,768]{2,1,0:T(8,128)(2,1)S(1)}, u32[]{:S(2)}, u32[]{:S(2)}) collective-permute-start(bf16[4,32,768]{2,1,0:T(8,128)(2,1)S(1)} %get-tuple-element.84), channel_id=1, source_target_pairs={{0,1},{1,0},{2,3},{3,2},{4,5},{5,4},{6,7},{7,6},{8,9},{9,8},{10,11... | collective-permute-start | bytes 589832 | tf_op jit(solution)/shard_map/ppermute | solution.py:412
  71.2 7.9 %collective-permute-start.15 = (bf16[4,32,768]{2,1,0:T(8,128)(2,1)S(1)}, bf16[4,32,768]{2,1,0:T(8,128)(2,1)S(1)}, u32[]{:S(2)}, u32[]{:S(2)}) collective-permute-start(bf16[4,32,768]{2,1,0:T(8,128)(2,1)S(1)} %get-tuple-element.70), channel_id=1, source_target_pairs={{0,2},{1,3},{2,0},{3,1},{4,6},{5,7},{6,4},{7,5},{8,10},{9,11},{10,... | collective-permute-start | bytes 589832 | tf_op jit(solution)/shard_map/ppermute | solution.py:412
  72.8 8.4 %collective-permute-start.16 = (bf16[4,32,768]{2,1,0:T(8,128)(2,1)S(1)}, bf16[4,32,768]{2,1,0:T(8,128)(2,1)S(1)}, u32[]{:S(2)}, u32[]{:S(2)}) collective-permute-start(bf16[4,32,768]{2,1,0:T(8,128)(2,1)S(1)} %get-tuple-element.71), channel_id=1, source_target_pairs={{0,3},{1,2},{2,1},{3,0},{4,7},{5,6},{6,5},{7,4},{8,11},{9,10},{10,... | collective-permute-start | bytes 589832 | tf_op jit(solution)/shard_map/ppermute | solution.py:412
  72.8 8.4 %collective-permute-start.17 = (bf16[4,32,768]{2,1,0:T(8,128)(2,1)S(1)}, bf16[4,32,768]{2,1,0:T(8,128)(2,1)S(1)}, u32[]{:S(2)}, u32[]{:S(2)}) collective-permute-start(bf16[4,32,768]{2,1,0:T(8,128)(2,1)S(1)} %get-tuple-element.72), channel_id=1, source_target_pairs={{0,1},{1,0},{2,3},{3,2},{4,5},{5,4},{6,7},{7,6},{8,9},{9,8},{10,11... | collective-permute-start | bytes 589832 | tf_op jit(solution)/shard_map/ppermute | solution.py:412
  73.5 9.8 %collective-permute-start.24 = (bf16[4,32,768]{2,1,0:T(8,128)(2,1)S(1)}, bf16[4,32,768]{2,1,0:T(8,128)(2,1)S(1)}, u32[]{:S(2)}, u32[]{:S(2)}) collective-permute-start(bf16[4,32,768]{2,1,0:T(8,128)(2,1)S(1)} %get-tuple-element.86), channel_id=1, source_target_pairs={{0,12},{1,13},{2,14},{3,15},{4,8},{5,9},{6,10},{7,11},{8,4},{9,5},... | collective-permute-start | bytes 589832 | tf_op jit(solution)/shard_map/ppermute | solution.py:412
  75.7 16.1 %collective-permute-start.25 = (bf16[4,32,768]{2,1,0:T(8,128)(2,1)S(1)}, bf16[4,32,768]{2,1,0:T(8,128)(2,1)S(1)}, u32[]{:S(2)}, u32[]{:S(2)}) collective-permute-start(bf16[4,32,768]{2,1,0:T(8,128)(2,1)S(1)} %get-tuple-element.87), channel_id=1, source_target_pairs={{0,8},{1,9},{2,10},{3,11},{4,12},{5,13},{6,14},{7,15},{8,0},{9,1},... | collective-permute-start | bytes 589832 | tf_op jit(solution)/shard_map/ppermute | solution.py:412
  79.1 12.6 %collective-permute-start.26 = (bf16[4,32,768]{2,1,0:T(8,128)(2,1)S(1)}, bf16[4,32,768]{2,1,0:T(8,128)(2,1)S(1)}, u32[]{:S(2)}, u32[]{:S(2)}) collective-permute-start(bf16[4,32,768]{2,1,0:T(8,128)(2,1)S(1)} %get-tuple-element.88), channel_id=1, source_target_pairs={{0,4},{1,5},{2,6},{3,7},{4,0},{5,1},{6,2},{7,3},{8,12},{9,13},{10,... | collective-permute-start | bytes 589832 | tf_op jit(solution)/shard_map/ppermute | solution.py:412
